TPU v7x, 32 devices: a whole 2x2x4 slice. The times are simulated.
32 devices in a mesh: groups: 2 (over y), ctx: 4 (over z), dp: 2 (over x), sub: 2 (over core).
Axes of the slice: x: 2, y: 2, z: 4, core: 2. Of those that a mesh axis runs over, the one named last changes fastest.
Arguments:
- q_glob: bfloat16 [1024, 2048], P(('groups', 'ctx'), ('dp', 'sub')), parts along dimension 0, may hold values from -6 to 6
- k_glob: bfloat16 [1024, 2048], P(('groups', 'ctx'), ('dp', 'sub')), parts along dimension 0, may hold values from -6 to 6
- v_glob: bfloat16 [1024, 2048], P(('groups', 'ctx'), ('dp', 'sub')), parts along dimension 0, may hold values from -6 to 6
- x_glob: bfloat16 [1024, 4096], P(('groups', 'ctx'), ('dp', 'sub')), parts along dimension 0, may hold values from -0.049804688 to 0.049804688
- out_weight: bfloat16 [2048, 4096], P(('dp', 'sub')), may hold values from -0.125 to 0.125
- bridge_weight: bfloat16 [512, 1024], P(('dp', 'sub')), may hold values from -0.25 to 0.25
- byte_embed: bfloat16 [1024, 8, 1024], P(('groups', 'ctx', 'dp', 'sub')), parts along dimension 0, may hold values from -0.049804688 to 0.049804688
- norm_gain: float32 [1024], replicated, may hold values from 0.1 to 1.9
- qkv_weight: bfloat16 [1024, 3072], P(None, ('dp', 'sub')), may hold values from -0.1875 to 0.1875
Outputs:
- local_qkv: bfloat16 [1024, 8, 3072], P(('groups', 'ctx', 'dp', 'sub')), parts along dimension 0
There are 2 independent parts, one for each index of `groups`. A program takes and returns all parts, laid end to end along the dimension named above; an argument that names none is the same for every part. Nothing has to cross between parts.
All inputs are finite; a program needn't handle non-finite values.
Results may differ from a plain program's by a relative error of at most 0.024.
Values may be sent and summed in bfloat16 or wider, within the bound.
No kernel may reach another device: no remote copies, remote signals or barrier semaphores. Data moves between devices by JAX's collectives and lax.ppermute only.
A program may use at most 64 MiB of HBM per device.

v0:
```python
import math

import jax
import jax.numpy as jnp
from jax import lax
from jax.sharding import PartitionSpec as P

HD = 128
DL = 1024
P_SIZE = 8
DSLICE = 512


def per_device(
    q_glob, k_glob, v_glob, x_glob, out_weight, bridge_weight, byte_embed, norm_gain, qkv_weight
):
    query_rows = q_glob.shape[0]
    query_width = q_glob.shape[1]
    head_count = query_width // HD
    score_scale = 1.0 / math.sqrt(HD)
    first_row = lax.axis_index("ctx") * query_rows
    queries = q_glob.reshape(query_rows, head_count, HD)
    query_pos = first_row + lax.iota(jnp.int32, query_rows)
    row_max = jnp.full((head_count, query_rows), -1e30, jnp.float32)
    key_piece = lax.all_gather(k_glob, "ctx", axis=0, tiled=True)
    value_piece = lax.all_gather(v_glob, "ctx", axis=0, tiled=True)
    count = key_piece.shape[0]
    keys = key_piece.reshape(count, head_count, HD)
    values = value_piece.reshape(count, head_count, HD)
    scores = (
        jnp.einsum("qhd,khd->hqk", queries, keys, preferred_element_type=jnp.float32) * score_scale
    )
    key_pos = lax.iota(jnp.int32, count)
    allowed = query_pos[:, None] >= key_pos[None, :]
    scores = jnp.where(allowed[None], scores, -jnp.inf)
    new_max = jnp.maximum(row_max, jnp.max(scores, axis=2))
    weights = jnp.exp(scores - new_max[:, :, None])
    row_sum = jnp.sum(weights, axis=2)
    weighted = jnp.einsum(
        "hqk,khd->hqd", weights.astype(jnp.bfloat16), values, preferred_element_type=jnp.float32
    )
    row_max, row_sum, weighted = (new_max, row_sum, weighted)
    attn = (
        (weighted / row_sum[:, :, None])
        .astype(jnp.bfloat16)
        .transpose(1, 0, 2)
        .reshape(query_rows, query_width)
    )
    head_terms = jnp.dot(attn, out_weight, preferred_element_type=jnp.float32)
    group_size = lax.axis_size(("dp", "sub"))
    own_bytes = P_SIZE // group_size
    feature_sum = lax.psum_scatter(
        head_terms.astype(jnp.bfloat16), ("dp", "sub"), scatter_dimension=1, tiled=True
    ).astype(jnp.float32)
    patch_out = (
        (feature_sum + x_glob.astype(jnp.float32))
        .astype(jnp.bfloat16)
        .reshape(query_rows, own_bytes, DSLICE)
    )
    patch_out = lax.all_to_all(patch_out, ("dp", "sub"), split_axis=0, concat_axis=1, tiled=True)
    glob_bytes = patch_out.reshape(-1, DSLICE)
    byte_rows = glob_bytes.shape[0]
    bridged = jnp.dot(
        glob_bytes,
        lax.all_gather(bridge_weight, ("dp", "sub"), axis=0, tiled=True),
        preferred_element_type=jnp.float32,
    )
    byte_in = byte_embed.reshape(byte_rows, DL).astype(jnp.float32) + bridged
    mean_square = jnp.mean(byte_in * byte_in, axis=1, keepdims=True)
    normalized = (byte_in * lax.rsqrt(mean_square + 1e-05) * norm_gain).astype(jnp.bfloat16)
    result_rows = jnp.dot(
        normalized,
        lax.all_gather(qkv_weight, ("dp", "sub"), axis=1, tiled=True),
        preferred_element_type=jnp.float32,
    ).astype(jnp.bfloat16)
    return result_rows.reshape(byte_embed.shape[0], P_SIZE, 3 * DL)


def solution(mesh):
    in_specs = (
        P(("groups", "ctx"), ("dp", "sub")),
        P(("groups", "ctx"), ("dp", "sub")),
        P(("groups", "ctx"), ("dp", "sub")),
        P(("groups", "ctx"), ("dp", "sub")),
        P(("dp", "sub"), None),
        P(("dp", "sub"), None),
        P(("groups", "ctx", "dp", "sub"), None, None),
        P(),
        P(None, ("dp", "sub")),
    )
    out_specs = P(("groups", "ctx", "dp", "sub"), None, None)
    return jax.shard_map(
        per_device, mesh=mesh, in_specs=in_specs, out_specs=out_specs, check_vma=False
    )
```

profile of v0, /device:TPU:25, one launch (start us, length us, event | category | flops | bytes accessed | tf_op | source)
XLA Modules:
  0.0 148.9 jit_solution(16916486692769152107)
XLA Ops:
  6.5 0.0 copy-start
  6.5 0.0 reduce-scatter.2.cloned.1.call-start
  6.5 1.1 copy.22
  7.6 11.0 %all_gather.12 = bf16[512,512]{0,1:T(8,128)(2,1)S(1)} all-gather(bf16[128,512]{0,1:T(8,128)(2,1)S(1)} %copy.22), channel_id=1, replica_groups=mesh['groups'=2,'ctx'=4,'dp'=2,'sub'=2] {'ctx'}, dimensions={0}, use_global_device_ids=true | all-gather | bytes 655360 | tf_op jit(solution)/shard_map/all_gather | solution.py:25
  18.6 0.1 iota_compare_fusion
  18.7 0.0 copy-done
  18.8 0.4 fusion.12
  19.1 14.1 %all_gather.13 = bf16[512,512]{1,0:T(8,128)(2,1)S(1)} all-gather(bf16[128,512]{1,0:T(8,128)(2,1)} %param.11), channel_id=1, replica_groups=mesh['groups'=2,'ctx'=4,'dp'=2,'sub'=2] {'ctx'}, dimensions={0}, use_global_device_ids=true | all-gather | bytes 655360 | tf_op jit(solution)/shard_map/all_gather | solution.py:26
  33.2 0.2 copy.25
  33.5 0.3 fusion.4
  33.8 0.4 fusion.3
  34.3 0.0 copy-start.2
  34.3 4.0 %convolution_convert_fusion = bf16[128,4096]{1,0:T(8,128)(2,1)} fusion(bf16[128,512]{0,1:T(8,128)(2,1)S(1)} %bitcast.37, bf16[512,4096]{1,0:T(8,128)(2,1)} %param.13), kind=kOutput, calls=%fused_computation | convolution fusion | flops 537395200 | bytes 5373952 | tf_op jit(solution)/shard_map/dot_general | solution.py:49
  38.2 0.0 reduce-scatter.2.cloned.1.call-update
  38.2 0.0 copy-start.3
  38.3 0.0 all-gather.3.cloned.1.call-start
  38.3 0.7 all-gather.3.cloned.1.call-update
  39.0 0.0 all-gather.5.cloned.1.call-start
  39.1 0.7 all-gather.5.cloned.1.call-update
  39.7 29.9 %reduce-scatter.2.cloned.1.call-done = bf16[128,1024]{1,0:T(8,128)(2,1)} async-done(((bf16[128,4096]{1,0:T(8,128)(2,1)}), bf16[128,1024]{1,0:T(8,128)(2,1)}) %reduce-scatter.2.cloned.1.call-update) | async-done | bytes 262160 | tf_op jit(solution)/shard_map/reduce_scatter | solution.py:52
  69.7 0.0 copy-done.2
  69.7 1.0 add_convert_fusion
  70.7 0.2 reshape.65
  70.9 8.1 %all_to_all.15 = bf16[128,2,512]{2,1,0:T(2,128)(2,1)S(1)} all-to-all(bf16[128,2,512]{2,1,0:T(2,128)(2,1)S(1)} %reshape.65), channel_id=1, replica_groups=mesh['groups'=2,'ctx'=4,'dp'=2,'sub'=2] {'dp','sub'}, dimensions={0} | all-to-all | bytes 524288 | tf_op jit(solution)/shard_map/all_to_all | solution.py:60
  79.0 0.3 copy.27
  79.3 0.1 reshape.66
  79.4 9.1 %all-gather.3.cloned.1.call-done = bf16[512,1024]{1,0:T(8,128)(2,1)} async-done(((bf16[128,1024]{1,0:T(8,128)(2,1)}), bf16[512,1024]{1,0:T(8,128)(2,1)}) %all-gather.3.cloned.1.call-update) | async-done | bytes 1048592 | tf_op jit(solution)/shard_map/all_gather | solution.py:65
  88.5 0.0 copy-done.1
  88.5 1.7 %multiply_reduce_fusion = (f32[256]{0:T(256)S(1)}, f32[256,1024]{1,0:T(8,128)S(1)}) fusion(bf16[256,512]{1,0:T(8,128)(2,1)S(1)} %reshape.66, bf16[512,1024]{1,0:T(8,128)(2,1)} %all-gather.3.cloned.1.call-done, bf16[32,8,1024]{2,1,0:T(8,128)(2,1)S(1)} %copy-done.1), kind=kOutput, calls=%fused_computation.10 | convolution fusion | flops 269483776 | bytes 2884608 | tf_op jit(solution)/shard_map/dot_general | solution.py:63
  90.2 46.3 %all-gather.5.cloned.1.call-done = bf16[1024,3072]{1,0:T(8,128)(2,1)} async-done(((bf16[1024,768]{1,0:T(8,128)(2,1)}), bf16[1024,3072]{1,0:T(8,128)(2,1)}) %all-gather.5.cloned.1.call-update) | async-done | bytes 6291472 | tf_op jit(solution)/shard_map/all_gather | solution.py:73
  136.6 0.0 copy-done.3
  136.6 5.8 %fusion = bf16[32,8,3072]{2,1,0:T(8,128)(2,1)} fusion(bf16[1024,3072]{1,0:T(8,128)(2,1)} %all-gather.5.cloned.1.call-done, f32[256,1024]{1,0:T(8,128)S(1)} %get-tuple-element.8, f32[1024]{0:T(1024)S(1)} %copy-done.3, f32[256]{0:T(256)S(1)} %add_rsqrt_fusion), kind=kOutput, calls=%fused_computation.2 | convolution fusion | flops 1612185600 | bytes 8918016 | tf_op jit(solution)/shard_map/dot_general | solution.py:71
  (5 shorter events, 0.0 us)
Async XLA Ops:
  6.5 12.2 %copy-start = (bf16[128,512]{1,0:T(8,128)(2,1)S(1)}, bf16[128,512]{1,0:T(8,128)(2,1)}, u32[]{:S(2)}) copy-start(bf16[128,512]{1,0:T(8,128)(2,1)} %param.9) | copy-start | bytes 393220
  6.5 63.1 %reduce-scatter.2.cloned.1.call-start = ((), (), s32[]{:S(2)}) async-start(), calls=%async_computation.2 | async-start | bytes 1310720 | tf_op jit(solution)/shard_map/reduce_scatter | solution.py:52
  34.3 35.4 %copy-start.2 = (bf16[128,1024]{1,0:T(8,128)(2,1)S(1)}, bf16[128,1024]{1,0:T(8,128)(2,1)}, u32[]{:S(2)}) copy-start(bf16[128,1024]{1,0:T(8,128)(2,1)} %param.12) | copy-start | bytes 786436
  38.2 50.3 %copy-start.1 = (bf16[32,8,1024]{2,1,0:T(8,128)(2,1)S(1)}, bf16[32,8,1024]{2,1,0:T(8,128)(2,1)}, u32[]{:S(2)}) copy-start(bf16[32,8,1024]{2,1,0:T(8,128)(2,1)} %param.15) | copy-start | bytes 1572868
  38.2 98.3 %copy-start.3 = (f32[1024]{0:T(1024)S(1)}, f32[1024]{0:T(1024)}, u32[]{:S(2)}) copy-start(f32[1024]{0:T(1024)} %param.16) | copy-start | bytes 12292
  38.3 50.2 %all-gather.3.cloned.1.call-start = ((), (), s32[]{:S(2)}) async-start(), calls=%async_computation.3 | async-start | bytes 1310720 | tf_op jit(solution)/shard_map/all_gather | solution.py:65
  39.0 97.6 %all-gather.5.cloned.1.call-start = ((), (), s32[]{:S(2)}) async-start(), calls=%async_computation.4 | async-start | bytes 7864320 | tf_op jit(solution)/shard_map/all_gather | solution.py:73
Sparse Core Ops, SparseCore 0:
  38.4 31.2 reduce-scatter.1
  71.3 17.1 all-gather.2
  90.1 46.3 all-gather.4
where the time goes:
time: 150 us; the launch traced here: 149 us
  waiting for transfers between devices  86.8 us (58%)
  blocking collectives  33.2 us (22%)
  between operations  13.2 us (9%)
  matrix products  12.3 us (8%)
  local copies, waits for them, and re-layouts  1.87 us (1%)
    all_gather x1, waiting for transfers between devices, per_device(): lax.all_gather(qkv_weight, ('dp', 'sub'), axis=1, tiled=True)  46.3 us
    reduce_scatter x1, waiting for transfers between devices, per_device(): lax.psum_scatter(head_terms.astype(jnp.bfloat16), ('dp', 'sub'), scatter_...  29.9 us
    all_gather x1, blocking collectives, per_device(): value_piece = lax.all_gather(v_glob, 'ctx', axis=0, tiled=True)  14.1 us
    all_gather x1, blocking collectives, per_device(): key_piece = lax.all_gather(k_glob, 'ctx', axis=0, tiled=True)  11 us
    all_gather x1, waiting for transfers between devices, per_device(): lax.all_gather(bridge_weight, ('dp', 'sub'), axis=0, tiled=True)  9.11 us
    all_to_all x1, blocking collectives, per_device(): lax.all_to_all(patch_out, ('dp', 'sub'), split_axis=0, concat_axis=1, til...  8.07 us
    dot_general x1, matrix products, per_device(): jnp.dot(normalized, lax.all_gather(qkv_weight, ('dp', 'sub'), axis=1, til...  5.78 us
    dot_general x1, matrix products, per_device(): head_terms = jnp.dot(attn, out_weight, preferred_element_type=jnp.float32)  3.96 us
  transfers between devices with their start and end apart: 3, of which 3 were waited for; matrix products, arithmetic and copies ran while one was open for 2% of the time, Pallas kernels for 0%

commit v1 on v0

v1 whole, which is shorter than its diff:
```python
import functools
import math

import jax
import jax.numpy as jnp
from jax import lax
from jax.experimental import pallas as pl
from jax.experimental.pallas import tpu as pltpu
from jax.sharding import PartitionSpec as P

HD = 128
DL = 1024
P_SIZE = 8
DSLICE = 512
GROUP = ("dp", "sub")
SCALE = 1.0 / math.sqrt(HD)
VMEM = pl.BlockSpec(memory_space=pltpu.VMEM)
SMEM = pl.BlockSpec(memory_space=pltpu.SMEM)
F32 = jnp.float32
BF16 = jnp.bfloat16


def dot(a, b):
    return jnp.dot(a, b, preferred_element_type=F32)


def any_mesh(
    q_glob, k_glob, v_glob, x_glob, out_weight, bridge_weight, byte_embed, norm_gain, qkv_weight
):
    query_rows, query_width = q_glob.shape
    head_count = query_width // HD
    first_row = lax.axis_index("ctx") * query_rows
    queries = q_glob.reshape(query_rows, head_count, HD)
    query_pos = first_row + lax.iota(jnp.int32, query_rows)
    keys = lax.all_gather(k_glob, "ctx", axis=0, tiled=True)
    values = lax.all_gather(v_glob, "ctx", axis=0, tiled=True)
    count = keys.shape[0]
    keys = keys.reshape(count, head_count, HD)
    values = values.reshape(count, head_count, HD)
    scores = jnp.einsum("qhd,khd->hqk", queries, keys, preferred_element_type=F32) * SCALE
    allowed = query_pos[:, None] >= lax.iota(jnp.int32, count)[None, :]
    scores = jnp.where(allowed[None], scores, -jnp.inf)
    weights = jnp.exp(scores - jnp.max(scores, axis=2)[:, :, None])
    row_sum = jnp.sum(weights, axis=2)
    weighted = jnp.einsum("hqk,khd->hqd", weights.astype(BF16), values, preferred_element_type=F32)
    attn = (weighted / row_sum[:, :, None]).astype(BF16)
    attn = attn.transpose(1, 0, 2).reshape(query_rows, query_width)
    head_terms = dot(attn, out_weight)
    own_bytes = P_SIZE // lax.axis_size(GROUP)
    feature_sum = lax.psum_scatter(
        head_terms.astype(BF16), GROUP, scatter_dimension=1, tiled=True
    ).astype(F32)
    patch_out = (feature_sum + x_glob.astype(F32)).astype(BF16)
    patch_out = patch_out.reshape(query_rows, own_bytes, DSLICE)
    patch_out = lax.all_to_all(patch_out, GROUP, split_axis=0, concat_axis=1, tiled=True)
    glob_bytes = patch_out.reshape(-1, DSLICE)
    byte_rows = glob_bytes.shape[0]
    bridged = dot(glob_bytes, lax.all_gather(bridge_weight, GROUP, axis=0, tiled=True))
    byte_in = byte_embed.reshape(byte_rows, DL).astype(F32) + bridged
    mean_square = jnp.mean(byte_in * byte_in, axis=1, keepdims=True)
    normalized = (byte_in * lax.rsqrt(mean_square + 1e-05) * norm_gain).astype(BF16)
    result = dot(normalized, lax.all_gather(qkv_weight, GROUP, axis=1, tiled=True)).astype(BF16)
    return result.reshape(byte_embed.shape[0], P_SIZE, 3 * DL)


def attend_project_kernel(
    place, q, x, w, *refs, heads, blocks
):
    keys, values = refs[:blocks], refs[blocks : 2 * blocks]
    away, kept, attn, xs = refs[2 * blocks :]
    ctx, dp, sub = place[0], place[1], place[2]
    rows = q.shape[0]
    quarter = rows // 4
    row = lax.broadcasted_iota(jnp.int32, (rows, rows), 0)
    col = lax.broadcasted_iota(jnp.int32, (rows, rows), 1)
    for h in range(heads):
        cols = pl.ds(h * HD, HD)
        qh = q[:, cols]
        scores = []
        for s in range(blocks):
            sc = lax.dot_general(
                qh, keys[s][:, cols], (((1,), (1,)), ((), ())), preferred_element_type=F32
            ) * SCALE
            keep = (row >= col) if s == 0 else (ctx >= s)
            scores.append(jnp.where(keep, sc, -jnp.inf))
        scores = jnp.concatenate(scores, axis=1)
        probs = jnp.exp(scores - jnp.max(scores, axis=1, keepdims=True))
        total = jnp.sum(probs, axis=1, keepdims=True)
        probs = probs.astype(BF16)
        mixed = dot(probs[:, :rows], values[0][:, cols])
        for s in range(1, blocks):
            mixed += dot(probs[:, s * rows : (s + 1) * rows], values[s][:, cols])
        attn[:, cols] = (mixed / total).astype(BF16)
    order = []
    for core in (1 - sub, sub):
        for chip in (1 - dp, dp):
            order.append(pl.ds(pl.multiple_of((chip * 2 + core) * quarter, quarter), quarter))
    a = jnp.concatenate([attn[o, :] for o in order], axis=0)
    for i, o in enumerate(order):
        xs[pl.ds(i * quarter, quarter), :] = x[o, :]
    block = x.shape[1]
    own = dp * 2 + sub
    for b in range(w.shape[1] // block):
        cols = pl.ds(b * block, block)
        terms = dot(a, w[:, cols])
        terms += jnp.where(own == b, xs[...].astype(F32), 0.0)
        away[:, cols] = terms[: 2 * quarter].astype(BF16)
        kept[:, cols] = terms[2 * quarter :]


def attend_project(place, q, x, w, keys, values):
    rows, width = q.shape
    half = rows // 2
    blocks = len(keys)
    return pl.pallas_call(
        functools.partial(attend_project_kernel, heads=width // HD, blocks=blocks),
        out_shape=(
            jax.ShapeDtypeStruct((half, w.shape[1]), BF16),
            jax.ShapeDtypeStruct((half, w.shape[1]), F32),
        ),
        in_specs=[SMEM] + [VMEM] * (3 + 2 * blocks),
        out_specs=(VMEM, VMEM),
        scratch_shapes=[pltpu.VMEM((rows, width), BF16), pltpu.VMEM(x.shape, BF16)],
        compiler_params=pltpu.CompilerParams(vmem_limit_bytes=32 * 2**20),
        cost_estimate=pl.CostEstimate(
            flops=2 * rows * width * (w.shape[1] + 2 * blocks * rows),
            bytes_accessed=2 * w.size + 6 * half * w.shape[1],
            transcendentals=rows * rows * blocks * width // HD,
        ),
    )(place, q, x, w, *keys, *values)


def local_kernel(place, g0, g1, embed, gain, *refs, pieces):
    bridge = refs[:4]
    whole = refs[4:6]
    parts = refs[6 : 6 + 4 * pieces]
    out, bw, hid = refs[6 + 4 * pieces :]
    dp, sub, grp = place[1], place[2], place[3]
    patches = g0.shape[0]
    bytes_ = g0.shape[1] // DSLICE
    rows = patches * bytes_
    depth = bridge[0].shape[0]
    blocks = [dp * 2 + sub, dp * 2 + 1 - sub, (1 - dp) * 2 + sub, (1 - dp) * 2 + 1 - sub]
    for b, ref in zip(blocks, bridge):
        bw[pl.ds(pl.multiple_of(b * depth, depth), depth), :] = ref[...]
    glob = (g0[...] + g1[...].astype(F32)).astype(BF16)
    stacked = jnp.concatenate(
        [glob[:, p * DSLICE : (p + 1) * DSLICE] for p in range(bytes_)], axis=0
    )
    to = lax.broadcasted_iota(jnp.int32, (rows, rows), 0)
    frm = lax.broadcasted_iota(jnp.int32, (rows, rows), 1)
    pick = ((to % bytes_) * patches + to // bytes_ == frm).astype(BF16)
    by_patch = dot(pick, stacked).astype(BF16)
    byte_in = embed[...].astype(F32) + dot(by_patch, bw[...])
    mean_square = jnp.mean(byte_in * byte_in, axis=1, keepdims=True)
    hid[...] = (byte_in * lax.rsqrt(mean_square + 1e-05) * gain[...]).astype(BF16)
    width = whole[0].shape[1]
    for b, ref in zip(blocks[:2], whole):
        out[:, pl.ds(pl.multiple_of(b * width, 128), width)] = dot(hid[...], ref[...]).astype(BF16)
    k = parts[0].shape[0]
    half = k * pieces
    for i, b in enumerate(blocks[2:]):
        total = None
        for j in range(2):
            first = (grp if j == 0 else 1 - grp) * half
            for n in range(pieces):
                ref = parts[(i * 2 + j) * pieces + n]
                lhs = hid[:, pl.ds(pl.multiple_of(first + n * k, k), k)]
                term = dot(lhs, ref[...])
                total = term if total is None else total + term
        out[:, pl.ds(pl.multiple_of(b * width, 128), width)] = total.astype(BF16)


def local(place, g0, g1, embed, gain, bridge, whole, parts):
    rows = embed.shape[0]
    width = 4 * whole[0].shape[1]
    pieces = len(parts) // 4
    return pl.pallas_call(
        functools.partial(local_kernel, pieces=pieces),
        out_shape=jax.ShapeDtypeStruct((rows, width), BF16),
        in_specs=[SMEM] + [VMEM] * (4 + 4 + 2 + len(parts)),
        out_specs=VMEM,
        scratch_shapes=[pltpu.VMEM((DSLICE, DL), BF16), pltpu.VMEM((rows, DL), BF16)],
        compiler_params=pltpu.CompilerParams(vmem_limit_bytes=40 * 2**20),
        cost_estimate=pl.CostEstimate(
            flops=2 * rows * DL * (width + DSLICE),
            bytes_accessed=2 * DL * width + 2 * rows * width,
            transcendentals=rows,
        ),
    )(place, g0, g1, embed, gain, *bridge, *whole, *parts)


def swap(x, axis):
    return lax.ppermute(x, axis, [(0, 1), (1, 0)])


def small_mesh(
    q_glob, k_glob, v_glob, x_glob, out_weight, bridge_weight, byte_embed, norm_gain, qkv_weight
):
    ctx_size = lax.axis_size("ctx")
    ctx, dp, sub, grp = (lax.axis_index(a) for a in ("ctx", "dp", "sub", "groups"))
    place = jnp.stack([ctx, dp, sub, grp]).astype(jnp.int32)
    keys, values = [k_glob], [v_glob]
    for s in range(1, ctx_size):
        hops = [(i, i + s) for i in range(ctx_size - s)]
        keys.append(lax.ppermute(k_glob, "ctx", hops))
        values.append(lax.ppermute(v_glob, "ctx", hops))

    pieces = 2
    depth = qkv_weight.shape[0] // 2 // pieces
    fetched = []
    for n in range(pieces):
        piece = lax.dynamic_slice_in_dim(qkv_weight, (grp * pieces + n) * depth, depth, 0)
        fetched.append(swap(piece, "dp"))
    passed = [swap(f, "groups") for f in fetched]
    core_fetched = [swap(f, "sub") for f in fetched]
    core_passed = [swap(f, "sub") for f in passed]
    other_core = swap(qkv_weight, "sub")
    bridge_chip = swap(bridge_weight, "dp")
    bridge = [bridge_weight, swap(bridge_weight, "sub"), bridge_chip, swap(bridge_chip, "sub")]

    away, kept = attend_project(place, q_glob, x_glob, out_weight, keys, values)
    summed = kept + swap(away, "sub").astype(F32)
    mid = summed.shape[0] // 2
    across = swap(summed[:mid].astype(BF16), "dp")
    rows = byte_embed.shape[0] * byte_embed.shape[1]
    result = local(
        place,
        summed[mid:],
        across,
        byte_embed.reshape(rows, DL),
        norm_gain.reshape(1, DL),
        bridge,
        [qkv_weight, other_core],
        fetched + passed + core_fetched + core_passed,
    )
    return result.reshape(byte_embed.shape[0], P_SIZE, result.shape[1])


def solution(mesh):
    rows = P(("groups", "ctx"), GROUP)
    in_specs = (
        rows,
        rows,
        rows,
        rows,
        P(GROUP, None),
        P(GROUP, None),
        P(("groups", "ctx", "dp", "sub"), None, None),
        P(),
        P(None, GROUP),
    )
    out_specs = P(("groups", "ctx", "dp", "sub"), None, None)
    pairs = all(mesh.shape[a] == 2 for a in ("groups", "dp", "sub"))
    per_device = small_mesh if pairs and mesh.shape["ctx"] <= 4 else any_mesh
    return jax.shard_map(
        per_device, mesh=mesh, in_specs=in_specs, out_specs=out_specs, check_vma=False
    )
```

time: 150 us -> 70.3 us (0.47)
  the two profiles are of different devices: /device:TPU:25 before, /device:TPU:20 now
where the time goes in v1:
time: 70.3 us; the launch traced here: 70 us
  waiting for transfers between devices  41.8 us (59%)
  starting transfers between devices  16.9 us (24%)
  Pallas kernels  7.49 us (11%)
  local copies, waits for them, and re-layouts  3.45 us (5%)
    ppermute x14, waiting for transfers between devices, swap(): return lax.ppermute(x, axis, [(0, 1), (1, 0)])  25 us
    ppermute x3, waiting for transfers between devices, small_mesh(): keys.append(lax.ppermute(k_glob, 'ctx', hops))  9.57 us
    ppermute x14, starting transfers between devices, swap(): return lax.ppermute(x, axis, [(0, 1), (1, 0)])  7.44 us
    ppermute x3, waiting for transfers between devices, small_mesh(): values.append(lax.ppermute(v_glob, 'ctx', hops))  7.23 us
    ppermute x3, starting transfers between devices, small_mesh(): keys.append(lax.ppermute(k_glob, 'ctx', hops))  5.58 us
    pallas_call x1, Pallas kernels, local(): pl.pallas_call(functools.partial(local_kernel, pieces=pieces), out_shape=...  4.73 us
    ppermute x3, starting transfers between devices, small_mesh(): values.append(lax.ppermute(v_glob, 'ctx', hops))  3.87 us
    pallas_call x1, Pallas kernels, attend_project(): pl.pallas_call(functools.partial(attend_project_kernel, heads=width // HD...  2.75 us
  transfers between devices with their start and end apart: 20, of which 6 were waited for; matrix products, arithmetic and copies ran while one was open for 2% of the time, Pallas kernels for 4%

profile of v1, /device:TPU:20, one launch (start us, length us, event | category | flops | bytes accessed | tf_op | source)
XLA Modules:
  0.0 70.0 jit_solution(4276852045127123232)
XLA Ops:
  0.0 1.4 %collective-permute-start.1 = (bf16[128,512]{1,0:T(8,128)(2,1)}, bf16[128,512]{1,0:T(8,128)(2,1)S(1)}, u32[]{:S(2)}, u32[]{:S(2)}) collective-permute-start(bf16[128,512]{1,0:T(8,128)(2,1)} %refs_0_.2), channel_id=1, source_target_pairs={{0,8},{4,12},{1,9},{5,13},{2,10},{6,14},{3,11},{7,15},{16,24},{20,... | collective-permute-start | bytes 393224 | tf_op jit(solution)/shard_map/ppermute | solution.py:206
  1.5 3.5 %collective-permute-start = (bf16[128,512]{1,0:T(8,128)(2,1)}, bf16[128,512]{1,0:T(8,128)(2,1)S(1)}, u32[]{:S(2)}, u32[]{:S(2)}) collective-permute-start(bf16[128,512]{1,0:T(8,128)(2,1)} %refs_0_.2), channel_id=1, source_target_pairs={{0,4},{4,8},{8,12},{1,5},{5,9},{9,13},{2,6},{6,10},{10,14},{3,7},{... | collective-permute-start | bytes 393224 | tf_op jit(solution)/shard_map/ppermute | solution.py:206
  5.0 0.7 collective-permute-start.2
  5.6 1.3 %collective-permute-start.4 = (bf16[128,512]{1,0:T(8,128)(2,1)}, bf16[128,512]{1,0:T(8,128)(2,1)S(1)}, u32[]{:S(2)}, u32[]{:S(2)}) collective-permute-start(bf16[128,512]{1,0:T(8,128)(2,1)} %refs_4_.2), channel_id=1, source_target_pairs={{0,8},{4,12},{1,9},{5,13},{2,10},{6,14},{3,11},{7,15},{16,24},{20,... | collective-permute-start | bytes 393224 | tf_op jit(solution)/shard_map/ppermute | solution.py:207
  6.9 1.2 %constant_dynamic-slice_fusion = (bf16[256,768]{1,0:T(8,128)(2,1)S(1)}, bf16[256,768]{1,0:T(8,128)(2,1)S(1)}) fusion(bf16[1024,768]{1,0:T(8,128)(2,1)} %refs_4_.3, s32[]{:T(128)S(6)} %select_n.7, s32[]{:T(128)S(6)} %select_n.6), kind=kLoop, calls=%fused_computation.3 | loop fusion | bytes 1572872 | tf_op jit(solution)/shard_map/dynamic_slice | solution.py:213
  8.1 1.6 %collective-permute-start.13 = (bf16[256,768]{1,0:T(8,128)(2,1)S(1)}, bf16[256,768]{1,0:T(8,128)(2,1)S(1)}, u32[]{:S(2)}, u32[]{:S(2)}) collective-permute-start(bf16[256,768]{1,0:T(8,128)(2,1)S(1)} %get-tuple-element.9), channel_id=1, source_target_pairs={{0,2},{2,0},{1,3},{3,1},{4,6},{6,4},{5,7},{7,5},{8,10},{10,8},{9,1... | collective-permute-start | bytes 1179656 | tf_op jit(solution)/shard_map/ppermute | solution.py:194
  9.7 0.5 collective-permute-start.12
  10.2 9.6 %collective-permute-done.refs_1_ = bf16[128,512]{1,0:T(8,128)(2,1)S(1)} collective-permute-done((bf16[128,512]{1,0:T(8,128)(2,1)}, bf16[128,512]{1,0:T(8,128)(2,1)S(1)}, u32[]{:S(2)}, u32[]{:S(2)}) %collective-permute-start) | collective-permute-done | bytes 131104 | tf_op jit(solution)/shard_map/ppermute | solution.py:206
  19.8 1.9 %collective-permute-start.3 = (bf16[128,512]{1,0:T(8,128)(2,1)S(1)}, bf16[128,512]{1,0:T(8,128)(2,1)S(1)}, u32[]{:S(2)}, u32[]{:S(2)}) collective-permute-start(bf16[128,512]{1,0:T(8,128)(2,1)S(1)} %copy-done.7), channel_id=1, source_target_pairs={{0,4},{4,8},{8,12},{1,5},{5,9},{9,13},{2,6},{6,10},{10,14},{3,7},{... | collective-permute-start | bytes 393224 | tf_op jit(solution)/shard_map/ppermute | solution.py:207
  21.7 0.7 collective-permute-start.5
  22.4 0.1 collective-permute-start.8
  22.5 0.1 pad_add_fusion.place
  22.6 7.2 %collective-permute-done.3.refs_5_ = bf16[128,512]{1,0:T(8,128)(2,1)S(1)} collective-permute-done((bf16[128,512]{1,0:T(8,128)(2,1)S(1)}, bf16[128,512]{1,0:T(8,128)(2,1)S(1)}, u32[]{:S(2)}, u32[]{:S(2)}) %collective-permute-start.3) | collective-permute-done | bytes 131104 | tf_op jit(solution)/shard_map/ppermute | solution.py:207
  29.8 1.5 %collective-permute-start.9 = (bf16[128,1024]{1,0:T(8,128)(2,1)S(1)}, bf16[128,1024]{1,0:T(8,128)(2,1)S(1)}, u32[]{:S(2)}, u32[]{:S(2)}) collective-permute-start(bf16[128,1024]{1,0:T(8,128)(2,1)S(1)} %copy-done.4), channel_id=1, source_target_pairs={{0,2},{2,0},{1,3},{3,1},{4,6},{6,4},{5,7},{7,5},{8,10},{10,8},{9,1... | collective-permute-start | bytes 786440 | tf_op jit(solution)/shard_map/ppermute | solution.py:194
  31.3 0.0 copy-start
  31.3 2.2 %copy-done = bf16[512,4096]{1,0:T(8,128)(2,1)S(1)} copy-done((bf16[512,4096]{1,0:T(8,128)(2,1)S(1)}, bf16[512,4096]{1,0:T(8,128)(2,1)}, u32[]{:S(2)}) %copy-start) | copy-done | bytes 4194328
  33.5 2.8 %shard_map.91 = (bf16[64,4096]{1,0:T(8,128)(2,1)S(1)}, f32[64,4096]{1,0:T(8,128)S(1)}) custom-call(s32[4]{0:T(128)S(1)} %pad_add_fusion.place, bf16[128,512]{1,0:T(8,128)(2,1)S(1)} %copy-done.5, bf16[128,1024]{1,0:T(8,128)(2,1)S(1)} %copy-done.3, bf16[512,4096]{1,0:T(8,128)(2,1)S(1)} %copy-done, bf16[128,512]{1,0:T(8,128)(2,1)S(1)} %copy-done.6, ...), custom_call_target="tpu_custom_call" | custom-call | flops 671088640 | bytes 5767168 | tf_op jit(solution)/shard_map/pallas_call | solution.py:115
  36.3 0.1 collective-permute-start.6
  36.3 0.0 collective-permute-done.13.refs_7_
  36.4 0.6 collective-permute-start.15
  36.9 0.0 collective-permute-done.12.refs_6_
  36.9 1.5 %collective-permute-start.14 = (bf16[256,768]{1,0:T(8,128)(2,1)S(1)}, bf16[256,768]{1,0:T(8,128)(2,1)S(1)}, u32[]{:S(2)}, u32[]{:S(2)}) collective-permute-start(bf16[256,768]{1,0:T(8,128)(2,1)S(1)} %collective-permute-done.12.refs_6_), channel_id=1, source_target_pairs={{0,16},{16,0},{1,17},{17,1},{2,18},{18,2},{3,19},{19,3},{4,20},{20... | collective-permute-start | bytes 1179656 | tf_op jit(solution)/shard_map/ppermute | solution.py:194
  38.5 0.5 collective-permute-start.10
  39.0 3.3 %collective-permute-done.10.refs_3_ = bf16[128,1024]{1,0:T(8,128)(2,1)S(1)} collective-permute-done((bf16[128,1024]{1,0:T(8,128)(2,1)S(1)}, bf16[128,1024]{1,0:T(8,128)(2,1)S(1)}, u32[]{:S(2)}, u32[]{:S(2)}) %collective-permute-start.10) | collective-permute-done | bytes 262176 | tf_op jit(solution)/shard_map/ppermute | solution.py:194
  42.2 0.1 collective-permute-start.17
  42.4 0.4 collective-permute-start.16
  42.8 5.6 %collective-permute-done.15.refs_9_ = bf16[256,768]{1,0:T(8,128)(2,1)S(1)} collective-permute-done((bf16[256,768]{1,0:T(8,128)(2,1)S(1)}, bf16[256,768]{1,0:T(8,128)(2,1)S(1)}, u32[]{:S(2)}, u32[]{:S(2)}) %collective-permute-start.15) | collective-permute-done | bytes 393248 | tf_op jit(solution)/shard_map/ppermute | solution.py:194
  48.3 8.0 %collective-permute-done.14.refs_8_ = bf16[256,768]{1,0:T(8,128)(2,1)S(1)} collective-permute-done((bf16[256,768]{1,0:T(8,128)(2,1)S(1)}, bf16[256,768]{1,0:T(8,128)(2,1)S(1)}, u32[]{:S(2)}, u32[]{:S(2)}) %collective-permute-start.14) | collective-permute-done | bytes 393248 | tf_op jit(solution)/shard_map/ppermute | solution.py:194
  56.3 0.1 convert_add_fusion
  56.5 0.6 collective-permute-start.7
  57.1 8.1 %collective-permute-done.7.g1 = bf16[32,4096]{1,0:T(8,128)(2,1)S(1)} collective-permute-done((bf16[32,4096]{1,0:T(8,128)(2,1)S(1)}, bf16[32,4096]{1,0:T(8,128)(2,1)S(1)}, u32[]{:S(2)}, u32[]{:S(2)}) %collective-permute-start.7) | collective-permute-done | bytes 262176 | tf_op jit(solution)/shard_map/ppermute | solution.py:194
  65.3 4.7 %shard_map.92 = bf16[256,3072]{1,0:T(8,128)(2,1)} custom-call(s32[4]{0:T(128)S(1)} %pad_add_fusion.place, f32[32,4096]{1,0:T(8,128)S(1)} %slice.9.g0, bf16[32,4096]{1,0:T(8,128)(2,1)S(1)} %collective-permute-done.7.g1, bf16[256,1024]{1,0:T(8,128)(2,1)S(1)} %bitcast.7, f32[1,1024]{1,0:T(1,128)S(1)} %bitcast.8, bf16[128,1024]{1,0:T(8,128)(2,1)S(1)} %copy-done.4, ...), custom_call_target="tpu_custom_call" | custom-call | flops 1879048192 | bytes 7864320 | tf_op jit(solution)/shard_map/pallas_call | solution.py:178
  (33 shorter events, 0.1 us)
Async XLA Ops:
  0.0 31.3 %copy-start.6 = (bf16[128,512]{1,0:T(8,128)(2,1)S(1)}, bf16[128,512]{1,0:T(8,128)(2,1)}, u32[]{:S(2)}) copy-start(bf16[128,512]{1,0:T(8,128)(2,1)} %refs_0_.2) | copy-start | bytes 393220
  0.0 19.8 %copy-start.7 = (bf16[128,512]{1,0:T(8,128)(2,1)S(1)}, bf16[128,512]{1,0:T(8,128)(2,1)}, u32[]{:S(2)}) copy-start(bf16[128,512]{1,0:T(8,128)(2,1)} %refs_4_.2) | copy-start | bytes 393220
  0.0 22.4 %copy-start.4 = (bf16[128,1024]{1,0:T(8,128)(2,1)S(1)}, bf16[128,1024]{1,0:T(8,128)(2,1)}, u32[]{:S(2)}) copy-start(bf16[128,1024]{1,0:T(8,128)(2,1)} %refs_0_.3) | copy-start | bytes 786436
  0.0 31.3 %copy-start.3 = (bf16[128,1024]{1,0:T(8,128)(2,1)S(1)}, bf16[128,1024]{1,0:T(8,128)(2,1)}, u32[]{:S(2)}) copy-start(bf16[128,1024]{1,0:T(8,128)(2,1)} %x.1) | copy-start | bytes 786436
  0.0 31.3 %copy-start.5 = (bf16[128,512]{1,0:T(8,128)(2,1)S(1)}, bf16[128,512]{1,0:T(8,128)(2,1)}, u32[]{:S(2)}) copy-start(bf16[128,512]{1,0:T(8,128)(2,1)} %q.1) | copy-start | bytes 393220
  0.0 9.6 %collective-permute-start.1 = (bf16[128,512]{1,0:T(8,128)(2,1)}, bf16[128,512]{1,0:T(8,128)(2,1)S(1)}, u32[]{:S(2)}, u32[]{:S(2)}) collective-permute-start(bf16[128,512]{1,0:T(8,128)(2,1)} %refs_0_.2), channel_id=1, source_target_pairs={{0,8},{4,12},{1,9},{5,13},{2,10},{6,14},{3,11},{7,15},{16,24},{20,... | collective-permute-start | bytes 393224 | tf_op jit(solution)/shard_map/ppermute | solution.py:206
  1.5 18.3 %collective-permute-start = (bf16[128,512]{1,0:T(8,128)(2,1)}, bf16[128,512]{1,0:T(8,128)(2,1)S(1)}, u32[]{:S(2)}, u32[]{:S(2)}) collective-permute-start(bf16[128,512]{1,0:T(8,128)(2,1)} %refs_0_.2), channel_id=1, source_target_pairs={{0,4},{4,8},{8,12},{1,5},{5,9},{9,13},{2,6},{6,10},{10,14},{3,7},{... | collective-permute-start | bytes 393224 | tf_op jit(solution)/shard_map/ppermute | solution.py:206
  5.0 16.7 %collective-permute-start.2 = (bf16[128,512]{1,0:T(8,128)(2,1)}, bf16[128,512]{1,0:T(8,128)(2,1)S(1)}, u32[]{:S(2)}, u32[]{:S(2)}) collective-permute-start(bf16[128,512]{1,0:T(8,128)(2,1)} %refs_0_.2), channel_id=1, source_target_pairs={{0,12},{1,13},{2,14},{3,15},{16,28},{17,29},{18,30},{19,31}} | collective-permute-start | bytes 393224 | tf_op jit(solution)/shard_map/ppermute | solution.py:206
  5.6 16.8 %collective-permute-start.4 = (bf16[128,512]{1,0:T(8,128)(2,1)}, bf16[128,512]{1,0:T(8,128)(2,1)S(1)}, u32[]{:S(2)}, u32[]{:S(2)}) collective-permute-start(bf16[128,512]{1,0:T(8,128)(2,1)} %refs_4_.2), channel_id=1, source_target_pairs={{0,8},{4,12},{1,9},{5,13},{2,10},{6,14},{3,11},{7,15},{16,24},{20,... | collective-permute-start | bytes 393224 | tf_op jit(solution)/shard_map/ppermute | solution.py:207
  8.1 28.2 %collective-permute-start.13 = (bf16[256,768]{1,0:T(8,128)(2,1)S(1)}, bf16[256,768]{1,0:T(8,128)(2,1)S(1)}, u32[]{:S(2)}, u32[]{:S(2)}) collective-permute-start(bf16[256,768]{1,0:T(8,128)(2,1)S(1)} %get-tuple-element.9), channel_id=1, source_target_pairs={{0,2},{2,0},{1,3},{3,1},{4,6},{6,4},{5,7},{7,5},{8,10},{10,8},{9,1... | collective-permute-start | bytes 1179656 | tf_op jit(solution)/shard_map/ppermute | solution.py:194
  9.7 27.3 %collective-permute-start.12 = (bf16[256,768]{1,0:T(8,128)(2,1)S(1)}, bf16[256,768]{1,0:T(8,128)(2,1)S(1)}, u32[]{:S(2)}, u32[]{:S(2)}) collective-permute-start(bf16[256,768]{1,0:T(8,128)(2,1)S(1)} %get-tuple-element.10), channel_id=1, source_target_pairs={{0,2},{2,0},{1,3},{3,1},{4,6},{6,4},{5,7},{7,5},{8,10},{10,8},{9,1... | collective-permute-start | bytes 1179656 | tf_op jit(solution)/shard_map/ppermute | solution.py:194
  19.8 10.0 %collective-permute-start.3 = (bf16[128,512]{1,0:T(8,128)(2,1)S(1)}, bf16[128,512]{1,0:T(8,128)(2,1)S(1)}, u32[]{:S(2)}, u32[]{:S(2)}) collective-permute-start(bf16[128,512]{1,0:T(8,128)(2,1)S(1)} %copy-done.7), channel_id=1, source_target_pairs={{0,4},{4,8},{8,12},{1,5},{5,9},{9,13},{2,6},{6,10},{10,14},{3,7},{... | collective-permute-start | bytes 393224 | tf_op jit(solution)/shard_map/ppermute | solution.py:207
  21.7 9.6 %collective-permute-start.5 = (bf16[128,512]{1,0:T(8,128)(2,1)S(1)}, bf16[128,512]{1,0:T(8,128)(2,1)S(1)}, u32[]{:S(2)}, u32[]{:S(2)}) collective-permute-start(bf16[128,512]{1,0:T(8,128)(2,1)S(1)} %copy-done.7), channel_id=1, source_target_pairs={{0,12},{1,13},{2,14},{3,15},{16,28},{17,29},{18,30},{19,31}} | collective-permute-start | bytes 393224 | tf_op jit(solution)/shard_map/ppermute | solution.py:207
  22.4 16.0 %collective-permute-start.8 = (bf16[128,1024]{1,0:T(8,128)(2,1)S(1)}, bf16[128,1024]{1,0:T(8,128)(2,1)S(1)}, u32[]{:S(2)}, u32[]{:S(2)}) collective-permute-start(bf16[128,1024]{1,0:T(8,128)(2,1)S(1)} %copy-done.4), channel_id=1, source_target_pairs={{0,1},{1,0},{2,3},{3,2},{4,5},{5,4},{6,7},{7,6},{8,9},{9,8},{10,11... | collective-permute-start | bytes 786440 | tf_op jit(solution)/shard_map/ppermute | solution.py:194
  29.8 8.7 %collective-permute-start.9 = (bf16[128,1024]{1,0:T(8,128)(2,1)S(1)}, bf16[128,1024]{1,0:T(8,128)(2,1)S(1)}, u32[]{:S(2)}, u32[]{:S(2)}) collective-permute-start(bf16[128,1024]{1,0:T(8,128)(2,1)S(1)} %copy-done.4), channel_id=1, source_target_pairs={{0,2},{2,0},{1,3},{3,1},{4,6},{6,4},{5,7},{7,5},{8,10},{10,8},{9,1... | collective-permute-start | bytes 786440 | tf_op jit(solution)/shard_map/ppermute | solution.py:194
  31.3 2.2 %copy-start = (bf16[512,4096]{1,0:T(8,128)(2,1)S(1)}, bf16[512,4096]{1,0:T(8,128)(2,1)}, u32[]{:S(2)}) copy-start(bf16[512,4096]{1,0:T(8,128)(2,1)} %w.1) | copy-start | bytes 12582916
  33.5 5.0 %copy-start.1 = (bf16[1024,768]{1,0:T(8,128)(2,1)S(1)}, bf16[1024,768]{1,0:T(8,128)(2,1)}, u32[]{:S(2)}) copy-start(bf16[1024,768]{1,0:T(8,128)(2,1)} %refs_4_.3) | copy-start | bytes 4718596
  36.3 6.1 %collective-permute-start.6 = (bf16[64,4096]{1,0:T(8,128)(2,1)S(1)}, bf16[64,4096]{1,0:T(8,128)(2,1)S(1)}, u32[]{:S(2)}, u32[]{:S(2)}) collective-permute-start(bf16[64,4096]{1,0:T(8,128)(2,1)S(1)} %get-tuple-element.8), channel_id=1, source_target_pairs={{0,1},{1,0},{2,3},{3,2},{4,5},{5,4},{6,7},{7,6},{8,9},{9,8},{10,11... | collective-permute-start | bytes 1572872 | tf_op jit(solution)/shard_map/ppermute | solution.py:194
  36.4 12.0 %collective-permute-start.15 = (bf16[256,768]{1,0:T(8,128)(2,1)S(1)}, bf16[256,768]{1,0:T(8,128)(2,1)S(1)}, u32[]{:S(2)}, u32[]{:S(2)}) collective-permute-start(bf16[256,768]{1,0:T(8,128)(2,1)S(1)} %collective-permute-done.13.refs_7_), channel_id=1, source_target_pairs={{0,16},{16,0},{1,17},{17,1},{2,18},{18,2},{3,19},{19,3},{4,20},{20... | collective-permute-start | bytes 1179656 | tf_op jit(solution)/shard_map/ppermute | solution.py:194
  36.9 19.4 %collective-permute-start.14 = (bf16[256,768]{1,0:T(8,128)(2,1)S(1)}, bf16[256,768]{1,0:T(8,128)(2,1)S(1)}, u32[]{:S(2)}, u32[]{:S(2)}) collective-permute-start(bf16[256,768]{1,0:T(8,128)(2,1)S(1)} %collective-permute-done.12.refs_6_), channel_id=1, source_target_pairs={{0,16},{16,0},{1,17},{17,1},{2,18},{18,2},{3,19},{19,3},{4,20},{20... | collective-permute-start | bytes 1179656 | tf_op jit(solution)/shard_map/ppermute | solution.py:194
  38.5 26.8 %collective-permute-start.11 = (bf16[1024,768]{1,0:T(8,128)(2,1)S(1)}, bf16[1024,768]{1,0:T(8,128)(2,1)S(1)}, u32[]{:S(2)}, u32[]{:S(2)}) collective-permute-start(bf16[1024,768]{1,0:T(8,128)(2,1)S(1)} %copy-done.1), channel_id=1, source_target_pairs={{0,1},{1,0},{2,3},{3,2},{4,5},{5,4},{6,7},{7,6},{8,9},{9,8},{10,11... | collective-permute-start | bytes 4718600 | tf_op jit(solution)/shard_map/ppermute | solution.py:194
  38.5 3.8 %collective-permute-start.10 = (bf16[128,1024]{1,0:T(8,128)(2,1)S(1)}, bf16[128,1024]{1,0:T(8,128)(2,1)S(1)}, u32[]{:S(2)}, u32[]{:S(2)}) collective-permute-start(bf16[128,1024]{1,0:T(8,128)(2,1)S(1)} %collective-permute-done.9.refs_2_), channel_id=1, source_target_pairs={{0,1},{1,0},{2,3},{3,2},{4,5},{5,4},{6,7},{7,6},{8,9},{9,8},{10,11... | collective-permute-start | bytes 786440 | tf_op jit(solution)/shard_map/ppermute | solution.py:194
  42.2 14.2 %collective-permute-start.17 = (bf16[256,768]{1,0:T(8,128)(2,1)S(1)}, bf16[256,768]{1,0:T(8,128)(2,1)S(1)}, u32[]{:S(2)}, u32[]{:S(2)}) collective-permute-start(bf16[256,768]{1,0:T(8,128)(2,1)S(1)} %collective-permute-done.13.refs_7_), channel_id=1, source_target_pairs={{0,1},{1,0},{2,3},{3,2},{4,5},{5,4},{6,7},{7,6},{8,9},{9,8},{10,11... | collective-permute-start | bytes 1179656 | tf_op jit(solution)/shard_map/ppermute | solution.py:194
  42.4 14.7 %collective-permute-start.16 = (bf16[256,768]{1,0:T(8,128)(2,1)S(1)}, bf16[256,768]{1,0:T(8,128)(2,1)S(1)}, u32[]{:S(2)}, u32[]{:S(2)}) collective-permute-start(bf16[256,768]{1,0:T(8,128)(2,1)S(1)} %collective-permute-done.12.refs_6_), channel_id=1, source_target_pairs={{0,1},{1,0},{2,3},{3,2},{4,5},{5,4},{6,7},{7,6},{8,9},{9,8},{10,11... | collective-permute-start | bytes 1179656 | tf_op jit(solution)/shard_map/ppermute | solution.py:194
  48.3 16.9 %collective-permute-start.19 = (bf16[256,768]{1,0:T(8,128)(2,1)S(1)}, bf16[256,768]{1,0:T(8,128)(2,1)S(1)}, u32[]{:S(2)}, u32[]{:S(2)}) collective-permute-start(bf16[256,768]{1,0:T(8,128)(2,1)S(1)} %collective-permute-done.15.refs_9_), channel_id=1, source_target_pairs={{0,1},{1,0},{2,3},{3,2},{4,5},{5,4},{6,7},{7,6},{8,9},{9,8},{10,11... | collective-permute-start | bytes 1179656 | tf_op jit(solution)/shard_map/ppermute | solution.py:194
  56.3 8.9 %collective-permute-start.18 = (bf16[256,768]{1,0:T(8,128)(2,1)S(1)}, bf16[256,768]{1,0:T(8,128)(2,1)S(1)}, u32[]{:S(2)}, u32[]{:S(2)}) collective-permute-start(bf16[256,768]{1,0:T(8,128)(2,1)S(1)} %collective-permute-done.14.refs_8_), channel_id=1, source_target_pairs={{0,1},{1,0},{2,3},{3,2},{4,5},{5,4},{6,7},{7,6},{8,9},{9,8},{10,11... | collective-permute-start | bytes 1179656 | tf_op jit(solution)/shard_map/ppermute | solution.py:194
  56.3 8.9 %copy-start.2 = (bf16[32,8,1024]{2,1,0:T(8,128)(2,1)S(1)}, bf16[32,8,1024]{2,1,0:T(8,128)(2,1)}, u32[]{:S(2)}) copy-start(bf16[32,8,1024]{2,1,0:T(8,128)(2,1)} %param.15) | copy-start | bytes 1572868
  56.3 9.0 %copy-start.8 = (f32[1024]{0:T(1024)S(1)}, f32[1024]{0:T(1024)}, u32[]{:S(2)}) copy-start(f32[1024]{0:T(1024)} %param.16) | copy-start | bytes 12292
  56.5 8.8 %collective-permute-start.7 = (bf16[32,4096]{1,0:T(8,128)(2,1)S(1)}, bf16[32,4096]{1,0:T(8,128)(2,1)S(1)}, u32[]{:S(2)}, u32[]{:S(2)}) collective-permute-start(bf16[32,4096]{1,0:T(8,128)(2,1)S(1)} %slice.12), channel_id=1, source_target_pairs={{0,2},{2,0},{1,3},{3,1},{4,6},{6,4},{5,7},{7,5},{8,10},{10,8},{9,1... | collective-permute-start | bytes 786440 | tf_op jit(solution)/shard_map/ppermute | solution.py:194

commit v2 on v1

--- a/solution.py
+++ b/solution.py
@@ -63,34 +63,105 @@
     return result.reshape(byte_embed.shape[0], P_SIZE, 3 * DL)
 
 
-def attend_project_kernel(
-    place, q, x, w, *refs, heads, blocks
-):
-    keys, values = refs[:blocks], refs[blocks : 2 * blocks]
-    away, kept, attn, xs = refs[2 * blocks :]
-    ctx, dp, sub = place[0], place[1], place[2]
-    rows = q.shape[0]
-    quarter = rows // 4
-    row = lax.broadcasted_iota(jnp.int32, (rows, rows), 0)
-    col = lax.broadcasted_iota(jnp.int32, (rows, rows), 1)
+def attend_kernel(place, q, q_up, q_up2, k, v, k_low, v_low, own, own_log, up, up2):
+    rows, width = q.shape
+    heads = width // HD
+    has_low = place[0] == 1
+    row = lax.broadcasted_iota(jnp.int32, (rows, 2 * rows), 0)
+    col = lax.broadcasted_iota(jnp.int32, (rows, 2 * rows), 1)
+    is_low = col >= rows
+    full = jnp.logical_or(col < rows, has_low)
+    causal = jnp.logical_or(row >= col, jnp.logical_and(is_low, has_low))
+    logs = [[], [], []]
     for h in range(heads):
         cols = pl.ds(h * HD, HD)
-        qh = q[:, cols]
-        scores = []
-        for s in range(blocks):
-            sc = lax.dot_general(
-                qh, keys[s][:, cols], (((1,), (1,)), ((), ())), preferred_element_type=F32
+        kh = jnp.concatenate([k[:, cols], k_low[:, cols]], axis=0)
+        vh = jnp.concatenate([v[:, cols], v_low[:, cols]], axis=0)
+        for i, (queries, mask, target) in enumerate(
+            ((q, causal, own), (q_up, full, up), (q_up2, full, up2))
+        ):
+            scores = lax.dot_general(
+                queries[:, cols], kh, (((1,), (1,)), ((), ())), preferred_element_type=F32
             ) * SCALE
-            keep = (row >= col) if s == 0 else (ctx >= s)
-            scores.append(jnp.where(keep, sc, -jnp.inf))
-        scores = jnp.concatenate(scores, axis=1)
-        probs = jnp.exp(scores - jnp.max(scores, axis=1, keepdims=True))
-        total = jnp.sum(probs, axis=1, keepdims=True)
-        probs = probs.astype(BF16)
-        mixed = dot(probs[:, :rows], values[0][:, cols])
-        for s in range(1, blocks):
-            mixed += dot(probs[:, s * rows : (s + 1) * rows], values[s][:, cols])
-        attn[:, cols] = (mixed / total).astype(BF16)
+            scores = jnp.where(mask, scores, -jnp.inf)
+            top = jnp.max(scores, axis=1, keepdims=True)
+            probs = jnp.exp(scores - top)
+            total = jnp.sum(probs, axis=1, keepdims=True)
+            mixed = dot(probs.astype(BF16), vh) / total
+            target[pl.ds(0, rows), cols] = mixed.astype(target.dtype)
+            logs[i].append(top + jnp.log(total))
+    lane = lax.broadcasted_iota(jnp.int32, (rows, HD), 1)
+
+    def by_lane(columns):
+        table = jnp.zeros((rows, HD), F32)
+        for i, column in enumerate(columns):
+            table = jnp.where(lane == i, column, table)
+        return table
+
+    own_log[...] = by_lane(logs[0])
+    for target, log in ((up, logs[1]), (up2, logs[2])):
+        terms = []
+        rest = log
+        for _ in range(3):
+            high = [r.astype(BF16).astype(F32) for r in rest]
+            rest = [r - t for r, t in zip(rest, high)]
+            terms += high
+        table = by_lane(terms).T
+        target[pl.ds(rows, 16), :] = jnp.zeros((16, width), BF16)
+        target[pl.ds(rows, 16), pl.ds(0, HD)] = table[:16, :rows].astype(BF16)
+
+
+def attend(place, q, q_up, q_up2, k, v, k_low, v_low):
+    rows, width = q.shape
+    sent = jax.ShapeDtypeStruct((rows + 16, width), BF16)
+    return pl.pallas_call(
+        attend_kernel,
+        out_shape=(
+            jax.ShapeDtypeStruct((rows, width), F32),
+            jax.ShapeDtypeStruct((rows, HD), F32),
+            sent,
+            sent,
+        ),
+        in_specs=[SMEM] + [VMEM] * 7,
+        out_specs=(VMEM,) * 4,
+        compiler_params=pltpu.CompilerParams(vmem_limit_bytes=16 * 2**20),
+        cost_estimate=pl.CostEstimate(
+            flops=24 * rows * rows * width,
+            bytes_accessed=24 * rows * width,
+            transcendentals=6 * rows * rows * width // HD,
+        ),
+    )(place, q, q_up, q_up2, k, v, k_low, v_low)
+
+
+def project_kernel(place, own, own_log, low, low2, x, w, away, kept, attn, xs):
+    ctx, dp, sub = place[0], place[1], place[2]
+    rows, width = own.shape
+    heads = width // HD
+    quarter = rows // 4
+    logs = [own_log[...]]
+    for part in (low, low2):
+        table = part[pl.ds(rows, 16), pl.ds(0, HD)].astype(F32)
+        table = jnp.concatenate([table, jnp.zeros((HD - 16, HD), F32)], axis=0).T
+        logs.append(table)
+    valid = (ctx >= 2, ctx >= 3)
+    for h in range(heads):
+        cols = pl.ds(h * HD, HD)
+        log = [logs[0][:, h : h + 1]]
+        for table, ok in zip(logs[1:], valid):
+            value = (
+                table[:, h : h + 1]
+                + table[:, heads + h : heads + h + 1]
+                + table[:, 2 * heads + h : 2 * heads + h + 1]
+            )
+            log.append(jnp.where(ok, value, -jnp.inf))
+        top = jnp.maximum(jnp.maximum(log[0], log[1]), log[2])
+        share = [jnp.exp(value - top) for value in log]
+        mixed = (
+            share[0] * own[:, cols]
+            + share[1] * low[pl.ds(0, rows), cols].astype(F32)
+            + share[2] * low2[pl.ds(0, rows), cols].astype(F32)
+        )
+        attn[:, cols] = (mixed / (share[0] + share[1] + share[2])).astype(BF16)
     order = []
     for core in (1 - sub, sub):
         for chip in (1 - dp, dp):
@@ -99,35 +170,34 @@
     for i, o in enumerate(order):
         xs[pl.ds(i * quarter, quarter), :] = x[o, :]
     block = x.shape[1]
-    own = dp * 2 + sub
+    mine = dp * 2 + sub
     for b in range(w.shape[1] // block):
         cols = pl.ds(b * block, block)
         terms = dot(a, w[:, cols])
-        terms += jnp.where(own == b, xs[...].astype(F32), 0.0)
+        terms += jnp.where(mine == b, xs[...].astype(F32), 0.0)
         away[:, cols] = terms[: 2 * quarter].astype(BF16)
         kept[:, cols] = terms[2 * quarter :]
 
 
-def attend_project(place, q, x, w, keys, values):
-    rows, width = q.shape
+def project(place, own, own_log, low, low2, x, w):
+    rows, width = own.shape
     half = rows // 2
-    blocks = len(keys)
     return pl.pallas_call(
-        functools.partial(attend_project_kernel, heads=width // HD, blocks=blocks),
+        project_kernel,
         out_shape=(
             jax.ShapeDtypeStruct((half, w.shape[1]), BF16),
             jax.ShapeDtypeStruct((half, w.shape[1]), F32),
         ),
-        in_specs=[SMEM] + [VMEM] * (3 + 2 * blocks),
+        in_specs=[SMEM] + [VMEM] * 6,
         out_specs=(VMEM, VMEM),
         scratch_shapes=[pltpu.VMEM((rows, width), BF16), pltpu.VMEM(x.shape, BF16)],
-        compiler_params=pltpu.CompilerParams(vmem_limit_bytes=32 * 2**20),
+        compiler_params=pltpu.CompilerParams(vmem_limit_bytes=24 * 2**20),
         cost_estimate=pl.CostEstimate(
-            flops=2 * rows * width * (w.shape[1] + 2 * blocks * rows),
+            flops=2 * rows * width * w.shape[1],
             bytes_accessed=2 * w.size + 6 * half * w.shape[1],
-            transcendentals=rows * rows * blocks * width // HD,
-        ),
-    )(place, q, x, w, *keys, *values)
+            transcendentals=3 * rows * width // HD,
+        ),
+    )(place, own, own_log, low, low2, x, w)
 
 
 def local_kernel(place, g0, g1, embed, gain, *refs, pieces):
@@ -197,29 +267,42 @@
 def small_mesh(
     q_glob, k_glob, v_glob, x_glob, out_weight, bridge_weight, byte_embed, norm_gain, qkv_weight
 ):
-    ctx_size = lax.axis_size("ctx")
     ctx, dp, sub, grp = (lax.axis_index(a) for a in ("ctx", "dp", "sub", "groups"))
     place = jnp.stack([ctx, dp, sub, grp]).astype(jnp.int32)
-    keys, values = [k_glob], [v_glob]
-    for s in range(1, ctx_size):
-        hops = [(i, i + s) for i in range(ctx_size - s)]
-        keys.append(lax.ppermute(k_glob, "ctx", hops))
-        values.append(lax.ppermute(v_glob, "ctx", hops))
-
     pieces = 2
     depth = qkv_weight.shape[0] // 2 // pieces
-    fetched = []
-    for n in range(pieces):
-        piece = lax.dynamic_slice_in_dim(qkv_weight, (grp * pieces + n) * depth, depth, 0)
-        fetched.append(swap(piece, "dp"))
-    passed = [swap(f, "groups") for f in fetched]
-    core_fetched = [swap(f, "sub") for f in fetched]
-    core_passed = [swap(f, "sub") for f in passed]
+    own_pieces = [
+        lax.dynamic_slice_in_dim(qkv_weight, (grp * pieces + n) * depth, depth, 0)
+        for n in range(pieces)
+    ]
+
+    fetched = [swap(own_pieces[0], "dp")]
+    bridge_chip = swap(bridge_weight, "dp")
+    bridge_core = swap(bridge_weight, "sub")
     other_core = swap(qkv_weight, "sub")
-    bridge_chip = swap(bridge_weight, "dp")
-    bridge = [bridge_weight, swap(bridge_weight, "sub"), bridge_chip, swap(bridge_chip, "sub")]
-
-    away, kept = attend_project(place, q_glob, x_glob, out_weight, keys, values)
+    k_low = lax.ppermute(k_glob, "ctx", [(0, 1)])
+    v_low = lax.ppermute(v_glob, "ctx", [(0, 1)])
+    q_up = lax.ppermute(q_glob, "ctx", [(2, 1), (3, 2)])
+    q_up2 = lax.ppermute(q_glob, "ctx", [(3, 1)])
+    (k_low, v_low, q_up, q_up2, fetched[0], bridge_chip, piece) = lax.optimization_barrier(
+        (k_low, v_low, q_up, q_up2, fetched[0], bridge_chip, own_pieces[1])
+    )
+
+    fetched.append(swap(piece, "dp"))
+    passed = [swap(fetched[0], "groups")]
+    core_fetched = [swap(fetched[0], "sub")]
+    bridge_both = swap(bridge_chip, "sub")
+    own, own_log, up, up2 = attend(place, q_glob, q_up, q_up2, k_glob, v_glob, k_low, v_low)
+    low = lax.ppermute(up, "ctx", [(1, 2), (2, 3)])
+    low2 = lax.ppermute(up2, "ctx", [(1, 3)])
+    (low, low2, fetched[1], passed[0]) = lax.optimization_barrier(
+        (low, low2, fetched[1], passed[0])
+    )
+
+    passed.append(swap(fetched[1], "groups"))
+    core_fetched.append(swap(fetched[1], "sub"))
+    core_passed = [swap(p, "sub") for p in passed]
+    away, kept = project(place, own, own_log, low, low2, x_glob, out_weight)
     summed = kept + swap(away, "sub").astype(F32)
     mid = summed.shape[0] // 2
     across = swap(summed[:mid].astype(BF16), "dp")
@@ -230,7 +313,7 @@
         across,
         byte_embed.reshape(rows, DL),
         norm_gain.reshape(1, DL),
-        bridge,
+        [bridge_weight, bridge_core, bridge_chip, bridge_both],
         [qkv_weight, other_core],
         fetched + passed + core_fetched + core_passed,
     )
@@ -252,7 +335,7 @@
     )
     out_specs = P(("groups", "ctx", "dp", "sub"), None, None)
     pairs = all(mesh.shape[a] == 2 for a in ("groups", "dp", "sub"))
-    per_device = small_mesh if pairs and mesh.shape["ctx"] <= 4 else any_mesh
+    per_device = small_mesh if pairs and mesh.shape["ctx"] == 4 else any_mesh
     return jax.shard_map(
         per_device, mesh=mesh, in_specs=in_specs, out_specs=out_specs, check_vma=False
     )

time: 70.3 us -> 62.2 us (0.88)
  the two profiles are of different devices: /device:TPU:20 before, /device:TPU:25 now
where the time goes in v2:
time: 62.2 us; the launch traced here: 61.3 us
  waiting for transfers between devices  29.2 us (47%)
  starting transfers between devices  19.9 us (32%)
  Pallas kernels  8.34 us (13%)
  local copies, waits for them, and re-layouts  3.53 us (6%)
    ppermute x14, waiting for transfers between devices, swap(): return lax.ppermute(x, axis, [(0, 1), (1, 0)])  20.5 us
    ppermute x14, starting transfers between devices, swap(): return lax.ppermute(x, axis, [(0, 1), (1, 0)])  9.71 us
    pallas_call x1, Pallas kernels, local(): pl.pallas_call(functools.partial(local_kernel, pieces=pieces), out_shape=...  4.73 us
    ppermute x1, starting transfers between devices, small_mesh(): q_up2 = lax.ppermute(q_glob, 'ctx', [(3, 1)])  4.18 us
    ppermute x1, waiting for transfers between devices, small_mesh(): low = lax.ppermute(up, 'ctx', [(1, 2), (2, 3)])  3.58 us
    ppermute x1, waiting for transfers between devices, small_mesh(): low2 = lax.ppermute(up2, 'ctx', [(1, 3)])  3.23 us
    unnamed x18, local copies, waits for them, and re-layouts  2.22 us
    ppermute x1, starting transfers between devices, small_mesh(): q_up = lax.ppermute(q_glob, 'ctx', [(2, 1), (3, 2)])  2.08 us
  transfers between devices with their start and end apart: 20, of which 9 were waited for; matrix products, arithmetic and copies ran while one was open for 0% of the time, Pallas kernels for 3%

profile of v2, /device:TPU:25, one launch (start us, length us, event | category | flops | bytes accessed | tf_op | source)
XLA Modules:
  0.0 61.3 jit_solution(2401696500785320464)
XLA Ops:
  0.0 1.2 %constant_dynamic-slice_fusion = (bf16[256,768]{1,0:T(8,128)(2,1)S(1)}, bf16[256,768]{1,0:T(8,128)(2,1)S(1)}) fusion(bf16[1024,768]{1,0:T(8,128)(2,1)} %refs_4_.1, s32[]{:T(128)S(6)} %select_n.7, s32[]{:T(128)S(6)} %select_n.6), kind=kLoop, calls=%fused_computation.3 | loop fusion | bytes 1572872 | tf_op jit(solution)/shard_map/dynamic_slice | solution.py:275
  1.3 1.3 %collective-permute-start.4 = (bf16[256,768]{1,0:T(8,128)(2,1)S(1)}, bf16[256,768]{1,0:T(8,128)(2,1)S(1)}, u32[]{:S(2)}, u32[]{:S(2)}) collective-permute-start(bf16[256,768]{1,0:T(8,128)(2,1)S(1)} %get-tuple-element.40), channel_id=1, source_target_pairs={{0,2},{2,0},{1,3},{3,1},{4,6},{6,4},{5,7},{7,5},{8,10},{10,8},{9,1... | collective-permute-start | bytes 1179656 | tf_op jit(solution)/shard_map/ppermute | solution.py:264
  2.6 0.7 %collective-permute-start = (bf16[128,512]{1,0:T(8,128)(2,1)S(1)}, bf16[128,512]{1,0:T(8,128)(2,1)S(1)}, u32[]{:S(2)}, u32[]{:S(2)}) collective-permute-start(bf16[128,512]{1,0:T(8,128)(2,1)S(1)} %copy-done.6), channel_id=1, source_target_pairs={{0,4},{1,5},{2,6},{3,7},{16,20},{17,21},{18,22},{19,23}} | collective-permute-start | bytes 393224 | tf_op jit(solution)/shard_map/ppermute | solution.py:283
  3.2 0.3 collective-permute-start.5
  3.6 0.7 %collective-permute-start.1 = (bf16[128,512]{1,0:T(8,128)(2,1)S(1)}, bf16[128,512]{1,0:T(8,128)(2,1)S(1)}, u32[]{:S(2)}, u32[]{:S(2)}) collective-permute-start(bf16[128,512]{1,0:T(8,128)(2,1)S(1)} %copy-done.7), channel_id=1, source_target_pairs={{0,4},{1,5},{2,6},{3,7},{16,20},{17,21},{18,22},{19,23}} | collective-permute-start | bytes 393224 | tf_op jit(solution)/shard_map/ppermute | solution.py:284
  4.2 2.1 %collective-permute-start.2 = (bf16[128,512]{1,0:T(8,128)(2,1)S(1)}, bf16[128,512]{1,0:T(8,128)(2,1)S(1)}, u32[]{:S(2)}, u32[]{:S(2)}) collective-permute-start(bf16[128,512]{1,0:T(8,128)(2,1)S(1)} %copy-done.5), channel_id=1, source_target_pairs={{8,4},{12,8},{9,5},{13,9},{10,6},{14,10},{11,7},{15,11},{24,20},{2... | collective-permute-start | bytes 393224 | tf_op jit(solution)/shard_map/ppermute | solution.py:285
  6.3 4.2 %collective-permute-start.3 = (bf16[128,512]{1,0:T(8,128)(2,1)S(1)}, bf16[128,512]{1,0:T(8,128)(2,1)S(1)}, u32[]{:S(2)}, u32[]{:S(2)}) collective-permute-start(bf16[128,512]{1,0:T(8,128)(2,1)S(1)} %copy-done.5), channel_id=1, source_target_pairs={{12,4},{13,5},{14,6},{15,7},{28,20},{29,21},{30,22},{31,23}} | collective-permute-start | bytes 393224 | tf_op jit(solution)/shard_map/ppermute | solution.py:286
  10.5 1.9 %collective-permute-done.3.q_up2 = bf16[128,512]{1,0:T(8,128)(2,1)S(1)} collective-permute-done((bf16[128,512]{1,0:T(8,128)(2,1)S(1)}, bf16[128,512]{1,0:T(8,128)(2,1)S(1)}, u32[]{:S(2)}, u32[]{:S(2)}) %collective-permute-start.3) | collective-permute-done | bytes 131104 | tf_op jit(solution)/shard_map/ppermute | solution.py:286
  12.4 4.5 %collective-permute-done.5.refs_2_ = bf16[128,1024]{1,0:T(8,128)(2,1)S(1)} collective-permute-done((bf16[128,1024]{1,0:T(8,128)(2,1)S(1)}, bf16[128,1024]{1,0:T(8,128)(2,1)S(1)}, u32[]{:S(2)}, u32[]{:S(2)}) %collective-permute-start.5) | collective-permute-done | bytes 262176 | tf_op jit(solution)/shard_map/ppermute | solution.py:264
  17.0 1.2 %collective-permute-start.8 = (bf16[256,768]{1,0:T(8,128)(2,1)S(1)}, bf16[256,768]{1,0:T(8,128)(2,1)S(1)}, u32[]{:S(2)}, u32[]{:S(2)}) collective-permute-start(bf16[256,768]{1,0:T(8,128)(2,1)S(1)} %get-tuple-element.30), channel_id=1, source_target_pairs={{0,2},{2,0},{1,3},{3,1},{4,6},{6,4},{5,7},{7,5},{8,10},{10,8},{9,1... | collective-permute-start | bytes 1179656 | tf_op jit(solution)/shard_map/ppermute | solution.py:264
  18.2 1.2 %collective-permute-start.9 = (bf16[256,768]{1,0:T(8,128)(2,1)S(1)}, bf16[256,768]{1,0:T(8,128)(2,1)S(1)}, u32[]{:S(2)}, u32[]{:S(2)}) collective-permute-start(bf16[256,768]{1,0:T(8,128)(2,1)S(1)} %collective-permute-done.4.refs_6_), channel_id=1, source_target_pairs={{0,16},{16,0},{1,17},{17,1},{2,18},{18,2},{3,19},{19,3},{4,20},{20... | collective-permute-start | bytes 1179656 | tf_op jit(solution)/shard_map/ppermute | solution.py:264
  19.5 1.8 %shard_map.91 = (f32[128,512]{1,0:T(8,128)S(1)}, f32[128,128]{1,0:T(8,128)S(1)}, bf16[144,512]{1,0:T(8,128)(2,1)S(1)}, bf16[144,512]{1,0:T(8,128)(2,1)S(1)}) custom-call(s32[4]{0:T(128)S(1)} %pad_add_fusion.place, bf16[128,512]{1,0:T(8,128)(2,1)S(1)} %copy-done.5, bf16[128,512]{1,0:T(8,128)(2,1)S(1)} %collective-permute-done.2.q_up, ...), custom_call_target="tpu_custom_call" | custom-call | flops 201326592 | bytes 1572864 | tf_op jit(solution)/shard_map/pallas_call | solution.py:117
  21.3 1.3 %collective-permute-start.6 = (bf16[144,512]{1,0:T(8,128)(2,1)S(1)}, bf16[144,512]{1,0:T(8,128)(2,1)S(1)}, u32[]{:S(2)}, u32[]{:S(2)}) collective-permute-start(bf16[144,512]{1,0:T(8,128)(2,1)S(1)} %get-tuple-element.28), channel_id=1, source_target_pairs={{4,8},{8,12},{5,9},{9,13},{6,10},{10,14},{7,11},{11,15},{20,24},{2... | collective-permute-start | bytes 442376 | tf_op jit(solution)/shard_map/ppermute | solution.py:296
  22.6 1.3 %collective-permute-start.7 = (bf16[144,512]{1,0:T(8,128)(2,1)S(1)}, bf16[144,512]{1,0:T(8,128)(2,1)S(1)}, u32[]{:S(2)}, u32[]{:S(2)}) collective-permute-start(bf16[144,512]{1,0:T(8,128)(2,1)S(1)} %get-tuple-element.29), channel_id=1, source_target_pairs={{4,12},{5,13},{6,14},{7,15},{20,28},{21,29},{22,30},{23,31}} | collective-permute-start | bytes 442376 | tf_op jit(solution)/shard_map/ppermute | solution.py:297
  23.9 3.6 %collective-permute-done.6.low = bf16[144,512]{1,0:T(8,128)(2,1)S(1)} collective-permute-done((bf16[144,512]{1,0:T(8,128)(2,1)S(1)}, bf16[144,512]{1,0:T(8,128)(2,1)S(1)}, u32[]{:S(2)}, u32[]{:S(2)}) %collective-permute-start.6) | collective-permute-done | bytes 147488 | tf_op jit(solution)/shard_map/ppermute | solution.py:296
  27.4 3.2 %collective-permute-done.7.low2 = bf16[144,512]{1,0:T(8,128)(2,1)S(1)} collective-permute-done((bf16[144,512]{1,0:T(8,128)(2,1)S(1)}, bf16[144,512]{1,0:T(8,128)(2,1)S(1)}, u32[]{:S(2)}, u32[]{:S(2)}) %collective-permute-start.7) | collective-permute-done | bytes 147488 | tf_op jit(solution)/shard_map/ppermute | solution.py:297
  30.7 2.2 %copy-done = bf16[512,4096]{1,0:T(8,128)(2,1)S(1)} copy-done((bf16[512,4096]{1,0:T(8,128)(2,1)S(1)}, bf16[512,4096]{1,0:T(8,128)(2,1)}, u32[]{:S(2)}) %copy-start) | copy-done | bytes 4194328
  32.9 1.8 %shard_map.92 = (bf16[64,4096]{1,0:T(8,128)(2,1)S(1)}, f32[64,4096]{1,0:T(8,128)S(1)}) custom-call(s32[4]{0:T(128)S(1)} %pad_add_fusion.place, f32[128,512]{1,0:T(8,128)S(1)} %get-tuple-element.26.own, f32[128,128]{1,0:T(8,128)S(1)} %get-tuple-element.27.own_log, bf16[144,512]{1,0:T(8,128)(2,1)S(1)} %collective-permute-done.6.low, ...), custom_call_target="tpu_custom_call" | custom-call | flops 536870912 | bytes 5767168 | tf_op jit(solution)/shard_map/pallas_call | solution.py:185
  34.7 2.7 %collective-permute-start.10 = (bf16[64,4096]{1,0:T(8,128)(2,1)S(1)}, bf16[64,4096]{1,0:T(8,128)(2,1)S(1)}, u32[]{:S(2)}, u32[]{:S(2)}) collective-permute-start(bf16[64,4096]{1,0:T(8,128)(2,1)S(1)} %get-tuple-element.35), channel_id=1, source_target_pairs={{0,1},{1,0},{2,3},{3,2},{4,5},{5,4},{6,7},{7,6},{8,9},{9,8},{10,11... | collective-permute-start | bytes 1572872 | tf_op jit(solution)/shard_map/ppermute | solution.py:264
  37.4 0.2 collective-permute-start.15
  37.6 0.3 collective-permute-start.14
  38.1 0.3 collective-permute-start.13
  38.5 3.1 %collective-permute-done.12.refs_1_ = bf16[128,1024]{1,0:T(8,128)(2,1)S(1)} collective-permute-done((bf16[128,1024]{1,0:T(8,128)(2,1)S(1)}, bf16[128,1024]{1,0:T(8,128)(2,1)S(1)}, u32[]{:S(2)}, u32[]{:S(2)}) %collective-permute-start.12) | collective-permute-done | bytes 262176 | tf_op jit(solution)/shard_map/ppermute | solution.py:264
  41.5 0.4 collective-permute-start.16
  41.9 0.4 collective-permute-start.17
  42.3 5.8 %collective-permute-done.15.refs_9_ = bf16[256,768]{1,0:T(8,128)(2,1)S(1)} collective-permute-done((bf16[256,768]{1,0:T(8,128)(2,1)S(1)}, bf16[256,768]{1,0:T(8,128)(2,1)S(1)}, u32[]{:S(2)}, u32[]{:S(2)}) %collective-permute-start.15) | collective-permute-done | bytes 393248 | tf_op jit(solution)/shard_map/ppermute | solution.py:264
  48.1 0.8 %collective-permute-start.18 = (bf16[256,768]{1,0:T(8,128)(2,1)S(1)}, bf16[256,768]{1,0:T(8,128)(2,1)S(1)}, u32[]{:S(2)}, u32[]{:S(2)}) collective-permute-start(bf16[256,768]{1,0:T(8,128)(2,1)S(1)} %collective-permute-done.9.refs_8_), channel_id=1, source_target_pairs={{0,1},{1,0},{2,3},{3,2},{4,5},{5,4},{6,7},{7,6},{8,9},{9,8},{10,11... | collective-permute-start | bytes 1179656 | tf_op jit(solution)/shard_map/ppermute | solution.py:264
  49.1 0.3 collective-permute-start.11
  49.5 0.8 %collective-permute-done.18.refs_12_ = bf16[256,768]{1,0:T(8,128)(2,1)S(1)} collective-permute-done((bf16[256,768]{1,0:T(8,128)(2,1)S(1)}, bf16[256,768]{1,0:T(8,128)(2,1)S(1)}, u32[]{:S(2)}, u32[]{:S(2)}) %collective-permute-start.18) | collective-permute-done | bytes 393248 | tf_op jit(solution)/shard_map/ppermute | solution.py:264
  50.3 0.6 collective-permute-done.19.refs_13_
  50.8 5.7 %collective-permute-done.11.g1 = bf16[32,4096]{1,0:T(8,128)(2,1)S(1)} collective-permute-done((bf16[32,4096]{1,0:T(8,128)(2,1)S(1)}, bf16[32,4096]{1,0:T(8,128)(2,1)S(1)}, u32[]{:S(2)}, u32[]{:S(2)}) %collective-permute-start.11) | collective-permute-done | bytes 262176 | tf_op jit(solution)/shard_map/ppermute | solution.py:264
  56.6 4.7 %shard_map.93 = bf16[256,3072]{1,0:T(8,128)(2,1)} custom-call(s32[4]{0:T(128)S(1)} %pad_add_fusion.place, f32[32,4096]{1,0:T(8,128)S(1)} %slice.9.g0, bf16[32,4096]{1,0:T(8,128)(2,1)S(1)} %collective-permute-done.11.g1, bf16[256,1024]{1,0:T(8,128)(2,1)S(1)} %bitcast.7, f32[1,1024]{1,0:T(1,128)S(1)} %bitcast.8, bf16[128,1024]{1,0:T(8,128)(2,1)S(1)} %copy-done.3, ...), custom_call_target="tpu_custom_call" | custom-call | flops 1879048192 | bytes 7864320 | tf_op jit(solution)/shard_map/pallas_call | solution.py:248
  (34 shorter events, 0.5 us)
Async XLA Ops:
  0.0 2.6 %copy-start.6 = (bf16[128,512]{1,0:T(8,128)(2,1)S(1)}, bf16[128,512]{1,0:T(8,128)(2,1)}, u32[]{:S(2)}) copy-start(bf16[128,512]{1,0:T(8,128)(2,1)} %k.1) | copy-start | bytes 393220
  0.0 3.2 %copy-start.3 = (bf16[128,1024]{1,0:T(8,128)(2,1)S(1)}, bf16[128,1024]{1,0:T(8,128)(2,1)}, u32[]{:S(2)}) copy-start(bf16[128,1024]{1,0:T(8,128)(2,1)} %refs_0_.1) | copy-start | bytes 786436
  0.0 3.6 %copy-start.7 = (bf16[128,512]{1,0:T(8,128)(2,1)S(1)}, bf16[128,512]{1,0:T(8,128)(2,1)}, u32[]{:S(2)}) copy-start(bf16[128,512]{1,0:T(8,128)(2,1)} %v.1) | copy-start | bytes 393220
  0.0 4.2 %copy-start.5 = (bf16[128,512]{1,0:T(8,128)(2,1)S(1)}, bf16[128,512]{1,0:T(8,128)(2,1)}, u32[]{:S(2)}) copy-start(bf16[128,512]{1,0:T(8,128)(2,1)} %q.1) | copy-start | bytes 393220
  0.0 30.6 %copy-start.4 = (bf16[128,1024]{1,0:T(8,128)(2,1)S(1)}, bf16[128,1024]{1,0:T(8,128)(2,1)}, u32[]{:S(2)}) copy-start(bf16[128,1024]{1,0:T(8,128)(2,1)} %x.1) | copy-start | bytes 786436
  1.3 15.7 %collective-permute-start.4 = (bf16[256,768]{1,0:T(8,128)(2,1)S(1)}, bf16[256,768]{1,0:T(8,128)(2,1)S(1)}, u32[]{:S(2)}, u32[]{:S(2)}) collective-permute-start(bf16[256,768]{1,0:T(8,128)(2,1)S(1)} %get-tuple-element.40), channel_id=1, source_target_pairs={{0,2},{2,0},{1,3},{3,1},{4,6},{6,4},{5,7},{7,5},{8,10},{10,8},{9,1... | collective-permute-start | bytes 1179656 | tf_op jit(solution)/shard_map/ppermute | solution.py:264
  2.6 3.8 %collective-permute-start = (bf16[128,512]{1,0:T(8,128)(2,1)S(1)}, bf16[128,512]{1,0:T(8,128)(2,1)S(1)}, u32[]{:S(2)}, u32[]{:S(2)}) collective-permute-start(bf16[128,512]{1,0:T(8,128)(2,1)S(1)} %copy-done.6), channel_id=1, source_target_pairs={{0,4},{1,5},{2,6},{3,7},{16,20},{17,21},{18,22},{19,23}} | collective-permute-start | bytes 393224 | tf_op jit(solution)/shard_map/ppermute | solution.py:283
  3.2 13.7 %collective-permute-start.5 = (bf16[128,1024]{1,0:T(8,128)(2,1)S(1)}, bf16[128,1024]{1,0:T(8,128)(2,1)S(1)}, u32[]{:S(2)}, u32[]{:S(2)}) collective-permute-start(bf16[128,1024]{1,0:T(8,128)(2,1)S(1)} %copy-done.3), channel_id=1, source_target_pairs={{0,2},{2,0},{1,3},{3,1},{4,6},{6,4},{5,7},{7,5},{8,10},{10,8},{9,1... | collective-permute-start | bytes 786440 | tf_op jit(solution)/shard_map/ppermute | solution.py:264
  3.6 7.0 %collective-permute-start.1 = (bf16[128,512]{1,0:T(8,128)(2,1)S(1)}, bf16[128,512]{1,0:T(8,128)(2,1)S(1)}, u32[]{:S(2)}, u32[]{:S(2)}) collective-permute-start(bf16[128,512]{1,0:T(8,128)(2,1)S(1)} %copy-done.7), channel_id=1, source_target_pairs={{0,4},{1,5},{2,6},{3,7},{16,20},{17,21},{18,22},{19,23}} | collective-permute-start | bytes 393224 | tf_op jit(solution)/shard_map/ppermute | solution.py:284
  4.2 6.3 %collective-permute-start.2 = (bf16[128,512]{1,0:T(8,128)(2,1)S(1)}, bf16[128,512]{1,0:T(8,128)(2,1)S(1)}, u32[]{:S(2)}, u32[]{:S(2)}) collective-permute-start(bf16[128,512]{1,0:T(8,128)(2,1)S(1)} %copy-done.5), channel_id=1, source_target_pairs={{8,4},{12,8},{9,5},{13,9},{10,6},{14,10},{11,7},{15,11},{24,20},{2... | collective-permute-start | bytes 393224 | tf_op jit(solution)/shard_map/ppermute | solution.py:285
  6.3 6.1 %collective-permute-start.3 = (bf16[128,512]{1,0:T(8,128)(2,1)S(1)}, bf16[128,512]{1,0:T(8,128)(2,1)S(1)}, u32[]{:S(2)}, u32[]{:S(2)}) collective-permute-start(bf16[128,512]{1,0:T(8,128)(2,1)S(1)} %copy-done.5), channel_id=1, source_target_pairs={{12,4},{13,5},{14,6},{15,7},{28,20},{29,21},{30,22},{31,23}} | collective-permute-start | bytes 393224 | tf_op jit(solution)/shard_map/ppermute | solution.py:286
  17.0 13.7 %collective-permute-start.8 = (bf16[256,768]{1,0:T(8,128)(2,1)S(1)}, bf16[256,768]{1,0:T(8,128)(2,1)S(1)}, u32[]{:S(2)}, u32[]{:S(2)}) collective-permute-start(bf16[256,768]{1,0:T(8,128)(2,1)S(1)} %get-tuple-element.30), channel_id=1, source_target_pairs={{0,2},{2,0},{1,3},{3,1},{4,6},{6,4},{5,7},{7,5},{8,10},{10,8},{9,1... | collective-permute-start | bytes 1179656 | tf_op jit(solution)/shard_map/ppermute | solution.py:264
  18.2 12.5 %collective-permute-start.9 = (bf16[256,768]{1,0:T(8,128)(2,1)S(1)}, bf16[256,768]{1,0:T(8,128)(2,1)S(1)}, u32[]{:S(2)}, u32[]{:S(2)}) collective-permute-start(bf16[256,768]{1,0:T(8,128)(2,1)S(1)} %collective-permute-done.4.refs_6_), channel_id=1, source_target_pairs={{0,16},{16,0},{1,17},{17,1},{2,18},{18,2},{3,19},{19,3},{4,20},{20... | collective-permute-start | bytes 1179656 | tf_op jit(solution)/shard_map/ppermute | solution.py:264
  21.3 6.2 %collective-permute-start.6 = (bf16[144,512]{1,0:T(8,128)(2,1)S(1)}, bf16[144,512]{1,0:T(8,128)(2,1)S(1)}, u32[]{:S(2)}, u32[]{:S(2)}) collective-permute-start(bf16[144,512]{1,0:T(8,128)(2,1)S(1)} %get-tuple-element.28), channel_id=1, source_target_pairs={{4,8},{8,12},{5,9},{9,13},{6,10},{10,14},{7,11},{11,15},{20,24},{2... | collective-permute-start | bytes 442376 | tf_op jit(solution)/shard_map/ppermute | solution.py:296
  22.6 8.1 %collective-permute-start.7 = (bf16[144,512]{1,0:T(8,128)(2,1)S(1)}, bf16[144,512]{1,0:T(8,128)(2,1)S(1)}, u32[]{:S(2)}, u32[]{:S(2)}) collective-permute-start(bf16[144,512]{1,0:T(8,128)(2,1)S(1)} %get-tuple-element.29), channel_id=1, source_target_pairs={{4,12},{5,13},{6,14},{7,15},{20,28},{21,29},{22,30},{23,31}} | collective-permute-start | bytes 442376 | tf_op jit(solution)/shard_map/ppermute | solution.py:297
  30.7 2.2 %copy-start = (bf16[512,4096]{1,0:T(8,128)(2,1)S(1)}, bf16[512,4096]{1,0:T(8,128)(2,1)}, u32[]{:S(2)}) copy-start(bf16[512,4096]{1,0:T(8,128)(2,1)} %w.1) | copy-start | bytes 12582916
  32.9 4.7 %copy-start.1 = (bf16[1024,768]{1,0:T(8,128)(2,1)S(1)}, bf16[1024,768]{1,0:T(8,128)(2,1)}, u32[]{:S(2)}) copy-start(bf16[1024,768]{1,0:T(8,128)(2,1)} %refs_4_.1) | copy-start | bytes 4718596
  34.7 14.2 %collective-permute-start.10 = (bf16[64,4096]{1,0:T(8,128)(2,1)S(1)}, bf16[64,4096]{1,0:T(8,128)(2,1)S(1)}, u32[]{:S(2)}, u32[]{:S(2)}) collective-permute-start(bf16[64,4096]{1,0:T(8,128)(2,1)S(1)} %get-tuple-element.35), channel_id=1, source_target_pairs={{0,1},{1,0},{2,3},{3,2},{4,5},{5,4},{6,7},{7,6},{8,9},{9,8},{10,11... | collective-permute-start | bytes 1572872 | tf_op jit(solution)/shard_map/ppermute | solution.py:264
  37.4 10.7 %collective-permute-start.15 = (bf16[256,768]{1,0:T(8,128)(2,1)S(1)}, bf16[256,768]{1,0:T(8,128)(2,1)S(1)}, u32[]{:S(2)}, u32[]{:S(2)}) collective-permute-start(bf16[256,768]{1,0:T(8,128)(2,1)S(1)} %collective-permute-done.8.refs_7_), channel_id=1, source_target_pairs={{0,16},{16,0},{1,17},{17,1},{2,18},{18,2},{3,19},{19,3},{4,20},{20... | collective-permute-start | bytes 1179656 | tf_op jit(solution)/shard_map/ppermute | solution.py:264
  37.6 18.9 %collective-permute-start.14 = (bf16[1024,768]{1,0:T(8,128)(2,1)S(1)}, bf16[1024,768]{1,0:T(8,128)(2,1)S(1)}, u32[]{:S(2)}, u32[]{:S(2)}) collective-permute-start(bf16[1024,768]{1,0:T(8,128)(2,1)S(1)} %copy-done.1), channel_id=1, source_target_pairs={{0,1},{1,0},{2,3},{3,2},{4,5},{5,4},{6,7},{7,6},{8,9},{9,8},{10,11... | collective-permute-start | bytes 4718600 | tf_op jit(solution)/shard_map/ppermute | solution.py:264
  38.0 3.6 %collective-permute-start.12 = (bf16[128,1024]{1,0:T(8,128)(2,1)S(1)}, bf16[128,1024]{1,0:T(8,128)(2,1)S(1)}, u32[]{:S(2)}, u32[]{:S(2)}) collective-permute-start(bf16[128,1024]{1,0:T(8,128)(2,1)S(1)} %copy-done.3), channel_id=1, source_target_pairs={{0,1},{1,0},{2,3},{3,2},{4,5},{5,4},{6,7},{7,6},{8,9},{9,8},{10,11... | collective-permute-start | bytes 786440 | tf_op jit(solution)/shard_map/ppermute | solution.py:264
  38.1 3.8 %collective-permute-start.13 = (bf16[128,1024]{1,0:T(8,128)(2,1)S(1)}, bf16[128,1024]{1,0:T(8,128)(2,1)S(1)}, u32[]{:S(2)}, u32[]{:S(2)}) collective-permute-start(bf16[128,1024]{1,0:T(8,128)(2,1)S(1)} %collective-permute-done.5.refs_2_), channel_id=1, source_target_pairs={{0,1},{1,0},{2,3},{3,2},{4,5},{5,4},{6,7},{7,6},{8,9},{9,8},{10,11... | collective-permute-start | bytes 786440 | tf_op jit(solution)/shard_map/ppermute | solution.py:264
  41.5 7.6 %collective-permute-start.16 = (bf16[256,768]{1,0:T(8,128)(2,1)S(1)}, bf16[256,768]{1,0:T(8,128)(2,1)S(1)}, u32[]{:S(2)}, u32[]{:S(2)}) collective-permute-start(bf16[256,768]{1,0:T(8,128)(2,1)S(1)} %collective-permute-done.4.refs_6_), channel_id=1, source_target_pairs={{0,1},{1,0},{2,3},{3,2},{4,5},{5,4},{6,7},{7,6},{8,9},{9,8},{10,11... | collective-permute-start | bytes 1179656 | tf_op jit(solution)/shard_map/ppermute | solution.py:264
  41.9 8.4 %collective-permute-start.17 = (bf16[256,768]{1,0:T(8,128)(2,1)S(1)}, bf16[256,768]{1,0:T(8,128)(2,1)S(1)}, u32[]{:S(2)}, u32[]{:S(2)}) collective-permute-start(bf16[256,768]{1,0:T(8,128)(2,1)S(1)} %collective-permute-done.8.refs_7_), channel_id=1, source_target_pairs={{0,1},{1,0},{2,3},{3,2},{4,5},{5,4},{6,7},{7,6},{8,9},{9,8},{10,11... | collective-permute-start | bytes 1179656 | tf_op jit(solution)/shard_map/ppermute | solution.py:264
  48.1 2.2 %collective-permute-start.18 = (bf16[256,768]{1,0:T(8,128)(2,1)S(1)}, bf16[256,768]{1,0:T(8,128)(2,1)S(1)}, u32[]{:S(2)}, u32[]{:S(2)}) collective-permute-start(bf16[256,768]{1,0:T(8,128)(2,1)S(1)} %collective-permute-done.9.refs_8_), channel_id=1, source_target_pairs={{0,1},{1,0},{2,3},{3,2},{4,5},{5,4},{6,7},{7,6},{8,9},{9,8},{10,11... | collective-permute-start | bytes 1179656 | tf_op jit(solution)/shard_map/ppermute | solution.py:264
  48.9 1.9 %collective-permute-start.19 = (bf16[256,768]{1,0:T(8,128)(2,1)S(1)}, bf16[256,768]{1,0:T(8,128)(2,1)S(1)}, u32[]{:S(2)}, u32[]{:S(2)}) collective-permute-start(bf16[256,768]{1,0:T(8,128)(2,1)S(1)} %collective-permute-done.15.refs_9_), channel_id=1, source_target_pairs={{0,1},{1,0},{2,3},{3,2},{4,5},{5,4},{6,7},{7,6},{8,9},{9,8},{10,11... | collective-permute-start | bytes 1179656 | tf_op jit(solution)/shard_map/ppermute | solution.py:264
  48.9 7.6 %copy-start.2 = (bf16[32,8,1024]{2,1,0:T(8,128)(2,1)S(1)}, bf16[32,8,1024]{2,1,0:T(8,128)(2,1)}, u32[]{:S(2)}) copy-start(bf16[32,8,1024]{2,1,0:T(8,128)(2,1)} %param.15) | copy-start | bytes 1572868
  48.9 7.6 %copy-start.8 = (f32[1024]{0:T(1024)S(1)}, f32[1024]{0:T(1024)}, u32[]{:S(2)}) copy-start(f32[1024]{0:T(1024)} %param.16) | copy-start | bytes 12292
  49.1 7.4 %collective-permute-start.11 = (bf16[32,4096]{1,0:T(8,128)(2,1)S(1)}, bf16[32,4096]{1,0:T(8,128)(2,1)S(1)}, u32[]{:S(2)}, u32[]{:S(2)}) collective-permute-start(bf16[32,4096]{1,0:T(8,128)(2,1)S(1)} %slice.12), channel_id=1, source_target_pairs={{0,2},{2,0},{1,3},{3,1},{4,6},{6,4},{5,7},{7,5},{8,10},{10,8},{9,1... | collective-permute-start | bytes 786440 | tf_op jit(solution)/shard_map/ppermute | solution.py:264

commit v3 on v2

v3 whole, which is shorter than its diff:
```python
import functools
import math

import jax
import jax.numpy as jnp
from jax import lax
from jax.experimental import pallas as pl
from jax.experimental.pallas import tpu as pltpu
from jax.sharding import PartitionSpec as P

HD = 128
DL = 1024
P_SIZE = 8
DSLICE = 512
GROUP = ("dp", "sub")
SCALE = 1.0 / math.sqrt(HD)
VMEM = pl.BlockSpec(memory_space=pltpu.VMEM)
SMEM = pl.BlockSpec(memory_space=pltpu.SMEM)
HBM = pl.BlockSpec(memory_space=pltpu.HBM)
F32 = jnp.float32
BF16 = jnp.bfloat16


def dot(a, b):
    return jnp.dot(a, b, preferred_element_type=F32)


def any_mesh(
    q_glob, k_glob, v_glob, x_glob, out_weight, bridge_weight, byte_embed, norm_gain, qkv_weight
):
    query_rows, query_width = q_glob.shape
    head_count = query_width // HD
    first_row = lax.axis_index("ctx") * query_rows
    queries = q_glob.reshape(query_rows, head_count, HD)
    query_pos = first_row + lax.iota(jnp.int32, query_rows)
    keys = lax.all_gather(k_glob, "ctx", axis=0, tiled=True)
    values = lax.all_gather(v_glob, "ctx", axis=0, tiled=True)
    count = keys.shape[0]
    keys = keys.reshape(count, head_count, HD)
    values = values.reshape(count, head_count, HD)
    scores = jnp.einsum("qhd,khd->hqk", queries, keys, preferred_element_type=F32) * SCALE
    allowed = query_pos[:, None] >= lax.iota(jnp.int32, count)[None, :]
    scores = jnp.where(allowed[None], scores, -jnp.inf)
    weights = jnp.exp(scores - jnp.max(scores, axis=2)[:, :, None])
    row_sum = jnp.sum(weights, axis=2)
    weighted = jnp.einsum("hqk,khd->hqd", weights.astype(BF16), values, preferred_element_type=F32)
    attn = (weighted / row_sum[:, :, None]).astype(BF16)
    attn = attn.transpose(1, 0, 2).reshape(query_rows, query_width)
    head_terms = dot(attn, out_weight)
    own_bytes = P_SIZE // lax.axis_size(GROUP)
    feature_sum = lax.psum_scatter(
        head_terms.astype(BF16), GROUP, scatter_dimension=1, tiled=True
    ).astype(F32)
    patch_out = (feature_sum + x_glob.astype(F32)).astype(BF16)
    patch_out = patch_out.reshape(query_rows, own_bytes, DSLICE)
    patch_out = lax.all_to_all(patch_out, GROUP, split_axis=0, concat_axis=1, tiled=True)
    glob_bytes = patch_out.reshape(-1, DSLICE)
    byte_rows = glob_bytes.shape[0]
    bridged = dot(glob_bytes, lax.all_gather(bridge_weight, GROUP, axis=0, tiled=True))
    byte_in = byte_embed.reshape(byte_rows, DL).astype(F32) + bridged
    mean_square = jnp.mean(byte_in * byte_in, axis=1, keepdims=True)
    normalized = (byte_in * lax.rsqrt(mean_square + 1e-05) * norm_gain).astype(BF16)
    result = dot(normalized, lax.all_gather(qkv_weight, GROUP, axis=1, tiled=True)).astype(BF16)
    return result.reshape(byte_embed.shape[0], P_SIZE, 3 * DL)


def attend_kernel(place, held, q_up, k_low, v_low, own, own_log, up):
    rows, width = q_up.shape
    heads = width // HD
    has_low = place[0] >= 1
    row = lax.broadcasted_iota(jnp.int32, (rows, 2 * rows), 0)
    col = lax.broadcasted_iota(jnp.int32, (rows, 2 * rows), 1)
    low = jnp.logical_and(col >= rows, has_low)
    full = jnp.logical_or(col < rows, low)
    causal = jnp.logical_or(row >= col, low)
    logs = [[], []]
    for h in range(heads):
        cols = pl.ds(h * HD, HD)
        qh, k, v = (held[:, pl.ds(i * width + h * HD, HD)] for i in range(3))
        kh = jnp.concatenate([k, k_low[:, cols]], axis=0)
        vh = jnp.concatenate([v, v_low[:, cols]], axis=0)
        for i, (queries, mask, target) in enumerate(((qh, causal, own), (q_up[:, cols], full, up))):
            scores = lax.dot_general(
                queries, kh, (((1,), (1,)), ((), ())), preferred_element_type=F32
            ) * SCALE
            scores = jnp.where(mask, scores, -jnp.inf)
            top = jnp.max(scores, axis=1, keepdims=True)
            probs = jnp.exp(scores - top)
            total = jnp.sum(probs, axis=1, keepdims=True)
            mixed = dot(probs.astype(BF16), vh) / total
            target[pl.ds(0, rows), cols] = mixed.astype(target.dtype)
            logs[i].append(top + jnp.log(total))
    lane = lax.broadcasted_iota(jnp.int32, (rows, HD), 1)

    def by_lane(columns):
        table = jnp.zeros((rows, HD), F32)
        for i, column in enumerate(columns):
            table = jnp.where(lane == i, column, table)
        return table

    own_log[...] = by_lane(logs[0])
    terms = []
    rest = logs[1]
    for _ in range(3):
        high = [r.astype(BF16).astype(F32) for r in rest]
        rest = [r - t for r, t in zip(rest, high)]
        terms += high
    up[pl.ds(rows, 16), :] = jnp.zeros((16, width), BF16)
    up[pl.ds(rows, 16), pl.ds(0, HD)] = by_lane(terms).T[:16, :rows].astype(BF16)


def attend(place, held, q_up, k_low, v_low):
    rows, width = q_up.shape
    return pl.pallas_call(
        attend_kernel,
        out_shape=(
            jax.ShapeDtypeStruct((rows, width), F32),
            jax.ShapeDtypeStruct((rows, HD), F32),
            jax.ShapeDtypeStruct((rows + 16, width), BF16),
        ),
        in_specs=[SMEM] + [VMEM] * 4,
        out_specs=(VMEM,) * 3,
        compiler_params=pltpu.CompilerParams(vmem_limit_bytes=6 * 2**20),
        cost_estimate=pl.CostEstimate(
            flops=16 * rows * rows * width,
            bytes_accessed=24 * rows * width,
            transcendentals=4 * rows * rows * width // HD,
        ),
    )(place, held, q_up, k_low, v_low)


def copy_all(pairs, sems):
    copies = [pltpu.make_async_copy(a, b, sems.at[i]) for i, (a, b) in enumerate(pairs)]
    for copy in copies:
        copy.start()
    for copy in copies:
        copy.wait()


def hold_kernel(q, k, v, held):
    width = q.shape[1]
    for i, source in enumerate((q, k, v)):
        held[:, pl.ds(i * width, width)] = source[...]


def hold(q, k, v):
    return pl.pallas_call(
        hold_kernel,
        out_shape=jax.ShapeDtypeStruct((q.shape[0], 3 * q.shape[1]), q.dtype),
        in_specs=[VMEM] * 3,
        out_specs=VMEM,
        compiler_params=pltpu.CompilerParams(vmem_limit_bytes=2 * 2**20),
    )(q, k, v)


def bring_kernel(source, target, sems):
    rows = source.shape[0] // sems.shape[0]
    cuts = [pl.ds(i * rows, rows) for i in range(sems.shape[0])]
    copy_all([(source.at[c, :], target.at[c, :]) for c in cuts], sems)


def bring(x, parts):
    return pl.pallas_call(
        bring_kernel,
        out_shape=jax.ShapeDtypeStruct(x.shape, x.dtype),
        in_specs=[HBM],
        out_specs=VMEM,
        scratch_shapes=[pltpu.SemaphoreType.DMA((parts,))],
        compiler_params=pltpu.CompilerParams(vmem_limit_bytes=2 * 2**20),
    )(x)


def project_kernel(place, own, own_log, low, x, w, away, kept, attn, xs):
    ctx, dp, sub = place[0], place[1], place[2]
    rows, width = own.shape
    heads = width // HD
    quarter = rows // 4
    table = low[pl.ds(rows, 16), pl.ds(0, HD)].astype(F32)
    table = jnp.concatenate([table, jnp.zeros((HD - 16, HD), F32)], axis=0).T
    for h in range(heads):
        cols = pl.ds(h * HD, HD)
        log = own_log[:, h : h + 1]
        log_low = (
            table[:, h : h + 1]
            + table[:, heads + h : heads + h + 1]
            + table[:, 2 * heads + h : 2 * heads + h + 1]
        )
        log_low = jnp.where(ctx >= 2, log_low, -jnp.inf)
        top = jnp.maximum(log, log_low)
        share, share_low = jnp.exp(log - top), jnp.exp(log_low - top)
        mixed = share * own[:, cols] + share_low * low[pl.ds(0, rows), cols].astype(F32)
        attn[:, cols] = (mixed / (share + share_low)).astype(BF16)
    order = []
    for core in (1 - sub, sub):
        for chip in (1 - dp, dp):
            order.append(pl.ds(pl.multiple_of((chip * 2 + core) * quarter, quarter), quarter))
    a = jnp.concatenate([attn[o, :] for o in order], axis=0)
    for i, o in enumerate(order):
        xs[pl.ds(i * quarter, quarter), :] = x[o, :]
    block = x.shape[1]
    mine = dp * 2 + sub
    for b in range(w.shape[1] // block):
        cols = pl.ds(b * block, block)
        terms = dot(a, w[:, cols])
        terms += jnp.where(mine == b, xs[...].astype(F32), 0.0)
        away[:, cols] = terms[: 2 * quarter].astype(BF16)
        kept[:, cols] = terms[2 * quarter :]


def project(place, own, own_log, low, x, w):
    rows, width = own.shape
    half = rows // 2
    return pl.pallas_call(
        project_kernel,
        out_shape=(
            jax.ShapeDtypeStruct((half, w.shape[1]), BF16),
            jax.ShapeDtypeStruct((half, w.shape[1]), F32),
        ),
        in_specs=[SMEM] + [VMEM] * 5,
        out_specs=(VMEM, VMEM),
        scratch_shapes=[pltpu.VMEM((rows, width), BF16), pltpu.VMEM(x.shape, BF16)],
        compiler_params=pltpu.CompilerParams(vmem_limit_bytes=12 * 2**20),
        cost_estimate=pl.CostEstimate(
            flops=2 * rows * width * w.shape[1],
            bytes_accessed=2 * w.size + 6 * half * w.shape[1],
            transcendentals=3 * rows * width // HD,
        ),
    )(place, own, own_log, low, x, w)


def bytes_kernel(place, g0, g1, embed, gain, *refs):
    bridge = refs[:4]
    hid, bw = refs[4:]
    dp, sub = place[1], place[2]
    patches = g0.shape[0]
    bytes_ = g0.shape[1] // DSLICE
    rows = patches * bytes_
    depth = bridge[0].shape[0]
    for b, ref in zip(block_order(dp, sub), bridge):
        bw[pl.ds(pl.multiple_of(b * depth, depth), depth), :] = ref[...]
    glob = (g0[...] + g1[...].astype(F32)).astype(BF16)
    stacked = jnp.concatenate(
        [glob[:, p * DSLICE : (p + 1) * DSLICE] for p in range(bytes_)], axis=0
    )
    to = lax.broadcasted_iota(jnp.int32, (rows, rows), 0)
    source = lax.broadcasted_iota(jnp.int32, (rows, rows), 1)
    pick = ((to % bytes_) * patches + to // bytes_ == source).astype(BF16)
    by_patch = dot(pick, stacked).astype(BF16)
    byte_in = embed[...].astype(F32) + dot(by_patch, bw[...])
    mean_square = jnp.mean(byte_in * byte_in, axis=1, keepdims=True)
    hid[...] = (byte_in * lax.rsqrt(mean_square + 1e-05) * gain[...]).astype(BF16)


def block_order(dp, sub):
    return [dp * 2 + sub, dp * 2 + 1 - sub, (1 - dp) * 2 + sub, (1 - dp) * 2 + 1 - sub]


def bytes_in(place, g0, g1, embed, gain, bridge):
    rows = embed.shape[0]
    return pl.pallas_call(
        bytes_kernel,
        out_shape=jax.ShapeDtypeStruct((rows, DL), BF16),
        in_specs=[SMEM] + [VMEM] * 8,
        out_specs=VMEM,
        scratch_shapes=[pltpu.VMEM((DSLICE, DL), BF16)],
        compiler_params=pltpu.CompilerParams(vmem_limit_bytes=10 * 2**20),
        cost_estimate=pl.CostEstimate(
            flops=2 * rows * DL * DSLICE, bytes_accessed=6 * rows * DL, transcendentals=rows
        ),
    )(place, g0, g1, embed, gain, *bridge)


def local_kernel(place, hid, *refs):
    whole, chips = refs[:2], (refs[2:7], refs[7:12])
    out, held, sems = refs[12:]
    ctx, dp, sub, grp = (place[i] for i in range(4))
    odd = ctx % 2
    depth, width = whole[0].shape
    quarter, eighth = depth // 4, depth // 8

    def columns(first, count):
        return hid[:, pl.ds(pl.multiple_of(first, 128), count)]

    copies = []
    for i, b in enumerate(block_order(dp, sub)):
        if i < 2:
            total = dot(hid[...], whole[i][...])
        else:
            x0, y0, x1, y1, z1 = chips[i - 2]
            total = dot(columns(grp * quarter, quarter), x0[...])
            total += dot(columns((1 - grp) * quarter, quarter), y0[...])
            mixed = [columns(4 * eighth + grp * eighth, eighth), columns(6 * eighth + odd * eighth, eighth)]
            total += dot(jnp.concatenate(mixed, axis=1), x1[...])
            total += dot(columns(4 * eighth + (1 - grp) * eighth, eighth), y1[...])
            total += dot(columns(6 * eighth + (1 - odd) * eighth, eighth), z1[...])
        held[i, :, :] = total.astype(BF16)
        copy = pltpu.make_async_copy(
            held.at[i], out.at[:, pl.ds(pl.multiple_of(b * width, 128), width)], sems.at[i]
        )
        copy.start()
        copies.append(copy)
    for copy in copies:
        copy.wait()


def local(place, hid, *weights):
    rows = hid.shape[0]
    block = weights[0].shape[1]
    return pl.pallas_call(
        local_kernel,
        out_shape=jax.ShapeDtypeStruct((rows, 4 * block), BF16),
        in_specs=[SMEM] + [VMEM] * (1 + len(weights)),
        out_specs=pl.BlockSpec(memory_space=pl.ANY),
        scratch_shapes=[pltpu.VMEM((4, rows, block), BF16), pltpu.SemaphoreType.DMA((4,))],
        compiler_params=pltpu.CompilerParams(vmem_limit_bytes=12 * 2**20),
        cost_estimate=pl.CostEstimate(
            flops=8 * rows * DL * block,
            bytes_accessed=8 * DL * block + 8 * rows * block,
            transcendentals=0,
        ),
    )(place, hid, *weights)


def swap(x, axis):
    return lax.ppermute(x, axis, [(0, 1), (1, 0)])


def after(x, *events):
    return lax.optimization_barrier((x, *events))[0]


def small_mesh(
    q_glob, k_glob, v_glob, x_glob, out_weight, bridge_weight, byte_embed, norm_gain, qkv_weight
):
    ctx, dp, sub, grp = (lax.axis_index(a) for a in ("ctx", "dp", "sub", "groups"))
    place = jnp.stack([ctx, dp, sub, grp]).astype(jnp.int32)

    quarter, eighth = qkv_weight.shape[0] // 4, qkv_weight.shape[0] // 8
    held = hold(q_glob, k_glob, v_glob)
    later = after(qkv_weight, held)
    w0 = lax.dynamic_slice_in_dim(qkv_weight, grp * quarter, quarter, 0)
    w1 = jnp.concatenate(
        [
            lax.dynamic_slice_in_dim(later, (4 + grp) * eighth, eighth, 0),
            lax.dynamic_slice_in_dim(later, (6 + ctx % 2) * eighth, eighth, 0),
        ],
        axis=0,
    )

    x0 = swap(w0, "dp")
    bridge_x = swap(bridge_weight, "dp")
    q_up = lax.ppermute(q_glob, "ctx", [(2, 0), (3, 1)])
    k_low = lax.ppermute(k_glob, "ctx", [(0, 1), (1, 2), (2, 3)])
    v_low = lax.ppermute(v_glob, "ctx", [(0, 1), (1, 2), (2, 3)])
    q_up, k_low, v_low, x0, bridge_x, w1, held, bridge_weight, place = lax.optimization_barrier(
        (q_up, k_low, v_low, x0, bridge_x, w1, held, bridge_weight, place)
    )

    own, own_log, up = attend(place, held, q_up, k_low, v_low)
    low = lax.ppermute(up, "ctx", [(0, 2), (1, 3)])
    x1 = swap(w1, "dp")
    y0 = swap(x0, "groups")
    core_x0 = swap(x0, "sub")
    bridge_core = swap(bridge_weight, "sub")
    out_weight = bring(after(out_weight, up), 4)
    low, core_x0, x1, y0, out_weight, bridge_x, bridge_core, qkv_weight = lax.optimization_barrier(
        (low, core_x0, x1, y0, out_weight, bridge_x, bridge_core, qkv_weight)
    )

    away, kept = project(place, own, own_log, low, x_glob, out_weight)
    away = swap(away, "sub")
    core_y0 = swap(y0, "sub")
    bridge_both = swap(bridge_x, "sub")
    away, bridge_both, core_y0, x1, qkv_weight = lax.optimization_barrier(
        (away, bridge_both, core_y0, x1, qkv_weight)
    )

    summed = kept + away.astype(F32)
    mid = summed.shape[0] // 2
    across = swap(summed[:mid].astype(BF16), "dp")
    y1 = swap(x1[:eighth], "groups")
    z1 = lax.ppermute(x1[eighth:], "ctx", [(0, 1), (1, 0), (2, 3), (3, 2)])
    core_x1 = swap(x1, "sub")
    other_core = swap(qkv_weight, "sub")
    across, y1, z1, core_x1, other_core = lax.optimization_barrier(
        (across, y1, z1, core_x1, other_core)
    )

    core_y1 = swap(y1, "sub")
    core_z1 = swap(z1, "sub")
    rows = byte_embed.shape[0] * byte_embed.shape[1]
    hidden = bytes_in(
        place,
        summed[mid:],
        across,
        byte_embed.reshape(rows, DL),
        norm_gain.reshape(1, DL),
        [bridge_weight, bridge_core, bridge_x, bridge_both],
    )
    result = local(
        place,
        hidden,
        *(qkv_weight, other_core),
        *(x0, y0, x1, y1, z1),
        *(core_x0, core_y0, core_x1, core_y1, core_z1),
    )
    return result.reshape(byte_embed.shape[0], P_SIZE, result.shape[1])


def solution(mesh):
    rows = P(("groups", "ctx"), GROUP)
    in_specs = (
        rows,
        rows,
        rows,
        rows,
        P(GROUP, None),
        P(GROUP, None),
        P(("groups", "ctx", "dp", "sub"), None, None),
        P(),
        P(None, GROUP),
    )
    out_specs = P(("groups", "ctx", "dp", "sub"), None, None)
    pairs = all(mesh.shape[a] == 2 for a in ("groups", "dp", "sub"))
    per_device = small_mesh if pairs and mesh.shape["ctx"] == 4 else any_mesh
    return jax.shard_map(
        per_device, mesh=mesh, in_specs=in_specs, out_specs=out_specs, check_vma=False
    )
```

time: 62.2 us -> 56 us (0.900)
  the two profiles are of different devices: /device:TPU:25 before, /device:TPU:0 now
where the time goes in v3:
time: 56 us; the launch traced here: 55.7 us
  starting transfers between devices  26.2 us (47%)
  waiting for transfers between devices  12.1 us (22%)
  Pallas kernels  8.38 us (15%)
  local copies, waits for them, and re-layouts  7.62 us (14%)
  other arithmetic  1.12 us (2%)
    ppermute x15, starting transfers between devices, swap(): return lax.ppermute(x, axis, [(0, 1), (1, 0)])  8.13 us
    ppermute x15, waiting for transfers between devices, swap(): return lax.ppermute(x, axis, [(0, 1), (1, 0)])  6.33 us
    ppermute x1, waiting for transfers between devices, small_mesh(): z1 = lax.ppermute(x1[eighth:], 'ctx', [(0, 1), (1, 0), (2, 3), (3, 2)])  4.99 us
    unnamed x18, local copies, waits for them, and re-layouts  4.91 us
    ppermute x1, starting transfers between devices, small_mesh(): z1 = lax.ppermute(x1[eighth:], 'ctx', [(0, 1), (1, 0), (2, 3), (3, 2)])  4.64 us
    ppermute x1, starting transfers between devices, small_mesh(): v_low = lax.ppermute(v_glob, 'ctx', [(0, 1), (1, 2), (2, 3)])  4.44 us
    ppermute x1, starting transfers between devices, small_mesh(): low = lax.ppermute(up, 'ctx', [(0, 2), (1, 3)])  4.2 us
    pallas_call x1, Pallas kernels, local(): pl.pallas_call(local_kernel, out_shape=jax.ShapeDtypeStruct((rows, 4 * bl...  3.51 us
  transfers between devices with their start and end apart: 20, of which 5 were waited for; matrix products, arithmetic and copies ran while one was open for 3% of the time, Pallas kernels for 6%

profile of v3, /device:TPU:0, one launch (start us, length us, event | category | flops | bytes accessed | tf_op | source)
XLA Modules:
  0.0 55.7 jit_solution(645457498276614264)
XLA Ops:
  0.0 1.9 %constant_dynamic-slice_fusion.2 = bf16[256,768]{1,0:T(8,128)(2,1)} fusion(bf16[1024,768]{1,0:T(8,128)(2,1)} %refs_0_.1, s32[]{:T(128)S(6)} %select_n.16), kind=kLoop, calls=%fused_computation.5 | loop fusion | bytes 786436 | tf_op jit(solution)/shard_map/dynamic_slice | solution.py:341
  1.9 2.9 %collective-permute-start.3 = (bf16[256,768]{1,0:T(8,128)(2,1)}, bf16[256,768]{1,0:T(8,128)(2,1)S(1)}, u32[]{:S(2)}, u32[]{:S(2)}) collective-permute-start(bf16[256,768]{1,0:T(8,128)(2,1)} %constant_dynamic-slice_fusion.2), channel_id=1, source_target_pairs={{0,2},{2,0},{1,3},{3,1},{4,6},{6,4},{5,7},{7,5},{8,10},{10,8},{9,1... | collective-permute-start | bytes 1179656 | tf_op jit(solution)/shard_map/ppermute | solution.py:325
  4.8 1.3 %collective-permute-start = (bf16[128,512]{1,0:T(8,128)(2,1)}, bf16[128,512]{1,0:T(8,128)(2,1)S(1)}, u32[]{:S(2)}, u32[]{:S(2)}) collective-permute-start(bf16[128,512]{1,0:T(8,128)(2,1)} %q.1), channel_id=1, source_target_pairs={{8,0},{12,4},{9,1},{13,5},{10,2},{14,6},{11,3},{15,7},{24,16},{28,... | collective-permute-start | bytes 393224 | tf_op jit(solution)/shard_map/ppermute | solution.py:352
  6.1 3.5 %collective-permute-start.1 = (bf16[128,512]{1,0:T(8,128)(2,1)}, bf16[128,512]{1,0:T(8,128)(2,1)S(1)}, u32[]{:S(2)}, u32[]{:S(2)}) collective-permute-start(bf16[128,512]{1,0:T(8,128)(2,1)} %k.1), channel_id=1, source_target_pairs={{0,4},{4,8},{8,12},{1,5},{5,9},{9,13},{2,6},{6,10},{10,14},{3,7},{... | collective-permute-start | bytes 393224 | tf_op jit(solution)/shard_map/ppermute | solution.py:353
  9.6 4.4 %collective-permute-start.2 = (bf16[128,512]{1,0:T(8,128)(2,1)}, bf16[128,512]{1,0:T(8,128)(2,1)S(1)}, u32[]{:S(2)}, u32[]{:S(2)}) collective-permute-start(bf16[128,512]{1,0:T(8,128)(2,1)} %v.1), channel_id=1, source_target_pairs={{0,4},{4,8},{8,12},{1,5},{5,9},{9,13},{2,6},{6,10},{10,14},{3,7},{... | collective-permute-start | bytes 393224 | tf_op jit(solution)/shard_map/ppermute | solution.py:354
  14.2 0.9 %copy-done.5 = bf16[128,512]{1,0:T(8,128)(2,1)S(1)} copy-done((bf16[128,512]{1,0:T(8,128)(2,1)S(1)}, bf16[128,512]{1,0:T(8,128)(2,1)}, u32[]{:S(2)}) %copy-start.5) | copy-done | bytes 131096
  15.1 0.9 %copy-done.6 = bf16[128,512]{1,0:T(8,128)(2,1)S(1)} copy-done((bf16[128,512]{1,0:T(8,128)(2,1)S(1)}, bf16[128,512]{1,0:T(8,128)(2,1)}, u32[]{:S(2)}) %copy-start.6) | copy-done | bytes 131096
  16.0 0.9 %copy-done.7 = bf16[128,512]{1,0:T(8,128)(2,1)S(1)} copy-done((bf16[128,512]{1,0:T(8,128)(2,1)S(1)}, bf16[128,512]{1,0:T(8,128)(2,1)}, u32[]{:S(2)}) %copy-start.7) | copy-done | bytes 131096
  16.9 0.7 %constant_dynamic-slice_fusion.1 = (bf16[128,768]{1,0:T(8,128)(2,1)S(1)}, bf16[128,768]{1,0:T(8,128)(2,1)}) fusion(bf16[1024,768]{1,0:T(8,128)(2,1)S(1)} %copy-done.1, s32[]{:T(128)S(6)} %select_n.17, s32[]{:T(128)S(6)} %select_n.19), kind=kLoop, calls=%fused_computation.4 | loop fusion | bytes 786440 | tf_op jit(solution)/shard_map/dynamic_slice | solution.py:344
  17.7 1.0 %pad_maximum_fusion = bf16[256,768]{1,0:T(8,128)(2,1)S(1)} fusion(bf16[128,768]{1,0:T(8,128)(2,1)} %get-tuple-element.74, bf16[128,768]{1,0:T(8,128)(2,1)S(1)} %get-tuple-element.73), kind=kLoop, calls=%fused_computation.2 | loop fusion | flops 786432 | bytes 786432 | tf_op jit(solution)/shard_map/concatenate | solution.py:342
  18.7 2.6 %collective-permute-done.4.refs_2_ = bf16[128,1024]{1,0:T(8,128)(2,1)S(1)} collective-permute-done((bf16[128,1024]{1,0:T(8,128)(2,1)}, bf16[128,1024]{1,0:T(8,128)(2,1)S(1)}, u32[]{:S(2)}, u32[]{:S(2)}) %collective-permute-start.4) | collective-permute-done | bytes 262176 | tf_op jit(solution)/shard_map/ppermute | solution.py:325
  21.3 0.3 collective-permute-start.7
  21.6 1.8 %collective-permute-start.8 = (bf16[256,768]{1,0:T(8,128)(2,1)S(1)}, bf16[256,768]{1,0:T(8,128)(2,1)S(1)}, u32[]{:S(2)}, u32[]{:S(2)}) collective-permute-start(bf16[256,768]{1,0:T(8,128)(2,1)S(1)} %collective-permute-done.3.refs_2_), channel_id=1, source_target_pairs={{0,16},{16,0},{1,17},{17,1},{2,18},{18,2},{3,19},{19,3},{4,20},{20... | collective-permute-start | bytes 1179656 | tf_op jit(solution)/shard_map/ppermute | solution.py:325
  23.3 0.5 collective-permute-start.9
  23.9 1.5 %shard_map.92 = (f32[128,512]{1,0:T(8,128)S(1)}, f32[128,128]{1,0:T(8,128)S(1)}, bf16[144,512]{1,0:T(8,128)(2,1)S(1)}) custom-call(s32[4]{0:T(128)S(1)} %pad_add_fusion.place, bf16[128,1536]{1,0:T(8,128)(2,1)S(1)} %shard_map.91.held, bf16[128,512]{1,0:T(8,128)(2,1)S(1)} %collective-permute-done.q_up, bf16[128,512]{1,0:T(8,128)(2,1)S(1)} %collective-permute-done.1.k_low, ...), custom_call_target="tpu_custom_call" | custom-call | flops 134217728 | bytes 1572864 | tf_op jit(solution)/shard_map/pallas_call | solution.py:114
  25.3 4.2 %collective-permute-start.5 = (bf16[144,512]{1,0:T(8,128)(2,1)S(1)}, bf16[144,512]{1,0:T(8,128)(2,1)S(1)}, u32[]{:S(2)}, u32[]{:S(2)}) collective-permute-start(bf16[144,512]{1,0:T(8,128)(2,1)S(1)} %get-tuple-element.47), channel_id=1, source_target_pairs={{0,8},{4,12},{1,9},{5,13},{2,10},{6,14},{3,11},{7,15},{16,24},{20,... | collective-permute-start | bytes 442376 | tf_op jit(solution)/shard_map/ppermute | solution.py:360
  29.6 2.2 %copy-done = bf16[512,4096]{1,0:T(8,128)(2,1)S(1)} copy-done((bf16[512,4096]{1,0:T(8,128)(2,1)S(1)}, bf16[512,4096]{1,0:T(8,128)(2,1)}, u32[]{:S(2)}) %copy-start) | copy-done | bytes 4194328
  31.7 0.3 shard_map.93.w
  32.1 0.8 %collective-permute-done.5.low = bf16[144,512]{1,0:T(8,128)(2,1)S(1)} collective-permute-done((bf16[144,512]{1,0:T(8,128)(2,1)S(1)}, bf16[144,512]{1,0:T(8,128)(2,1)S(1)}, u32[]{:S(2)}, u32[]{:S(2)}) %collective-permute-start.5) | collective-permute-done | bytes 147488 | tf_op jit(solution)/shard_map/ppermute | solution.py:360
  32.9 1.8 %shard_map.94 = (bf16[64,4096]{1,0:T(8,128)(2,1)S(1)}, f32[64,4096]{1,0:T(8,128)S(1)}) custom-call(s32[4]{0:T(128)S(1)} %pad_add_fusion.place, f32[128,512]{1,0:T(8,128)S(1)} %get-tuple-element.45.own, f32[128,128]{1,0:T(8,128)S(1)} %get-tuple-element.46.own_log, bf16[144,512]{1,0:T(8,128)(2,1)S(1)} %collective-permute-done.5.low, ...), custom_call_target="tpu_custom_call" | custom-call | flops 536870912 | bytes 5767168 | tf_op jit(solution)/shard_map/pallas_call | solution.py:213
  34.7 0.5 collective-permute-start.12
  35.3 2.3 %collective-permute-done.11.refs_3_ = bf16[128,1024]{1,0:T(8,128)(2,1)S(1)} collective-permute-done((bf16[128,1024]{1,0:T(8,128)(2,1)S(1)}, bf16[128,1024]{1,0:T(8,128)(2,1)S(1)}, u32[]{:S(2)}, u32[]{:S(2)}) %collective-permute-start.11) | collective-permute-done | bytes 262176 | tf_op jit(solution)/shard_map/ppermute | solution.py:325
  37.6 0.1 collective-permute-start.17
  37.7 0.1 convert_add_fusion
  37.9 0.6 %collective-permute-start.13 = (bf16[32,4096]{1,0:T(8,128)(2,1)S(1)}, bf16[32,4096]{1,0:T(8,128)(2,1)S(1)}, u32[]{:S(2)}, u32[]{:S(2)}) collective-permute-start(bf16[32,4096]{1,0:T(8,128)(2,1)S(1)} %slice.20), channel_id=1, source_target_pairs={{0,2},{2,0},{1,3},{3,1},{4,6},{6,4},{5,7},{7,5},{8,10},{10,8},{9,1... | collective-permute-start | bytes 786440 | tf_op jit(solution)/shard_map/ppermute | solution.py:325
  38.6 4.6 %collective-permute-start.15 = (bf16[128,768]{1,0:T(8,128)(2,1)S(1)}, bf16[128,768]{1,0:T(8,128)(2,1)S(1)}, u32[]{:S(2)}, u32[]{:S(2)}) collective-permute-start(bf16[128,768]{1,0:T(8,128)(2,1)S(1)} %get-tuple-element.75), channel_id=1, source_target_pairs={{0,4},{4,0},{8,12},{12,8},{1,5},{5,1},{9,13},{13,9},{2,6},{6,2},{1... | collective-permute-start | bytes 589832 | tf_op jit(solution)/shard_map/ppermute | solution.py:382
  43.2 0.5 collective-permute-start.14
  43.7 5.0 %collective-permute-done.15.refs_6_ = bf16[128,768]{1,0:T(8,128)(2,1)S(1)} collective-permute-done((bf16[128,768]{1,0:T(8,128)(2,1)S(1)}, bf16[128,768]{1,0:T(8,128)(2,1)S(1)}, u32[]{:S(2)}, u32[]{:S(2)}) %collective-permute-start.15) | collective-permute-done | bytes 196640 | tf_op jit(solution)/shard_map/ppermute | solution.py:382
  48.7 1.5 %collective-permute-done.14.refs_5_ = bf16[128,768]{1,0:T(8,128)(2,1)S(1)} collective-permute-done((bf16[128,768]{1,0:T(8,128)(2,1)S(1)}, bf16[128,768]{1,0:T(8,128)(2,1)S(1)}, u32[]{:S(2)}, u32[]{:S(2)}) %collective-permute-start.14) | collective-permute-done | bytes 196640 | tf_op jit(solution)/shard_map/ppermute | solution.py:325
  50.3 0.5 collective-permute-start.19
  50.9 1.3 %shard_map.95.hid = bf16[256,1024]{1,0:T(8,128)(2,1)S(1)} custom-call(s32[4]{0:T(128)S(1)} %pad_add_fusion.place, f32[32,4096]{1,0:T(8,128)S(1)} %slice.17.g0, bf16[32,4096]{1,0:T(8,128)(2,1)S(1)} %collective-permute-done.13.g1, bf16[256,1024]{1,0:T(8,128)(2,1)S(1)} %bitcast.7, f32[1,1024]{1,0:T(1,128)S(1)} %bitcast.8, bf16[128,1024]{1,0:T(8,128)(2,1)S(1)} %copy-done.4, ...), custom_call_target="tpu_custom_call" | custom-call | flops 268435456 | bytes 1572864 | tf_op jit(solution)/shard_map/pallas_call | solution.py:260
  52.1 3.5 %shard_map.96 = bf16[256,3072]{1,0:T(8,128)(2,1)} custom-call(s32[4]{0:T(128)S(1)} %pad_add_fusion.place, bf16[256,1024]{1,0:T(8,128)(2,1)S(1)} %shard_map.95.hid, bf16[1024,768]{1,0:T(8,128)(2,1)S(1)} %copy-done.1, bf16[1024,768]{1,0:T(8,128)(2,1)S(1)} %collective-permute-done.17.refs_1_, bf16[256,768]{1,0:T(8,128)(2,1)S(1)} %collective-permute-done.3.refs_2_, ...), custom_call_target="tpu_custom_call" | custom-call | flops 1610612736 | bytes 7864320 | tf_op jit(solution)/shard_map/pallas_call | solution.py:309
  (40 shorter events, 0.6 us)
Async XLA Ops:
  0.0 16.9 %copy-start.1 = (bf16[1024,768]{1,0:T(8,128)(2,1)S(1)}, bf16[1024,768]{1,0:T(8,128)(2,1)}, u32[]{:S(2)}) copy-start(bf16[1024,768]{1,0:T(8,128)(2,1)} %refs_0_.1) | copy-start | bytes 4718596
  0.0 23.3 %copy-start.4 = (bf16[128,1024]{1,0:T(8,128)(2,1)S(1)}, bf16[128,1024]{1,0:T(8,128)(2,1)}, u32[]{:S(2)}) copy-start(bf16[128,1024]{1,0:T(8,128)(2,1)} %refs_0_) | copy-start | bytes 786436
  1.9 19.4 %collective-permute-start.3 = (bf16[256,768]{1,0:T(8,128)(2,1)}, bf16[256,768]{1,0:T(8,128)(2,1)S(1)}, u32[]{:S(2)}, u32[]{:S(2)}) collective-permute-start(bf16[256,768]{1,0:T(8,128)(2,1)} %constant_dynamic-slice_fusion.2), channel_id=1, source_target_pairs={{0,2},{2,0},{1,3},{3,1},{4,6},{6,4},{5,7},{7,5},{8,10},{10,8},{9,1... | collective-permute-start | bytes 1179656 | tf_op jit(solution)/shard_map/ppermute | solution.py:325
  4.8 13.8 %collective-permute-start = (bf16[128,512]{1,0:T(8,128)(2,1)}, bf16[128,512]{1,0:T(8,128)(2,1)S(1)}, u32[]{:S(2)}, u32[]{:S(2)}) collective-permute-start(bf16[128,512]{1,0:T(8,128)(2,1)} %q.1), channel_id=1, source_target_pairs={{8,0},{12,4},{9,1},{13,5},{10,2},{14,6},{11,3},{15,7},{24,16},{28,... | collective-permute-start | bytes 393224 | tf_op jit(solution)/shard_map/ppermute | solution.py:352
  6.1 12.6 %collective-permute-start.1 = (bf16[128,512]{1,0:T(8,128)(2,1)}, bf16[128,512]{1,0:T(8,128)(2,1)S(1)}, u32[]{:S(2)}, u32[]{:S(2)}) collective-permute-start(bf16[128,512]{1,0:T(8,128)(2,1)} %k.1), channel_id=1, source_target_pairs={{0,4},{4,8},{8,12},{1,5},{5,9},{9,13},{2,6},{6,10},{10,14},{3,7},{... | collective-permute-start | bytes 393224 | tf_op jit(solution)/shard_map/ppermute | solution.py:353
  9.6 9.1 %collective-permute-start.2 = (bf16[128,512]{1,0:T(8,128)(2,1)}, bf16[128,512]{1,0:T(8,128)(2,1)S(1)}, u32[]{:S(2)}, u32[]{:S(2)}) collective-permute-start(bf16[128,512]{1,0:T(8,128)(2,1)} %v.1), channel_id=1, source_target_pairs={{0,4},{4,8},{8,12},{1,5},{5,9},{9,13},{2,6},{6,10},{10,14},{3,7},{... | collective-permute-start | bytes 393224 | tf_op jit(solution)/shard_map/ppermute | solution.py:354
  14.1 7.2 %collective-permute-start.4 = (bf16[128,1024]{1,0:T(8,128)(2,1)}, bf16[128,1024]{1,0:T(8,128)(2,1)S(1)}, u32[]{:S(2)}, u32[]{:S(2)}) collective-permute-start(bf16[128,1024]{1,0:T(8,128)(2,1)} %refs_0_), channel_id=1, source_target_pairs={{0,2},{2,0},{1,3},{3,1},{4,6},{6,4},{5,7},{7,5},{8,10},{10,8},{9,1... | collective-permute-start | bytes 786440 | tf_op jit(solution)/shard_map/ppermute | solution.py:325
  14.2 0.9 %copy-start.5 = (bf16[128,512]{1,0:T(8,128)(2,1)S(1)}, bf16[128,512]{1,0:T(8,128)(2,1)}, u32[]{:S(2)}) copy-start(bf16[128,512]{1,0:T(8,128)(2,1)} %q.1) | copy-start | bytes 393220
  15.1 0.9 %copy-start.6 = (bf16[128,512]{1,0:T(8,128)(2,1)S(1)}, bf16[128,512]{1,0:T(8,128)(2,1)}, u32[]{:S(2)}) copy-start(bf16[128,512]{1,0:T(8,128)(2,1)} %k.1) | copy-start | bytes 393220
  16.0 0.9 %copy-start.7 = (bf16[128,512]{1,0:T(8,128)(2,1)S(1)}, bf16[128,512]{1,0:T(8,128)(2,1)}, u32[]{:S(2)}) copy-start(bf16[128,512]{1,0:T(8,128)(2,1)} %v.1) | copy-start | bytes 393220
  21.3 11.6 %collective-permute-start.7 = (bf16[256,768]{1,0:T(8,128)(2,1)S(1)}, bf16[256,768]{1,0:T(8,128)(2,1)S(1)}, u32[]{:S(2)}, u32[]{:S(2)}) collective-permute-start(bf16[256,768]{1,0:T(8,128)(2,1)S(1)} %pad_maximum_fusion), channel_id=1, source_target_pairs={{0,2},{2,0},{1,3},{3,1},{4,6},{6,4},{5,7},{7,5},{8,10},{10,8},{9,1... | collective-permute-start | bytes 1179656 | tf_op jit(solution)/shard_map/ppermute | solution.py:325
  21.6 11.3 %collective-permute-start.8 = (bf16[256,768]{1,0:T(8,128)(2,1)S(1)}, bf16[256,768]{1,0:T(8,128)(2,1)S(1)}, u32[]{:S(2)}, u32[]{:S(2)}) collective-permute-start(bf16[256,768]{1,0:T(8,128)(2,1)S(1)} %collective-permute-done.3.refs_2_), channel_id=1, source_target_pairs={{0,16},{16,0},{1,17},{17,1},{2,18},{18,2},{3,19},{19,3},{4,20},{20... | collective-permute-start | bytes 1179656 | tf_op jit(solution)/shard_map/ppermute | solution.py:325
  23.3 9.5 %collective-permute-start.6 = (bf16[256,768]{1,0:T(8,128)(2,1)S(1)}, bf16[256,768]{1,0:T(8,128)(2,1)S(1)}, u32[]{:S(2)}, u32[]{:S(2)}) collective-permute-start(bf16[256,768]{1,0:T(8,128)(2,1)S(1)} %collective-permute-done.3.refs_2_), channel_id=1, source_target_pairs={{0,1},{1,0},{2,3},{3,2},{4,5},{5,4},{6,7},{7,6},{8,9},{9,8},{10,11... | collective-permute-start | bytes 1179656 | tf_op jit(solution)/shard_map/ppermute | solution.py:325
  23.3 9.5 %collective-permute-start.9 = (bf16[128,1024]{1,0:T(8,128)(2,1)S(1)}, bf16[128,1024]{1,0:T(8,128)(2,1)S(1)}, u32[]{:S(2)}, u32[]{:S(2)}) collective-permute-start(bf16[128,1024]{1,0:T(8,128)(2,1)S(1)} %copy-done.4), channel_id=1, source_target_pairs={{0,1},{1,0},{2,3},{3,2},{4,5},{5,4},{6,7},{7,6},{8,9},{9,8},{10,11... | collective-permute-start | bytes 786440 | tf_op jit(solution)/shard_map/ppermute | solution.py:325
  25.3 7.5 %collective-permute-start.5 = (bf16[144,512]{1,0:T(8,128)(2,1)S(1)}, bf16[144,512]{1,0:T(8,128)(2,1)S(1)}, u32[]{:S(2)}, u32[]{:S(2)}) collective-permute-start(bf16[144,512]{1,0:T(8,128)(2,1)S(1)} %get-tuple-element.47), channel_id=1, source_target_pairs={{0,8},{4,12},{1,9},{5,13},{2,10},{6,14},{3,11},{7,15},{16,24},{20,... | collective-permute-start | bytes 442376 | tf_op jit(solution)/shard_map/ppermute | solution.py:360
  29.5 2.2 %copy-start = (bf16[512,4096]{1,0:T(8,128)(2,1)S(1)}, bf16[512,4096]{1,0:T(8,128)(2,1)}, u32[]{:S(2)}) copy-start(bf16[512,4096]{1,0:T(8,128)(2,1)} %source) | copy-start | bytes 12582916
  31.7 1.1 %copy-start.3 = (bf16[128,1024]{1,0:T(8,128)(2,1)S(1)}, bf16[128,1024]{1,0:T(8,128)(2,1)}, u32[]{:S(2)}) copy-start(bf16[128,1024]{1,0:T(8,128)(2,1)} %x.1) | copy-start | bytes 786436
  34.7 2.9 %collective-permute-start.10 = (bf16[64,4096]{1,0:T(8,128)(2,1)S(1)}, bf16[64,4096]{1,0:T(8,128)(2,1)S(1)}, u32[]{:S(2)}, u32[]{:S(2)}) collective-permute-start(bf16[64,4096]{1,0:T(8,128)(2,1)S(1)} %get-tuple-element.56), channel_id=1, source_target_pairs={{0,1},{1,0},{2,3},{3,2},{4,5},{5,4},{6,7},{7,6},{8,9},{9,8},{10,11... | collective-permute-start | bytes 1572872 | tf_op jit(solution)/shard_map/ppermute | solution.py:325
  34.7 2.8 %collective-permute-start.12 = (bf16[256,768]{1,0:T(8,128)(2,1)S(1)}, bf16[256,768]{1,0:T(8,128)(2,1)S(1)}, u32[]{:S(2)}, u32[]{:S(2)}) collective-permute-start(bf16[256,768]{1,0:T(8,128)(2,1)S(1)} %collective-permute-done.8.refs_3_), channel_id=1, source_target_pairs={{0,1},{1,0},{2,3},{3,2},{4,5},{5,4},{6,7},{7,6},{8,9},{9,8},{10,11... | collective-permute-start | bytes 1179656 | tf_op jit(solution)/shard_map/ppermute | solution.py:325
  35.2 2.3 %collective-permute-start.11 = (bf16[128,1024]{1,0:T(8,128)(2,1)S(1)}, bf16[128,1024]{1,0:T(8,128)(2,1)S(1)}, u32[]{:S(2)}, u32[]{:S(2)}) collective-permute-start(bf16[128,1024]{1,0:T(8,128)(2,1)S(1)} %collective-permute-done.4.refs_2_), channel_id=1, source_target_pairs={{0,1},{1,0},{2,3},{3,2},{4,5},{5,4},{6,7},{7,6},{8,9},{9,8},{10,11... | collective-permute-start | bytes 786440 | tf_op jit(solution)/shard_map/ppermute | solution.py:325
  37.6 12.6 %collective-permute-start.17 = (bf16[1024,768]{1,0:T(8,128)(2,1)S(1)}, bf16[1024,768]{1,0:T(8,128)(2,1)S(1)}, u32[]{:S(2)}, u32[]{:S(2)}) collective-permute-start(bf16[1024,768]{1,0:T(8,128)(2,1)S(1)} %copy-done.1), channel_id=1, source_target_pairs={{0,1},{1,0},{2,3},{3,2},{4,5},{5,4},{6,7},{7,6},{8,9},{9,8},{10,11... | collective-permute-start | bytes 4718600 | tf_op jit(solution)/shard_map/ppermute | solution.py:325
  37.8 13.0 %copy-start.2 = (bf16[32,8,1024]{2,1,0:T(8,128)(2,1)S(1)}, bf16[32,8,1024]{2,1,0:T(8,128)(2,1)}, u32[]{:S(2)}) copy-start(bf16[32,8,1024]{2,1,0:T(8,128)(2,1)} %param.15) | copy-start | bytes 1572868
  37.8 13.0 %copy-start.8 = (f32[1024]{0:T(1024)S(1)}, f32[1024]{0:T(1024)}, u32[]{:S(2)}) copy-start(f32[1024]{0:T(1024)} %param.16) | copy-start | bytes 12292
  37.9 12.3 %collective-permute-start.13 = (bf16[32,4096]{1,0:T(8,128)(2,1)S(1)}, bf16[32,4096]{1,0:T(8,128)(2,1)S(1)}, u32[]{:S(2)}, u32[]{:S(2)}) collective-permute-start(bf16[32,4096]{1,0:T(8,128)(2,1)S(1)} %slice.20), channel_id=1, source_target_pairs={{0,2},{2,0},{1,3},{3,1},{4,6},{6,4},{5,7},{7,5},{8,10},{10,8},{9,1... | collective-permute-start | bytes 786440 | tf_op jit(solution)/shard_map/ppermute | solution.py:325
  38.5 11.7 %collective-permute-start.16 = (bf16[256,768]{1,0:T(8,128)(2,1)S(1)}, bf16[256,768]{1,0:T(8,128)(2,1)S(1)}, u32[]{:S(2)}, u32[]{:S(2)}) collective-permute-start(bf16[256,768]{1,0:T(8,128)(2,1)S(1)} %collective-permute-done.7.refs_4_), channel_id=1, source_target_pairs={{0,1},{1,0},{2,3},{3,2},{4,5},{5,4},{6,7},{7,6},{8,9},{9,8},{10,11... | collective-permute-start | bytes 1179656 | tf_op jit(solution)/shard_map/ppermute | solution.py:325
  38.6 10.1 %collective-permute-start.15 = (bf16[128,768]{1,0:T(8,128)(2,1)S(1)}, bf16[128,768]{1,0:T(8,128)(2,1)S(1)}, u32[]{:S(2)}, u32[]{:S(2)}) collective-permute-start(bf16[128,768]{1,0:T(8,128)(2,1)S(1)} %get-tuple-element.75), channel_id=1, source_target_pairs={{0,4},{4,0},{8,12},{12,8},{1,5},{5,1},{9,13},{13,9},{2,6},{6,2},{1... | collective-permute-start | bytes 589832 | tf_op jit(solution)/shard_map/ppermute | solution.py:382
  43.2 7.0 %collective-permute-start.14 = (bf16[128,768]{1,0:T(8,128)(2,1)S(1)}, bf16[128,768]{1,0:T(8,128)(2,1)S(1)}, u32[]{:S(2)}, u32[]{:S(2)}) collective-permute-start(bf16[128,768]{1,0:T(8,128)(2,1)S(1)} %get-tuple-element.76), channel_id=1, source_target_pairs={{0,16},{16,0},{1,17},{17,1},{2,18},{18,2},{3,19},{19,3},{4,20},{20... | collective-permute-start | bytes 589832 | tf_op jit(solution)/shard_map/ppermute | solution.py:325
  50.2 1.9 %collective-permute-start.18 = (bf16[128,768]{1,0:T(8,128)(2,1)S(1)}, bf16[128,768]{1,0:T(8,128)(2,1)S(1)}, u32[]{:S(2)}, u32[]{:S(2)}) collective-permute-start(bf16[128,768]{1,0:T(8,128)(2,1)S(1)} %collective-permute-done.14.refs_5_), channel_id=1, source_target_pairs={{0,1},{1,0},{2,3},{3,2},{4,5},{5,4},{6,7},{7,6},{8,9},{9,8},{10,11... | collective-permute-start | bytes 589832 | tf_op jit(solution)/shard_map/ppermute | solution.py:325
  50.3 1.8 %collective-permute-start.19 = (bf16[128,768]{1,0:T(8,128)(2,1)S(1)}, bf16[128,768]{1,0:T(8,128)(2,1)S(1)}, u32[]{:S(2)}, u32[]{:S(2)}) collective-permute-start(bf16[128,768]{1,0:T(8,128)(2,1)S(1)} %collective-permute-done.15.refs_6_), channel_id=1, source_target_pairs={{0,1},{1,0},{2,3},{3,2},{4,5},{5,4},{6,7},{7,6},{8,9},{9,8},{10,11... | collective-permute-start | bytes 589832 | tf_op jit(solution)/shard_map/ppermute | solution.py:325

commit v4 on v3

--- a/solution.py
+++ b/solution.py
@@ -270,29 +270,27 @@
     )(place, g0, g1, embed, gain, *bridge)
 
 
-def local_kernel(place, hid, *refs):
-    whole, chips = refs[:2], (refs[2:7], refs[7:12])
-    out, held, sems = refs[12:]
-    ctx, dp, sub, grp = (place[i] for i in range(4))
-    odd = ctx % 2
-    depth, width = whole[0].shape
-    quarter, eighth = depth // 4, depth // 8
-
-    def columns(first, count):
-        return hid[:, pl.ds(pl.multiple_of(first, 128), count)]
-
+def local_kernel(place, hid, *refs, pieces):
+    whole = refs[:2]
+    parts = refs[2 : 2 + 4 * pieces]
+    out, held, sems = refs[2 + 4 * pieces :]
+    dp, sub, grp = place[1], place[2], place[3]
+    width = whole[0].shape[1]
     copies = []
     for i, b in enumerate(block_order(dp, sub)):
         if i < 2:
             total = dot(hid[...], whole[i][...])
         else:
-            x0, y0, x1, y1, z1 = chips[i - 2]
-            total = dot(columns(grp * quarter, quarter), x0[...])
-            total += dot(columns((1 - grp) * quarter, quarter), y0[...])
-            mixed = [columns(4 * eighth + grp * eighth, eighth), columns(6 * eighth + odd * eighth, eighth)]
-            total += dot(jnp.concatenate(mixed, axis=1), x1[...])
-            total += dot(columns(4 * eighth + (1 - grp) * eighth, eighth), y1[...])
-            total += dot(columns(6 * eighth + (1 - odd) * eighth, eighth), z1[...])
+            total = None
+            for j in range(2):
+                first = (grp if j == 0 else 1 - grp) * (hid.shape[1] // 2)
+                for n in range(pieces):
+                    ref = parts[((i - 2) * 2 + j) * pieces + n]
+                    depth = ref.shape[0]
+                    lhs = hid[:, pl.ds(pl.multiple_of(first, 128), depth)]
+                    first += depth
+                    term = dot(lhs, ref[...])
+                    total = term if total is None else total + term
         held[i, :, :] = total.astype(BF16)
         copy = pltpu.make_async_copy(
             held.at[i], out.at[:, pl.ds(pl.multiple_of(b * width, 128), width)], sems.at[i]
@@ -303,13 +301,14 @@
         copy.wait()
 
 
-def local(place, hid, *weights):
+def local(place, hid, whole, parts):
     rows = hid.shape[0]
-    block = weights[0].shape[1]
-    return pl.pallas_call(
-        local_kernel,
+    block = whole[0].shape[1]
+    pieces = len(parts) // 4
+    return pl.pallas_call(
+        functools.partial(local_kernel, pieces=pieces),
         out_shape=jax.ShapeDtypeStruct((rows, 4 * block), BF16),
-        in_specs=[SMEM] + [VMEM] * (1 + len(weights)),
+        in_specs=[SMEM] + [VMEM] * (3 + len(parts)),
         out_specs=pl.BlockSpec(memory_space=pl.ANY),
         scratch_shapes=[pltpu.VMEM((4, rows, block), BF16), pltpu.SemaphoreType.DMA((4,))],
         compiler_params=pltpu.CompilerParams(vmem_limit_bytes=12 * 2**20),
@@ -318,7 +317,7 @@
             bytes_accessed=8 * DL * block + 8 * rows * block,
             transcendentals=0,
         ),
-    )(place, hid, *weights)
+    )(place, hid, *whole, *parts)
 
 
 def swap(x, axis):
@@ -335,59 +334,52 @@
     ctx, dp, sub, grp = (lax.axis_index(a) for a in ("ctx", "dp", "sub", "groups"))
     place = jnp.stack([ctx, dp, sub, grp]).astype(jnp.int32)
 
-    quarter, eighth = qkv_weight.shape[0] // 4, qkv_weight.shape[0] // 8
+    quarter = qkv_weight.shape[0] // 4
     held = hold(q_glob, k_glob, v_glob)
-    later = after(qkv_weight, held)
-    w0 = lax.dynamic_slice_in_dim(qkv_weight, grp * quarter, quarter, 0)
-    w1 = jnp.concatenate(
-        [
-            lax.dynamic_slice_in_dim(later, (4 + grp) * eighth, eighth, 0),
-            lax.dynamic_slice_in_dim(later, (6 + ctx % 2) * eighth, eighth, 0),
-        ],
-        axis=0,
-    )
+    w0 = lax.dynamic_slice_in_dim(qkv_weight, grp * 2 * quarter, quarter, 0)
+    w1 = lax.dynamic_slice_in_dim(after(qkv_weight, held), (grp * 2 + 1) * quarter, quarter, 0)
 
     x0 = swap(w0, "dp")
-    bridge_x = swap(bridge_weight, "dp")
     q_up = lax.ppermute(q_glob, "ctx", [(2, 0), (3, 1)])
     k_low = lax.ppermute(k_glob, "ctx", [(0, 1), (1, 2), (2, 3)])
     v_low = lax.ppermute(v_glob, "ctx", [(0, 1), (1, 2), (2, 3)])
-    q_up, k_low, v_low, x0, bridge_x, w1, held, bridge_weight, place = lax.optimization_barrier(
-        (q_up, k_low, v_low, x0, bridge_x, w1, held, bridge_weight, place)
+    q_up, k_low, v_low, x0, held, w1, bridge_weight, qkv_weight, place = (
+        lax.optimization_barrier(
+            (q_up, k_low, v_low, x0, held, w1, bridge_weight, qkv_weight, place)
+        )
     )
 
     own, own_log, up = attend(place, held, q_up, k_low, v_low)
     low = lax.ppermute(up, "ctx", [(0, 2), (1, 3)])
     x1 = swap(w1, "dp")
     y0 = swap(x0, "groups")
-    core_x0 = swap(x0, "sub")
-    bridge_core = swap(bridge_weight, "sub")
+    other_core = swap(qkv_weight, "sub")
     out_weight = bring(after(out_weight, up), 4)
-    low, core_x0, x1, y0, out_weight, bridge_x, bridge_core, qkv_weight = lax.optimization_barrier(
-        (low, core_x0, x1, y0, out_weight, bridge_x, bridge_core, qkv_weight)
+    bridge_x = swap(bridge_weight, "dp")
+    low, x0, x1, y0, other_core, out_weight = lax.optimization_barrier(
+        (low, x0, x1, y0, other_core, out_weight)
     )
 
     away, kept = project(place, own, own_log, low, x_glob, out_weight)
     away = swap(away, "sub")
+    y1 = swap(x1, "groups")
+    bridge_both = swap(bridge_x, "sub")
     core_y0 = swap(y0, "sub")
-    bridge_both = swap(bridge_x, "sub")
-    away, bridge_both, core_y0, x1, qkv_weight = lax.optimization_barrier(
-        (away, bridge_both, core_y0, x1, qkv_weight)
+    away, core_y0, bridge_both, x0, x1, bridge_weight = lax.optimization_barrier(
+        (away, core_y0, bridge_both, x0, x1, bridge_weight)
     )
 
     summed = kept + away.astype(F32)
     mid = summed.shape[0] // 2
     across = swap(summed[:mid].astype(BF16), "dp")
-    y1 = swap(x1[:eighth], "groups")
-    z1 = lax.ppermute(x1[eighth:], "ctx", [(0, 1), (1, 0), (2, 3), (3, 2)])
     core_x1 = swap(x1, "sub")
-    other_core = swap(qkv_weight, "sub")
-    across, y1, z1, core_x1, other_core = lax.optimization_barrier(
-        (across, y1, z1, core_x1, other_core)
+    bridge_core = swap(bridge_weight, "sub")
+    core_x0 = swap(x0, "sub")
+    across, y1, core_x0, core_x1, bridge_core = lax.optimization_barrier(
+        (across, y1, core_x0, core_x1, bridge_core)
     )
 
     core_y1 = swap(y1, "sub")
-    core_z1 = swap(z1, "sub")
     rows = byte_embed.shape[0] * byte_embed.shape[1]
     hidden = bytes_in(
         place,
@@ -400,9 +392,8 @@
     result = local(
         place,
         hidden,
-        *(qkv_weight, other_core),
-        *(x0, y0, x1, y1, z1),
-        *(core_x0, core_y0, core_x1, core_y1, core_z1),
+        [qkv_weight, other_core],
+        [x0, x1, y0, y1, core_x0, core_x1, core_y0, core_y1],
     )
     return result.reshape(byte_embed.shape[0], P_SIZE, result.shape[1])
 

time: 56 us -> 53 us (0.946)
  starting transfers between devices: 26.2 us -> 24.1 us
  waiting for transfers between devices: 12.1 us -> 13.2 us
  other arithmetic: 1.12 us -> 0.17 us
  local copies, waits for them, and re-layouts: 7.62 us -> 6.77 us
    ppermute x15 -> x14, waiting for transfers between devices: 6.33 us -> 13.2 us  [swap(): return lax.ppermute(x, axis, [(0, 1), (1, 0)])]
    ppermute x1 -> x0, waiting for transfers between devices: 4.99 us -> none  [small_mesh(): z1 = lax.ppermute(x1[eighth:], 'ctx', [(0, 1), (1, 0), (2, 3), (3, 2)])]
    ppermute x1 -> x0, starting transfers between devices: 4.64 us -> none  [small_mesh(): z1 = lax.ppermute(x1[eighth:], 'ctx', [(0, 1), (1, 0), (2, 3), (3, 2)])]
    ppermute x15 -> x14, starting transfers between devices: 8.13 us -> 9.91 us  [swap(): return lax.ppermute(x, axis, [(0, 1), (1, 0)])]
    dynamic_slice x2, local copies, waits for them, and re-layouts: 2.61 us -> 1.18 us  [the longest x1 1.14 us: small_mesh(): w0 = lax.dynamic_slice_in_dim(qkv_weight, grp * 2 * quarter, quarter, 0)]
    concatenate x1 -> x0, other arithmetic: 0.95 us -> none  [small_mesh(): jnp.concatenate([lax.dynamic_slice_in_dim(later, (4 + grp) * eighth, eigh...]
    ppermute x1, starting transfers between devices: 4.2 us -> 5.01 us  [small_mesh(): low = lax.ppermute(up, 'ctx', [(0, 2), (1, 3)])]
    ppermute x1, waiting for transfers between devices: 0.77 us -> 0.01 us  [small_mesh(): low = lax.ppermute(up, 'ctx', [(0, 2), (1, 3)])]
  transfers between devices with their start and end apart: 20 -> 18, of which waited for: 5 -> 4; matrix products, arithmetic and copies ran while one was open for 3% -> 1% of each run, Pallas kernels for 6% -> 9%
where the time goes in v4:
time: 53 us; the launch traced here: 52.7 us
  starting transfers between devices  24.1 us (45%)
  waiting for transfers between devices  13.2 us (25%)
  Pallas kernels  8.19 us (15%)
  local copies, waits for them, and re-layouts  6.77 us (13%)
    ppermute x14, waiting for transfers between devices, swap(): return lax.ppermute(x, axis, [(0, 1), (1, 0)])  13.2 us
    ppermute x14, starting transfers between devices, swap(): return lax.ppermute(x, axis, [(0, 1), (1, 0)])  9.91 us
    unnamed x18, local copies, waits for them, and re-layouts  5.53 us
    ppermute x1, starting transfers between devices, small_mesh(): low = lax.ppermute(up, 'ctx', [(0, 2), (1, 3)])  5.01 us
    ppermute x1, starting transfers between devices, small_mesh(): v_low = lax.ppermute(v_glob, 'ctx', [(0, 1), (1, 2), (2, 3)])  4.44 us
    ppermute x1, starting transfers between devices, small_mesh(): k_low = lax.ppermute(k_glob, 'ctx', [(0, 1), (1, 2), (2, 3)])  3.49 us
    pallas_call x1, Pallas kernels, local(): pl.pallas_call(functools.partial(local_kernel, pieces=pieces), out_shape=...  3.32 us
    pallas_call x1, Pallas kernels, project(): pl.pallas_call(project_kernel, out_shape=(jax.ShapeDtypeStruct((half, w.s...  1.77 us
  transfers between devices with their start and end apart: 18, of which 4 were waited for; matrix products, arithmetic and copies ran while one was open for 1% of the time, Pallas kernels for 9%

profile of v4, /device:TPU:0, one launch (start us, length us, event | category | flops | bytes accessed | tf_op | source)
XLA Modules:
  0.0 52.7 jit_solution(7718617405115148517)
XLA Ops:
  0.0 1.1 %constant_dynamic-slice_fusion.1 = bf16[256,768]{1,0:T(8,128)(2,1)S(1)} fusion(bf16[1024,768]{1,0:T(8,128)(2,1)} %refs_0_.1, s32[]{:T(128)S(6)} %select_n.6), kind=kLoop, calls=%fused_computation.4 | loop fusion | bytes 786436 | tf_op jit(solution)/shard_map/dynamic_slice | solution.py:339
  1.1 3.0 %collective-permute-start.3 = (bf16[256,768]{1,0:T(8,128)(2,1)S(1)}, bf16[256,768]{1,0:T(8,128)(2,1)S(1)}, u32[]{:S(2)}, u32[]{:S(2)}) collective-permute-start(bf16[256,768]{1,0:T(8,128)(2,1)S(1)} %constant_dynamic-slice_fusion.1), channel_id=1, source_target_pairs={{0,2},{2,0},{1,3},{3,1},{4,6},{6,4},{5,7},{7,5},{8,10},{10,8},{9,1... | collective-permute-start | bytes 1179656 | tf_op jit(solution)/shard_map/ppermute | solution.py:324
  4.2 1.3 %collective-permute-start = (bf16[128,512]{1,0:T(8,128)(2,1)}, bf16[128,512]{1,0:T(8,128)(2,1)S(1)}, u32[]{:S(2)}, u32[]{:S(2)}) collective-permute-start(bf16[128,512]{1,0:T(8,128)(2,1)} %q.1), channel_id=1, source_target_pairs={{8,0},{12,4},{9,1},{13,5},{10,2},{14,6},{11,3},{15,7},{24,16},{28,... | collective-permute-start | bytes 393224 | tf_op jit(solution)/shard_map/ppermute | solution.py:343
  5.4 3.5 %collective-permute-start.1 = (bf16[128,512]{1,0:T(8,128)(2,1)}, bf16[128,512]{1,0:T(8,128)(2,1)S(1)}, u32[]{:S(2)}, u32[]{:S(2)}) collective-permute-start(bf16[128,512]{1,0:T(8,128)(2,1)} %k.1), channel_id=1, source_target_pairs={{0,4},{4,8},{8,12},{1,5},{5,9},{9,13},{2,6},{6,10},{10,14},{3,7},{... | collective-permute-start | bytes 393224 | tf_op jit(solution)/shard_map/ppermute | solution.py:344
  8.9 4.4 %collective-permute-start.2 = (bf16[128,512]{1,0:T(8,128)(2,1)}, bf16[128,512]{1,0:T(8,128)(2,1)S(1)}, u32[]{:S(2)}, u32[]{:S(2)}) collective-permute-start(bf16[128,512]{1,0:T(8,128)(2,1)} %v.1), channel_id=1, source_target_pairs={{0,4},{4,8},{8,12},{1,5},{5,9},{9,13},{2,6},{6,10},{10,14},{3,7},{... | collective-permute-start | bytes 393224 | tf_op jit(solution)/shard_map/ppermute | solution.py:345
  13.4 0.1 pad_add_fusion.place
  13.5 0.9 %copy-done.5 = bf16[128,512]{1,0:T(8,128)(2,1)S(1)} copy-done((bf16[128,512]{1,0:T(8,128)(2,1)S(1)}, bf16[128,512]{1,0:T(8,128)(2,1)}, u32[]{:S(2)}) %copy-start.5) | copy-done | bytes 131096
  14.4 0.9 %copy-done.6 = bf16[128,512]{1,0:T(8,128)(2,1)S(1)} copy-done((bf16[128,512]{1,0:T(8,128)(2,1)S(1)}, bf16[128,512]{1,0:T(8,128)(2,1)}, u32[]{:S(2)}) %copy-start.6) | copy-done | bytes 131096
  15.3 0.9 %copy-done.7 = bf16[128,512]{1,0:T(8,128)(2,1)S(1)} copy-done((bf16[128,512]{1,0:T(8,128)(2,1)S(1)}, bf16[128,512]{1,0:T(8,128)(2,1)}, u32[]{:S(2)}) %copy-start.7) | copy-done | bytes 131096
  16.3 0.1 collective-permute-start.7
  16.4 1.6 %collective-permute-start.6 = (bf16[256,768]{1,0:T(8,128)(2,1)S(1)}, bf16[256,768]{1,0:T(8,128)(2,1)S(1)}, u32[]{:S(2)}, u32[]{:S(2)}) collective-permute-start(bf16[256,768]{1,0:T(8,128)(2,1)S(1)} %collective-permute-done.3.refs_2_), channel_id=1, source_target_pairs={{0,16},{16,0},{1,17},{17,1},{2,18},{18,2},{3,19},{19,3},{4,20},{20... | collective-permute-start | bytes 1179656 | tf_op jit(solution)/shard_map/ppermute | solution.py:324
  18.0 0.5 %collective-permute-start.5 = (bf16[256,768]{1,0:T(8,128)(2,1)S(1)}, bf16[256,768]{1,0:T(8,128)(2,1)S(1)}, u32[]{:S(2)}, u32[]{:S(2)}) collective-permute-start(bf16[256,768]{1,0:T(8,128)(2,1)S(1)} %constant_dynamic-slice_fusion), channel_id=1, source_target_pairs={{0,2},{2,0},{1,3},{3,1},{4,6},{6,4},{5,7},{7,5},{8,10},{10,8},{9,1... | collective-permute-start | bytes 1179656 | tf_op jit(solution)/shard_map/ppermute | solution.py:324
  18.5 1.5 %shard_map.92 = (f32[128,512]{1,0:T(8,128)S(1)}, f32[128,128]{1,0:T(8,128)S(1)}, bf16[144,512]{1,0:T(8,128)(2,1)S(1)}) custom-call(s32[4]{0:T(128)S(1)} %pad_add_fusion.place, bf16[128,1536]{1,0:T(8,128)(2,1)S(1)} %shard_map.91.held, bf16[128,512]{1,0:T(8,128)(2,1)S(1)} %collective-permute-done.q_up, bf16[128,512]{1,0:T(8,128)(2,1)S(1)} %collective-permute-done.1.k_low, ...), custom_call_target="tpu_custom_call" | custom-call | flops 134217728 | bytes 1572864 | tf_op jit(solution)/shard_map/pallas_call | solution.py:114
  20.0 5.0 %collective-permute-start.4 = (bf16[144,512]{1,0:T(8,128)(2,1)S(1)}, bf16[144,512]{1,0:T(8,128)(2,1)S(1)}, u32[]{:S(2)}, u32[]{:S(2)}) collective-permute-start(bf16[144,512]{1,0:T(8,128)(2,1)S(1)} %get-tuple-element.46), channel_id=1, source_target_pairs={{0,8},{4,12},{1,9},{5,13},{2,10},{6,14},{3,11},{7,15},{16,24},{20,... | collective-permute-start | bytes 442376 | tf_op jit(solution)/shard_map/ppermute | solution.py:353
  25.0 2.2 %copy-done = bf16[512,4096]{1,0:T(8,128)(2,1)S(1)} copy-done((bf16[512,4096]{1,0:T(8,128)(2,1)S(1)}, bf16[512,4096]{1,0:T(8,128)(2,1)}, u32[]{:S(2)}) %copy-start) | copy-done | bytes 4194328
  27.2 0.3 shard_map.93.w
  27.5 0.6 %copy-done.4 = bf16[128,1024]{1,0:T(8,128)(2,1)S(1)} copy-done((bf16[128,1024]{1,0:T(8,128)(2,1)S(1)}, bf16[128,1024]{1,0:T(8,128)(2,1)}, u32[]{:S(2)}) %copy-start.4) | copy-done | bytes 262168
  28.2 1.5 %collective-permute-start.10 = (bf16[128,1024]{1,0:T(8,128)(2,1)S(1)}, bf16[128,1024]{1,0:T(8,128)(2,1)S(1)}, u32[]{:S(2)}, u32[]{:S(2)}) collective-permute-start(bf16[128,1024]{1,0:T(8,128)(2,1)S(1)} %copy-done.4), channel_id=1, source_target_pairs={{0,2},{2,0},{1,3},{3,1},{4,6},{6,4},{5,7},{7,5},{8,10},{10,8},{9,1... | collective-permute-start | bytes 786440 | tf_op jit(solution)/shard_map/ppermute | solution.py:324
  29.7 1.8 %shard_map.94 = (bf16[64,4096]{1,0:T(8,128)(2,1)S(1)}, f32[64,4096]{1,0:T(8,128)S(1)}) custom-call(s32[4]{0:T(128)S(1)} %pad_add_fusion.place, f32[128,512]{1,0:T(8,128)S(1)} %get-tuple-element.44.own, f32[128,128]{1,0:T(8,128)S(1)} %get-tuple-element.45.own_log, bf16[144,512]{1,0:T(8,128)(2,1)S(1)} %collective-permute-done.4.low, ...), custom_call_target="tpu_custom_call" | custom-call | flops 536870912 | bytes 5767168 | tf_op jit(solution)/shard_map/pallas_call | solution.py:213
  31.5 0.5 collective-permute-start.9
  32.0 4.0 %collective-permute-done.10.refs_2_ = bf16[128,1024]{1,0:T(8,128)(2,1)S(1)} collective-permute-done((bf16[128,1024]{1,0:T(8,128)(2,1)S(1)}, bf16[128,1024]{1,0:T(8,128)(2,1)S(1)}, u32[]{:S(2)}, u32[]{:S(2)}) %collective-permute-start.10) | collective-permute-done | bytes 262176 | tf_op jit(solution)/shard_map/ppermute | solution.py:324
  36.0 0.5 collective-permute-start.13
  36.5 1.0 %collective-permute-done.11.refs_3_ = bf16[128,1024]{1,0:T(8,128)(2,1)S(1)} collective-permute-done((bf16[128,1024]{1,0:T(8,128)(2,1)S(1)}, bf16[128,1024]{1,0:T(8,128)(2,1)S(1)}, u32[]{:S(2)}, u32[]{:S(2)}) %collective-permute-start.11) | collective-permute-done | bytes 262176 | tf_op jit(solution)/shard_map/ppermute | solution.py:324
  37.6 0.1 collective-permute-start.14
  37.7 0.4 collective-permute-start.15
  38.1 0.1 convert_add_fusion
  38.2 1.6 %collective-permute-start.12 = (bf16[32,4096]{1,0:T(8,128)(2,1)S(1)}, bf16[32,4096]{1,0:T(8,128)(2,1)S(1)}, u32[]{:S(2)}, u32[]{:S(2)}) collective-permute-start(bf16[32,4096]{1,0:T(8,128)(2,1)S(1)} %slice.12), channel_id=1, source_target_pairs={{0,2},{2,0},{1,3},{3,1},{4,6},{6,4},{5,7},{7,5},{8,10},{10,8},{9,1... | collective-permute-start | bytes 786440 | tf_op jit(solution)/shard_map/ppermute | solution.py:324
  39.8 7.8 %collective-permute-done.13.refs_5_ = bf16[256,768]{1,0:T(8,128)(2,1)S(1)} collective-permute-done((bf16[256,768]{1,0:T(8,128)(2,1)S(1)}, bf16[256,768]{1,0:T(8,128)(2,1)S(1)}, u32[]{:S(2)}, u32[]{:S(2)}) %collective-permute-start.13) | collective-permute-done | bytes 393248 | tf_op jit(solution)/shard_map/ppermute | solution.py:324
  47.6 0.1 collective-permute-start.17
  47.7 1.3 %shard_map.95.hid = bf16[256,1024]{1,0:T(8,128)(2,1)S(1)} custom-call(s32[4]{0:T(128)S(1)} %pad_add_fusion.place, f32[32,4096]{1,0:T(8,128)S(1)} %slice.9.g0, bf16[32,4096]{1,0:T(8,128)(2,1)S(1)} %collective-permute-done.12.g1, bf16[256,1024]{1,0:T(8,128)(2,1)S(1)} %bitcast.7, f32[1,1024]{1,0:T(1,128)S(1)} %bitcast.8, bf16[128,1024]{1,0:T(8,128)(2,1)S(1)} %copy-done.4, ...), custom_call_target="tpu_custom_call" | custom-call | flops 268435456 | bytes 1572864 | tf_op jit(solution)/shard_map/pallas_call | solution.py:260
  49.0 0.4 collective-permute-done.17.refs_9_
  49.4 3.3 %shard_map.96 = bf16[256,3072]{1,0:T(8,128)(2,1)} custom-call(s32[4]{0:T(128)S(1)} %pad_add_fusion.place, bf16[256,1024]{1,0:T(8,128)(2,1)S(1)} %shard_map.95.hid, bf16[1024,768]{1,0:T(8,128)(2,1)S(1)} %copy-done.1, bf16[1024,768]{1,0:T(8,128)(2,1)S(1)} %collective-permute-done.7.refs_1_, bf16[256,768]{1,0:T(8,128)(2,1)S(1)} %collective-permute-done.3.refs_2_, ...), custom_call_target="tpu_custom_call" | custom-call | flops 1610612736 | bytes 7864320 | tf_op jit(solution)/shard_map/pallas_call | solution.py:308
  (34 shorter events, 0.3 us)
Async XLA Ops:
  0.0 16.2 %copy-start.1 = (bf16[1024,768]{1,0:T(8,128)(2,1)S(1)}, bf16[1024,768]{1,0:T(8,128)(2,1)}, u32[]{:S(2)}) copy-start(bf16[1024,768]{1,0:T(8,128)(2,1)} %refs_0_.1) | copy-start | bytes 4718596
  1.1 15.2 %collective-permute-start.3 = (bf16[256,768]{1,0:T(8,128)(2,1)S(1)}, bf16[256,768]{1,0:T(8,128)(2,1)S(1)}, u32[]{:S(2)}, u32[]{:S(2)}) collective-permute-start(bf16[256,768]{1,0:T(8,128)(2,1)S(1)} %constant_dynamic-slice_fusion.1), channel_id=1, source_target_pairs={{0,2},{2,0},{1,3},{3,1},{4,6},{6,4},{5,7},{7,5},{8,10},{10,8},{9,1... | collective-permute-start | bytes 1179656 | tf_op jit(solution)/shard_map/ppermute | solution.py:324
  4.2 12.1 %collective-permute-start = (bf16[128,512]{1,0:T(8,128)(2,1)}, bf16[128,512]{1,0:T(8,128)(2,1)S(1)}, u32[]{:S(2)}, u32[]{:S(2)}) collective-permute-start(bf16[128,512]{1,0:T(8,128)(2,1)} %q.1), channel_id=1, source_target_pairs={{8,0},{12,4},{9,1},{13,5},{10,2},{14,6},{11,3},{15,7},{24,16},{28,... | collective-permute-start | bytes 393224 | tf_op jit(solution)/shard_map/ppermute | solution.py:343
  5.4 10.8 %collective-permute-start.1 = (bf16[128,512]{1,0:T(8,128)(2,1)}, bf16[128,512]{1,0:T(8,128)(2,1)S(1)}, u32[]{:S(2)}, u32[]{:S(2)}) collective-permute-start(bf16[128,512]{1,0:T(8,128)(2,1)} %k.1), channel_id=1, source_target_pairs={{0,4},{4,8},{8,12},{1,5},{5,9},{9,13},{2,6},{6,10},{10,14},{3,7},{... | collective-permute-start | bytes 393224 | tf_op jit(solution)/shard_map/ppermute | solution.py:344
  8.9 7.4 %collective-permute-start.2 = (bf16[128,512]{1,0:T(8,128)(2,1)}, bf16[128,512]{1,0:T(8,128)(2,1)S(1)}, u32[]{:S(2)}, u32[]{:S(2)}) collective-permute-start(bf16[128,512]{1,0:T(8,128)(2,1)} %v.1), channel_id=1, source_target_pairs={{0,4},{4,8},{8,12},{1,5},{5,9},{9,13},{2,6},{6,10},{10,14},{3,7},{... | collective-permute-start | bytes 393224 | tf_op jit(solution)/shard_map/ppermute | solution.py:345
  13.5 0.9 %copy-start.5 = (bf16[128,512]{1,0:T(8,128)(2,1)S(1)}, bf16[128,512]{1,0:T(8,128)(2,1)}, u32[]{:S(2)}) copy-start(bf16[128,512]{1,0:T(8,128)(2,1)} %q.1) | copy-start | bytes 393220
  14.4 0.9 %copy-start.6 = (bf16[128,512]{1,0:T(8,128)(2,1)S(1)}, bf16[128,512]{1,0:T(8,128)(2,1)}, u32[]{:S(2)}) copy-start(bf16[128,512]{1,0:T(8,128)(2,1)} %k.1) | copy-start | bytes 393220
  15.3 0.9 %copy-start.7 = (bf16[128,512]{1,0:T(8,128)(2,1)S(1)}, bf16[128,512]{1,0:T(8,128)(2,1)}, u32[]{:S(2)}) copy-start(bf16[128,512]{1,0:T(8,128)(2,1)} %v.1) | copy-start | bytes 393220
  16.3 13.3 %collective-permute-start.7 = (bf16[1024,768]{1,0:T(8,128)(2,1)S(1)}, bf16[1024,768]{1,0:T(8,128)(2,1)S(1)}, u32[]{:S(2)}, u32[]{:S(2)}) collective-permute-start(bf16[1024,768]{1,0:T(8,128)(2,1)S(1)} %copy-done.1), channel_id=1, source_target_pairs={{0,1},{1,0},{2,3},{3,2},{4,5},{5,4},{6,7},{7,6},{8,9},{9,8},{10,11... | collective-permute-start | bytes 4718600 | tf_op jit(solution)/shard_map/ppermute | solution.py:324
  16.4 13.3 %collective-permute-start.6 = (bf16[256,768]{1,0:T(8,128)(2,1)S(1)}, bf16[256,768]{1,0:T(8,128)(2,1)S(1)}, u32[]{:S(2)}, u32[]{:S(2)}) collective-permute-start(bf16[256,768]{1,0:T(8,128)(2,1)S(1)} %collective-permute-done.3.refs_2_), channel_id=1, source_target_pairs={{0,16},{16,0},{1,17},{17,1},{2,18},{18,2},{3,19},{19,3},{4,20},{20... | collective-permute-start | bytes 1179656 | tf_op jit(solution)/shard_map/ppermute | solution.py:324
  18.0 11.7 %collective-permute-start.5 = (bf16[256,768]{1,0:T(8,128)(2,1)S(1)}, bf16[256,768]{1,0:T(8,128)(2,1)S(1)}, u32[]{:S(2)}, u32[]{:S(2)}) collective-permute-start(bf16[256,768]{1,0:T(8,128)(2,1)S(1)} %constant_dynamic-slice_fusion), channel_id=1, source_target_pairs={{0,2},{2,0},{1,3},{3,1},{4,6},{6,4},{5,7},{7,5},{8,10},{10,8},{9,1... | collective-permute-start | bytes 1179656 | tf_op jit(solution)/shard_map/ppermute | solution.py:324
  20.0 9.7 %collective-permute-start.4 = (bf16[144,512]{1,0:T(8,128)(2,1)S(1)}, bf16[144,512]{1,0:T(8,128)(2,1)S(1)}, u32[]{:S(2)}, u32[]{:S(2)}) collective-permute-start(bf16[144,512]{1,0:T(8,128)(2,1)S(1)} %get-tuple-element.46), channel_id=1, source_target_pairs={{0,8},{4,12},{1,9},{5,13},{2,10},{6,14},{3,11},{7,15},{16,24},{20,... | collective-permute-start | bytes 442376 | tf_op jit(solution)/shard_map/ppermute | solution.py:353
  25.0 2.2 %copy-start = (bf16[512,4096]{1,0:T(8,128)(2,1)S(1)}, bf16[512,4096]{1,0:T(8,128)(2,1)}, u32[]{:S(2)}) copy-start(bf16[512,4096]{1,0:T(8,128)(2,1)} %source) | copy-start | bytes 12582916
  27.2 0.9 %copy-start.4 = (bf16[128,1024]{1,0:T(8,128)(2,1)S(1)}, bf16[128,1024]{1,0:T(8,128)(2,1)}, u32[]{:S(2)}) copy-start(bf16[128,1024]{1,0:T(8,128)(2,1)} %refs_0_) | copy-start | bytes 786436
  27.2 2.5 %copy-start.3 = (bf16[128,1024]{1,0:T(8,128)(2,1)S(1)}, bf16[128,1024]{1,0:T(8,128)(2,1)}, u32[]{:S(2)}) copy-start(bf16[128,1024]{1,0:T(8,128)(2,1)} %x.1) | copy-start | bytes 786436
  28.2 7.9 %collective-permute-start.10 = (bf16[128,1024]{1,0:T(8,128)(2,1)S(1)}, bf16[128,1024]{1,0:T(8,128)(2,1)S(1)}, u32[]{:S(2)}, u32[]{:S(2)}) collective-permute-start(bf16[128,1024]{1,0:T(8,128)(2,1)S(1)} %copy-done.4), channel_id=1, source_target_pairs={{0,2},{2,0},{1,3},{3,1},{4,6},{6,4},{5,7},{7,5},{8,10},{10,8},{9,1... | collective-permute-start | bytes 786440 | tf_op jit(solution)/shard_map/ppermute | solution.py:324
  31.5 6.1 %collective-permute-start.8 = (bf16[64,4096]{1,0:T(8,128)(2,1)S(1)}, bf16[64,4096]{1,0:T(8,128)(2,1)S(1)}, u32[]{:S(2)}, u32[]{:S(2)}) collective-permute-start(bf16[64,4096]{1,0:T(8,128)(2,1)S(1)} %get-tuple-element.54), channel_id=1, source_target_pairs={{0,1},{1,0},{2,3},{3,2},{4,5},{5,4},{6,7},{7,6},{8,9},{9,8},{10,11... | collective-permute-start | bytes 1572872 | tf_op jit(solution)/shard_map/ppermute | solution.py:324
  31.5 6.0 %collective-permute-start.9 = (bf16[256,768]{1,0:T(8,128)(2,1)S(1)}, bf16[256,768]{1,0:T(8,128)(2,1)S(1)}, u32[]{:S(2)}, u32[]{:S(2)}) collective-permute-start(bf16[256,768]{1,0:T(8,128)(2,1)S(1)} %collective-permute-done.6.refs_4_), channel_id=1, source_target_pairs={{0,1},{1,0},{2,3},{3,2},{4,5},{5,4},{6,7},{7,6},{8,9},{9,8},{10,11... | collective-permute-start | bytes 1179656 | tf_op jit(solution)/shard_map/ppermute | solution.py:324
  36.0 1.5 %collective-permute-start.11 = (bf16[128,1024]{1,0:T(8,128)(2,1)S(1)}, bf16[128,1024]{1,0:T(8,128)(2,1)S(1)}, u32[]{:S(2)}, u32[]{:S(2)}) collective-permute-start(bf16[128,1024]{1,0:T(8,128)(2,1)S(1)} %collective-permute-done.10.refs_2_), channel_id=1, source_target_pairs={{0,1},{1,0},{2,3},{3,2},{4,5},{5,4},{6,7},{7,6},{8,9},{9,8},{10,11... | collective-permute-start | bytes 786440 | tf_op jit(solution)/shard_map/ppermute | solution.py:324
  36.0 11.5 %collective-permute-start.13 = (bf16[256,768]{1,0:T(8,128)(2,1)S(1)}, bf16[256,768]{1,0:T(8,128)(2,1)S(1)}, u32[]{:S(2)}, u32[]{:S(2)}) collective-permute-start(bf16[256,768]{1,0:T(8,128)(2,1)S(1)} %collective-permute-done.5.refs_3_), channel_id=1, source_target_pairs={{0,16},{16,0},{1,17},{17,1},{2,18},{18,2},{3,19},{19,3},{4,20},{20... | collective-permute-start | bytes 1179656 | tf_op jit(solution)/shard_map/ppermute | solution.py:324
  37.6 10.0 %collective-permute-start.14 = (bf16[256,768]{1,0:T(8,128)(2,1)S(1)}, bf16[256,768]{1,0:T(8,128)(2,1)S(1)}, u32[]{:S(2)}, u32[]{:S(2)}) collective-permute-start(bf16[256,768]{1,0:T(8,128)(2,1)S(1)} %collective-permute-done.3.refs_2_), channel_id=1, source_target_pairs={{0,1},{1,0},{2,3},{3,2},{4,5},{5,4},{6,7},{7,6},{8,9},{9,8},{10,11... | collective-permute-start | bytes 1179656 | tf_op jit(solution)/shard_map/ppermute | solution.py:324
  37.7 9.9 %collective-permute-start.15 = (bf16[256,768]{1,0:T(8,128)(2,1)S(1)}, bf16[256,768]{1,0:T(8,128)(2,1)S(1)}, u32[]{:S(2)}, u32[]{:S(2)}) collective-permute-start(bf16[256,768]{1,0:T(8,128)(2,1)S(1)} %collective-permute-done.5.refs_3_), channel_id=1, source_target_pairs={{0,1},{1,0},{2,3},{3,2},{4,5},{5,4},{6,7},{7,6},{8,9},{9,8},{10,11... | collective-permute-start | bytes 1179656 | tf_op jit(solution)/shard_map/ppermute | solution.py:324
  38.1 9.6 %copy-start.2 = (bf16[32,8,1024]{2,1,0:T(8,128)(2,1)S(1)}, bf16[32,8,1024]{2,1,0:T(8,128)(2,1)}, u32[]{:S(2)}) copy-start(bf16[32,8,1024]{2,1,0:T(8,128)(2,1)} %param.15) | copy-start | bytes 1572868
  38.1 9.6 %copy-start.8 = (f32[1024]{0:T(1024)S(1)}, f32[1024]{0:T(1024)}, u32[]{:S(2)}) copy-start(f32[1024]{0:T(1024)} %param.16) | copy-start | bytes 12292
  38.2 9.3 %collective-permute-start.12 = (bf16[32,4096]{1,0:T(8,128)(2,1)S(1)}, bf16[32,4096]{1,0:T(8,128)(2,1)S(1)}, u32[]{:S(2)}, u32[]{:S(2)}) collective-permute-start(bf16[32,4096]{1,0:T(8,128)(2,1)S(1)} %slice.12), channel_id=1, source_target_pairs={{0,2},{2,0},{1,3},{3,1},{4,6},{6,4},{5,7},{7,5},{8,10},{10,8},{9,1... | collective-permute-start | bytes 786440 | tf_op jit(solution)/shard_map/ppermute | solution.py:324
  39.8 7.8 %collective-permute-start.16 = (bf16[128,1024]{1,0:T(8,128)(2,1)S(1)}, bf16[128,1024]{1,0:T(8,128)(2,1)S(1)}, u32[]{:S(2)}, u32[]{:S(2)}) collective-permute-start(bf16[128,1024]{1,0:T(8,128)(2,1)S(1)} %copy-done.4), channel_id=1, source_target_pairs={{0,1},{1,0},{2,3},{3,2},{4,5},{5,4},{6,7},{7,6},{8,9},{9,8},{10,11... | collective-permute-start | bytes 786440 | tf_op jit(solution)/shard_map/ppermute | solution.py:324
  47.6 1.8 %collective-permute-start.17 = (bf16[256,768]{1,0:T(8,128)(2,1)S(1)}, bf16[256,768]{1,0:T(8,128)(2,1)S(1)}, u32[]{:S(2)}, u32[]{:S(2)}) collective-permute-start(bf16[256,768]{1,0:T(8,128)(2,1)S(1)} %collective-permute-done.13.refs_5_), channel_id=1, source_target_pairs={{0,1},{1,0},{2,3},{3,2},{4,5},{5,4},{6,7},{7,6},{8,9},{9,8},{10,11... | collective-permute-start | bytes 1179656 | tf_op jit(solution)/shard_map/ppermute | solution.py:324

commit v5 on v4

--- a/solution.py
+++ b/solution.py
@@ -15,7 +15,6 @@
 GROUP = ("dp", "sub")
 SCALE = 1.0 / math.sqrt(HD)
 VMEM = pl.BlockSpec(memory_space=pltpu.VMEM)
-SMEM = pl.BlockSpec(memory_space=pltpu.SMEM)
 HBM = pl.BlockSpec(memory_space=pltpu.HBM)
 F32 = jnp.float32
 BF16 = jnp.bfloat16
@@ -64,10 +63,10 @@
     return result.reshape(byte_embed.shape[0], P_SIZE, 3 * DL)
 
 
-def attend_kernel(place, held, q_up, k_low, v_low, own, own_log, up):
+def attend_kernel(held, q_up, k_low, v_low, own, own_log, up):
     rows, width = q_up.shape
     heads = width // HD
-    has_low = place[0] >= 1
+    has_low = lax.axis_index("ctx") >= 1
     row = lax.broadcasted_iota(jnp.int32, (rows, 2 * rows), 0)
     col = lax.broadcasted_iota(jnp.int32, (rows, 2 * rows), 1)
     low = jnp.logical_and(col >= rows, has_low)
@@ -109,7 +108,7 @@
     up[pl.ds(rows, 16), pl.ds(0, HD)] = by_lane(terms).T[:16, :rows].astype(BF16)
 
 
-def attend(place, held, q_up, k_low, v_low):
+def attend(held, q_up, k_low, v_low):
     rows, width = q_up.shape
     return pl.pallas_call(
         attend_kernel,
@@ -118,7 +117,7 @@
             jax.ShapeDtypeStruct((rows, HD), F32),
             jax.ShapeDtypeStruct((rows + 16, width), BF16),
         ),
-        in_specs=[SMEM] + [VMEM] * 4,
+        in_specs=[VMEM] * 4,
         out_specs=(VMEM,) * 3,
         compiler_params=pltpu.CompilerParams(vmem_limit_bytes=6 * 2**20),
         cost_estimate=pl.CostEstimate(
@@ -126,7 +125,7 @@
             bytes_accessed=24 * rows * width,
             transcendentals=4 * rows * rows * width // HD,
         ),
-    )(place, held, q_up, k_low, v_low)
+    )(held, q_up, k_low, v_low)
 
 
 def copy_all(pairs, sems):
@@ -170,8 +169,8 @@
     )(x)
 
 
-def project_kernel(place, own, own_log, low, x, w, away, kept, attn, xs):
-    ctx, dp, sub = place[0], place[1], place[2]
+def project_kernel(own, own_log, low, x, w, away, kept, attn, xs):
+    ctx, dp, sub = lax.axis_index("ctx"), lax.axis_index("dp"), lax.axis_index("sub")
     rows, width = own.shape
     heads = width // HD
     quarter = rows // 4
@@ -207,7 +206,7 @@
         kept[:, cols] = terms[2 * quarter :]
 
 
-def project(place, own, own_log, low, x, w):
+def project(own, own_log, low, x, w):
     rows, width = own.shape
     half = rows // 2
     return pl.pallas_call(
@@ -216,7 +215,7 @@
             jax.ShapeDtypeStruct((half, w.shape[1]), BF16),
             jax.ShapeDtypeStruct((half, w.shape[1]), F32),
         ),
-        in_specs=[SMEM] + [VMEM] * 5,
+        in_specs=[VMEM] * 5,
         out_specs=(VMEM, VMEM),
         scratch_shapes=[pltpu.VMEM((rows, width), BF16), pltpu.VMEM(x.shape, BF16)],
         compiler_params=pltpu.CompilerParams(vmem_limit_bytes=12 * 2**20),
@@ -225,13 +224,34 @@
             bytes_accessed=2 * w.size + 6 * half * w.shape[1],
             transcendentals=3 * rows * width // HD,
         ),
-    )(place, own, own_log, low, x, w)
-
-
-def bytes_kernel(place, g0, g1, embed, gain, *refs):
+    )(own, own_log, low, x, w)
+
+
+def sum_kernel(kept, away, send, stay):
+    rows = send.shape[0]
+    summed = kept[...] + away[...].astype(F32)
+    send[...] = summed[:rows].astype(BF16)
+    stay[...] = summed[rows:]
+
+
+def sum_cores(kept, away):
+    rows, width = kept.shape[0] // 2, kept.shape[1]
+    return pl.pallas_call(
+        sum_kernel,
+        out_shape=(
+            jax.ShapeDtypeStruct((rows, width), BF16),
+            jax.ShapeDtypeStruct((rows, width), F32),
+        ),
+        in_specs=[VMEM] * 2,
+        out_specs=(VMEM,) * 2,
+        compiler_params=pltpu.CompilerParams(vmem_limit_bytes=2 * 2**20),
+    )(kept, away)
+
+
+def bytes_kernel(g0, g1, embed, gain, *refs):
     bridge = refs[:4]
-    hid, bw = refs[4:]
-    dp, sub = place[1], place[2]
+    hid, turned, bw = refs[4:]
+    dp, sub, grp = lax.axis_index("dp"), lax.axis_index("sub"), lax.axis_index("groups")
     patches = g0.shape[0]
     bytes_ = g0.shape[1] // DSLICE
     rows = patches * bytes_
@@ -248,49 +268,45 @@
     by_patch = dot(pick, stacked).astype(BF16)
     byte_in = embed[...].astype(F32) + dot(by_patch, bw[...])
     mean_square = jnp.mean(byte_in * byte_in, axis=1, keepdims=True)
-    hid[...] = (byte_in * lax.rsqrt(mean_square + 1e-05) * gain[...]).astype(BF16)
+    normalized = (byte_in * lax.rsqrt(mean_square + 1e-05) * gain[...]).astype(BF16)
+    hid[...] = normalized
+    half = normalized.shape[1] // 2
+    turned[:, pl.ds(pl.multiple_of(grp * half, half), half)] = normalized[:, :half]
+    turned[:, pl.ds(pl.multiple_of((1 - grp) * half, half), half)] = normalized[:, half:]
 
 
 def block_order(dp, sub):
     return [dp * 2 + sub, dp * 2 + 1 - sub, (1 - dp) * 2 + sub, (1 - dp) * 2 + 1 - sub]
 
 
-def bytes_in(place, g0, g1, embed, gain, bridge):
+def bytes_in(g0, g1, embed, gain, bridge):
     rows = embed.shape[0]
     return pl.pallas_call(
         bytes_kernel,
-        out_shape=jax.ShapeDtypeStruct((rows, DL), BF16),
-        in_specs=[SMEM] + [VMEM] * 8,
-        out_specs=VMEM,
+        out_shape=(jax.ShapeDtypeStruct((rows, DL), BF16),) * 2,
+        in_specs=[VMEM] * 8,
+        out_specs=(VMEM,) * 2,
         scratch_shapes=[pltpu.VMEM((DSLICE, DL), BF16)],
         compiler_params=pltpu.CompilerParams(vmem_limit_bytes=10 * 2**20),
         cost_estimate=pl.CostEstimate(
             flops=2 * rows * DL * DSLICE, bytes_accessed=6 * rows * DL, transcendentals=rows
         ),
-    )(place, g0, g1, embed, gain, *bridge)
-
-
-def local_kernel(place, hid, *refs, pieces):
-    whole = refs[:2]
-    parts = refs[2 : 2 + 4 * pieces]
-    out, held, sems = refs[2 + 4 * pieces :]
-    dp, sub, grp = place[1], place[2], place[3]
-    width = whole[0].shape[1]
-    copies = []
+    )(g0, g1, embed, gain, *bridge)
+
+
+def local_kernel(hid, turned, *refs, counts):
+    dp, sub = lax.axis_index("dp"), lax.axis_index("sub")
+    width = refs[0].shape[1]
+    out, held, sems = refs[sum(counts) :]
+    copies, at = [], 0
     for i, b in enumerate(block_order(dp, sub)):
-        if i < 2:
-            total = dot(hid[...], whole[i][...])
-        else:
-            total = None
-            for j in range(2):
-                first = (grp if j == 0 else 1 - grp) * (hid.shape[1] // 2)
-                for n in range(pieces):
-                    ref = parts[((i - 2) * 2 + j) * pieces + n]
-                    depth = ref.shape[0]
-                    lhs = hid[:, pl.ds(pl.multiple_of(first, 128), depth)]
-                    first += depth
-                    term = dot(lhs, ref[...])
-                    total = term if total is None else total + term
+        source = hid if counts[i] == 1 else turned
+        total, row = None, 0
+        for ref in refs[at : at + counts[i]]:
+            term = dot(source[:, row : row + ref.shape[0]], ref[...])
+            total = term if total is None else total + term
+            row += ref.shape[0]
+        at += counts[i]
         held[i, :, :] = total.astype(BF16)
         copy = pltpu.make_async_copy(
             held.at[i], out.at[:, pl.ds(pl.multiple_of(b * width, 128), width)], sems.at[i]
@@ -301,23 +317,18 @@
         copy.wait()
 
 
-def local(place, hid, whole, parts):
+def local(hid, turned, *blocks):
     rows = hid.shape[0]
-    block = whole[0].shape[1]
-    pieces = len(parts) // 4
-    return pl.pallas_call(
-        functools.partial(local_kernel, pieces=pieces),
-        out_shape=jax.ShapeDtypeStruct((rows, 4 * block), BF16),
-        in_specs=[SMEM] + [VMEM] * (3 + len(parts)),
+    weights = [piece for block in blocks for piece in block]
+    width = weights[0].shape[1]
+    return pl.pallas_call(
+        functools.partial(local_kernel, counts=tuple(len(block) for block in blocks)),
+        out_shape=jax.ShapeDtypeStruct((rows, 4 * width), BF16),
+        in_specs=[VMEM] * (2 + len(weights)),
         out_specs=pl.BlockSpec(memory_space=pl.ANY),
-        scratch_shapes=[pltpu.VMEM((4, rows, block), BF16), pltpu.SemaphoreType.DMA((4,))],
+        scratch_shapes=[pltpu.VMEM((4, rows, width), BF16), pltpu.SemaphoreType.DMA((4,))],
         compiler_params=pltpu.CompilerParams(vmem_limit_bytes=12 * 2**20),
-        cost_estimate=pl.CostEstimate(
-            flops=8 * rows * DL * block,
-            bytes_accessed=8 * DL * block + 8 * rows * block,
-            transcendentals=0,
-        ),
-    )(place, hid, *whole, *parts)
+    )(hid, turned, *weights)
 
 
 def swap(x, axis):
@@ -331,8 +342,7 @@
 def small_mesh(
     q_glob, k_glob, v_glob, x_glob, out_weight, bridge_weight, byte_embed, norm_gain, qkv_weight
 ):
-    ctx, dp, sub, grp = (lax.axis_index(a) for a in ("ctx", "dp", "sub", "groups"))
-    place = jnp.stack([ctx, dp, sub, grp]).astype(jnp.int32)
+    grp = lax.axis_index("groups")
 
     quarter = qkv_weight.shape[0] // 4
     held = hold(q_glob, k_glob, v_glob)
@@ -340,60 +350,60 @@
     w1 = lax.dynamic_slice_in_dim(after(qkv_weight, held), (grp * 2 + 1) * quarter, quarter, 0)
 
     x0 = swap(w0, "dp")
+    bridge_x = swap(bridge_weight, "dp")
     q_up = lax.ppermute(q_glob, "ctx", [(2, 0), (3, 1)])
     k_low = lax.ppermute(k_glob, "ctx", [(0, 1), (1, 2), (2, 3)])
     v_low = lax.ppermute(v_glob, "ctx", [(0, 1), (1, 2), (2, 3)])
-    q_up, k_low, v_low, x0, held, w1, bridge_weight, qkv_weight, place = (
+    q_up, k_low, v_low, x0, bridge_x, held, w1, bridge_weight, qkv_weight = (
         lax.optimization_barrier(
-            (q_up, k_low, v_low, x0, held, w1, bridge_weight, qkv_weight, place)
+            (q_up, k_low, v_low, x0, bridge_x, held, w1, bridge_weight, qkv_weight)
         )
     )
 
-    own, own_log, up = attend(place, held, q_up, k_low, v_low)
+    own, own_log, up = attend(held, q_up, k_low, v_low)
     low = lax.ppermute(up, "ctx", [(0, 2), (1, 3)])
     x1 = swap(w1, "dp")
     y0 = swap(x0, "groups")
     other_core = swap(qkv_weight, "sub")
+    core_x0 = swap(x0, "sub")
     out_weight = bring(after(out_weight, up), 4)
-    bridge_x = swap(bridge_weight, "dp")
-    low, x0, x1, y0, other_core, out_weight = lax.optimization_barrier(
-        (low, x0, x1, y0, other_core, out_weight)
-    )
-
-    away, kept = project(place, own, own_log, low, x_glob, out_weight)
+    low, core_x0, x1, other_core, out_weight, bridge_x = lax.optimization_barrier(
+        (low, core_x0, x1, other_core, out_weight, bridge_x)
+    )
+
+    away, kept = project(own, own_log, low, x_glob, out_weight)
     away = swap(away, "sub")
     y1 = swap(x1, "groups")
     bridge_both = swap(bridge_x, "sub")
     core_y0 = swap(y0, "sub")
-    away, core_y0, bridge_both, x0, x1, bridge_weight = lax.optimization_barrier(
-        (away, core_y0, bridge_both, x0, x1, bridge_weight)
-    )
-
-    summed = kept + away.astype(F32)
-    mid = summed.shape[0] // 2
-    across = swap(summed[:mid].astype(BF16), "dp")
+    away, core_y0, bridge_both, x1, bridge_weight = lax.optimization_barrier(
+        (away, core_y0, bridge_both, x1, bridge_weight)
+    )
+
+    send, stay = sum_cores(kept, away)
+    across = swap(send, "dp")
     core_x1 = swap(x1, "sub")
     bridge_core = swap(bridge_weight, "sub")
-    core_x0 = swap(x0, "sub")
-    across, y1, core_x0, core_x1, bridge_core = lax.optimization_barrier(
-        (across, y1, core_x0, core_x1, bridge_core)
+    across, y1, core_x1, bridge_core = lax.optimization_barrier(
+        (across, y1, core_x1, bridge_core)
     )
 
     core_y1 = swap(y1, "sub")
     rows = byte_embed.shape[0] * byte_embed.shape[1]
-    hidden = bytes_in(
-        place,
-        summed[mid:],
+    hidden, turned = bytes_in(
+        stay,
         across,
         byte_embed.reshape(rows, DL),
         norm_gain.reshape(1, DL),
         [bridge_weight, bridge_core, bridge_x, bridge_both],
     )
     result = local(
-        place,
         hidden,
-        [qkv_weight, other_core],
-        [x0, x1, y0, y1, core_x0, core_x1, core_y0, core_y1],
+        turned,
+        [qkv_weight],
+        [other_core],
+        [x0, x1, y0, y1],
+        [core_x0, core_x1, core_y0, core_y1],
     )
     return result.reshape(byte_embed.shape[0], P_SIZE, result.shape[1])
 

time: 53 us -> 51.7 us (0.975)
  the two profiles are of different devices: /device:TPU:0 before, /device:TPU:25 now
where the time goes in v5:
time: 51.7 us; the launch traced here: 51.4 us
  waiting for transfers between devices  24.4 us (47%)
  starting transfers between devices  14.7 us (28%)
  local copies, waits for them, and re-layouts  6.09 us (12%)
  Pallas kernels  6.06 us (12%)
    ppermute x14, waiting for transfers between devices, swap(): return lax.ppermute(x, axis, [(0, 1), (1, 0)])  12.5 us
    ppermute x14, starting transfers between devices, swap(): return lax.ppermute(x, axis, [(0, 1), (1, 0)])  8.88 us
    ppermute x1, waiting for transfers between devices, small_mesh(): low = lax.ppermute(up, 'ctx', [(0, 2), (1, 3)])  7.78 us
    unnamed x18, local copies, waits for them, and re-layouts  4.92 us
    ppermute x1, waiting for transfers between devices, small_mesh(): v_low = lax.ppermute(v_glob, 'ctx', [(0, 1), (1, 2), (2, 3)])  3.28 us
    pallas_call x1, Pallas kernels, local(): pl.pallas_call(functools.partial(local_kernel, counts=tuple((len(block) f...  2.77 us
    ppermute x1, starting transfers between devices, small_mesh(): q_up = lax.ppermute(q_glob, 'ctx', [(2, 0), (3, 1)])  1.96 us
    ppermute x1, starting transfers between devices, small_mesh(): k_low = lax.ppermute(k_glob, 'ctx', [(0, 1), (1, 2), (2, 3)])  1.29 us
  transfers between devices with their start and end apart: 18, of which 8 were waited for; matrix products, arithmetic and copies ran while one was open for 0% of the time, Pallas kernels for 6%

profile of v5, /device:TPU:25, one launch (start us, length us, event | category | flops | bytes accessed | tf_op | source)
XLA Modules:
  0.0 51.4 jit_solution(628780367759492196)
XLA Ops:
  0.0 1.1 %constant_dynamic-slice_fusion.1 = bf16[256,768]{1,0:T(8,128)(2,1)S(1)} fusion(bf16[1024,768]{1,0:T(8,128)(2,1)} %refs_0_.1, s32[]{:T(128)S(6)} %select_n.6), kind=kLoop, calls=%fused_computation.1 | loop fusion | bytes 786436 | tf_op jit(solution)/shard_map/dynamic_slice | solution.py:349
  1.1 1.3 %collective-permute-start.3 = (bf16[256,768]{1,0:T(8,128)(2,1)S(1)}, bf16[256,768]{1,0:T(8,128)(2,1)S(1)}, u32[]{:S(2)}, u32[]{:S(2)}) collective-permute-start(bf16[256,768]{1,0:T(8,128)(2,1)S(1)} %constant_dynamic-slice_fusion.1), channel_id=1, source_target_pairs={{0,2},{2,0},{1,3},{3,1},{4,6},{6,4},{5,7},{7,5},{8,10},{10,8},{9,1... | collective-permute-start | bytes 1179656 | tf_op jit(solution)/shard_map/ppermute | solution.py:335
  2.7 2.0 %collective-permute-start = (bf16[128,512]{1,0:T(8,128)(2,1)}, bf16[128,512]{1,0:T(8,128)(2,1)S(1)}, u32[]{:S(2)}, u32[]{:S(2)}) collective-permute-start(bf16[128,512]{1,0:T(8,128)(2,1)} %q.1), channel_id=1, source_target_pairs={{8,0},{12,4},{9,1},{13,5},{10,2},{14,6},{11,3},{15,7},{24,16},{28,... | collective-permute-start | bytes 393224 | tf_op jit(solution)/shard_map/ppermute | solution.py:354
  4.6 1.3 %collective-permute-start.1 = (bf16[128,512]{1,0:T(8,128)(2,1)}, bf16[128,512]{1,0:T(8,128)(2,1)S(1)}, u32[]{:S(2)}, u32[]{:S(2)}) collective-permute-start(bf16[128,512]{1,0:T(8,128)(2,1)} %k.1), channel_id=1, source_target_pairs={{0,4},{4,8},{8,12},{1,5},{5,9},{9,13},{2,6},{6,10},{10,14},{3,7},{... | collective-permute-start | bytes 393224 | tf_op jit(solution)/shard_map/ppermute | solution.py:355
  5.9 1.3 %collective-permute-start.2 = (bf16[128,512]{1,0:T(8,128)(2,1)}, bf16[128,512]{1,0:T(8,128)(2,1)S(1)}, u32[]{:S(2)}, u32[]{:S(2)}) collective-permute-start(bf16[128,512]{1,0:T(8,128)(2,1)} %v.1), channel_id=1, source_target_pairs={{0,4},{4,8},{8,12},{1,5},{5,9},{9,13},{2,6},{6,10},{10,14},{3,7},{... | collective-permute-start | bytes 393224 | tf_op jit(solution)/shard_map/ppermute | solution.py:356
  7.3 0.9 %copy-done.5 = bf16[128,512]{1,0:T(8,128)(2,1)S(1)} copy-done((bf16[128,512]{1,0:T(8,128)(2,1)S(1)}, bf16[128,512]{1,0:T(8,128)(2,1)}, u32[]{:S(2)}) %copy-start.5) | copy-done | bytes 131096
  8.2 0.9 %copy-done.6 = bf16[128,512]{1,0:T(8,128)(2,1)S(1)} copy-done((bf16[128,512]{1,0:T(8,128)(2,1)S(1)}, bf16[128,512]{1,0:T(8,128)(2,1)}, u32[]{:S(2)}) %copy-start.6) | copy-done | bytes 131096
  9.1 0.9 %copy-done.7 = bf16[128,512]{1,0:T(8,128)(2,1)S(1)} copy-done((bf16[128,512]{1,0:T(8,128)(2,1)S(1)}, bf16[128,512]{1,0:T(8,128)(2,1)}, u32[]{:S(2)}) %copy-start.7) | copy-done | bytes 131096
  10.1 0.8 %collective-permute-done.1.k_low = bf16[128,512]{1,0:T(8,128)(2,1)S(1)} collective-permute-done((bf16[128,512]{1,0:T(8,128)(2,1)}, bf16[128,512]{1,0:T(8,128)(2,1)S(1)}, u32[]{:S(2)}, u32[]{:S(2)}) %collective-permute-start.1) | collective-permute-done | bytes 131104 | tf_op jit(solution)/shard_map/ppermute | solution.py:355
  10.9 3.3 %collective-permute-done.2.v_low = bf16[128,512]{1,0:T(8,128)(2,1)S(1)} collective-permute-done((bf16[128,512]{1,0:T(8,128)(2,1)}, bf16[128,512]{1,0:T(8,128)(2,1)S(1)}, u32[]{:S(2)}, u32[]{:S(2)}) %collective-permute-start.2) | collective-permute-done | bytes 131104 | tf_op jit(solution)/shard_map/ppermute | solution.py:356
  14.1 2.7 %collective-permute-done.4.refs_2_ = bf16[128,1024]{1,0:T(8,128)(2,1)S(1)} collective-permute-done((bf16[128,1024]{1,0:T(8,128)(2,1)}, bf16[128,1024]{1,0:T(8,128)(2,1)S(1)}, u32[]{:S(2)}, u32[]{:S(2)}) %collective-permute-start.4) | collective-permute-done | bytes 262176 | tf_op jit(solution)/shard_map/ppermute | solution.py:335
  16.8 1.5 %collective-permute-start.8 = (bf16[1024,768]{1,0:T(8,128)(2,1)S(1)}, bf16[1024,768]{1,0:T(8,128)(2,1)S(1)}, u32[]{:S(2)}, u32[]{:S(2)}) collective-permute-start(bf16[1024,768]{1,0:T(8,128)(2,1)S(1)} %copy-done.1), channel_id=1, source_target_pairs={{0,1},{1,0},{2,3},{3,2},{4,5},{5,4},{6,7},{7,6},{8,9},{9,8},{10,11... | collective-permute-start | bytes 4718600 | tf_op jit(solution)/shard_map/ppermute | solution.py:335
  18.4 1.2 %collective-permute-start.7 = (bf16[256,768]{1,0:T(8,128)(2,1)S(1)}, bf16[256,768]{1,0:T(8,128)(2,1)S(1)}, u32[]{:S(2)}, u32[]{:S(2)}) collective-permute-start(bf16[256,768]{1,0:T(8,128)(2,1)S(1)} %constant_dynamic-slice_fusion), channel_id=1, source_target_pairs={{0,2},{2,0},{1,3},{3,1},{4,6},{6,4},{5,7},{7,5},{8,10},{10,8},{9,1... | collective-permute-start | bytes 1179656 | tf_op jit(solution)/shard_map/ppermute | solution.py:335
  19.6 1.2 %collective-permute-start.10 = (bf16[256,768]{1,0:T(8,128)(2,1)S(1)}, bf16[256,768]{1,0:T(8,128)(2,1)S(1)}, u32[]{:S(2)}, u32[]{:S(2)}) collective-permute-start(bf16[256,768]{1,0:T(8,128)(2,1)S(1)} %collective-permute-done.3.refs_2_), channel_id=1, source_target_pairs={{0,16},{16,0},{1,17},{17,1},{2,18},{18,2},{3,19},{19,3},{4,20},{20... | collective-permute-start | bytes 1179656 | tf_op jit(solution)/shard_map/ppermute | solution.py:335
  20.8 0.9 %shard_map.92 = (f32[128,512]{1,0:T(8,128)S(1)}, f32[128,128]{1,0:T(8,128)S(1)}, bf16[144,512]{1,0:T(8,128)(2,1)S(1)}) custom-call(bf16[128,1536]{1,0:T(8,128)(2,1)S(1)} %shard_map.91.held, bf16[128,512]{1,0:T(8,128)(2,1)S(1)} %collective-permute-done.q_up, bf16[128,512]{1,0:T(8,128)(2,1)S(1)} %collective-permute-done.1.k_low, ...), custom_call_target="tpu_custom_call" | custom-call | flops 134217728 | bytes 1572864 | tf_op jit(solution)/shard_map/pallas_call | solution.py:113
  21.8 1.3 %collective-permute-start.5 = (bf16[144,512]{1,0:T(8,128)(2,1)S(1)}, bf16[144,512]{1,0:T(8,128)(2,1)S(1)}, u32[]{:S(2)}, u32[]{:S(2)}) collective-permute-start(bf16[144,512]{1,0:T(8,128)(2,1)S(1)} %get-tuple-element.47), channel_id=1, source_target_pairs={{0,8},{4,12},{1,9},{5,13},{2,10},{6,14},{3,11},{7,15},{16,24},{20,... | collective-permute-start | bytes 442376 | tf_op jit(solution)/shard_map/ppermute | solution.py:364
  23.1 2.2 %copy-done = bf16[512,4096]{1,0:T(8,128)(2,1)S(1)} copy-done((bf16[512,4096]{1,0:T(8,128)(2,1)S(1)}, bf16[512,4096]{1,0:T(8,128)(2,1)}, u32[]{:S(2)}) %copy-start) | copy-done | bytes 4194328
  25.2 0.3 shard_map.93.w
  25.6 7.8 %collective-permute-done.5.low = bf16[144,512]{1,0:T(8,128)(2,1)S(1)} collective-permute-done((bf16[144,512]{1,0:T(8,128)(2,1)S(1)}, bf16[144,512]{1,0:T(8,128)(2,1)S(1)}, u32[]{:S(2)}, u32[]{:S(2)}) %collective-permute-start.5) | collective-permute-done | bytes 147488 | tf_op jit(solution)/shard_map/ppermute | solution.py:364
  33.4 1.1 %shard_map.94 = (bf16[64,4096]{1,0:T(8,128)(2,1)S(1)}, f32[64,4096]{1,0:T(8,128)S(1)}) custom-call(f32[128,512]{1,0:T(8,128)S(1)} %get-tuple-element.45.own, f32[128,128]{1,0:T(8,128)S(1)} %get-tuple-element.46.own_log, bf16[144,512]{1,0:T(8,128)(2,1)S(1)} %collective-permute-done.5.low, bf16[128,1024]{1,0:T(8,128)(2,1)S(1)} %copy-done.3, ...), custom_call_target="tpu_custom_call" | custom-call | flops 536870912 | bytes 5767168 | tf_op jit(solution)/shard_map/pallas_call | solution.py:212
  34.6 0.6 %collective-permute-start.9 = (bf16[64,4096]{1,0:T(8,128)(2,1)S(1)}, bf16[64,4096]{1,0:T(8,128)(2,1)S(1)}, u32[]{:S(2)}, u32[]{:S(2)}) collective-permute-start(bf16[64,4096]{1,0:T(8,128)(2,1)S(1)} %get-tuple-element.56), channel_id=1, source_target_pairs={{0,1},{1,0},{2,3},{3,2},{4,5},{5,4},{6,7},{7,6},{8,9},{9,8},{10,11... | collective-permute-start | bytes 1572872 | tf_op jit(solution)/shard_map/ppermute | solution.py:335
  35.2 0.4 collective-permute-start.12
  35.9 1.3 %collective-permute-done.11.refs_8_ = bf16[256,768]{1,0:T(8,128)(2,1)S(1)} collective-permute-done((bf16[256,768]{1,0:T(8,128)(2,1)S(1)}, bf16[256,768]{1,0:T(8,128)(2,1)S(1)}, u32[]{:S(2)}, u32[]{:S(2)}) %collective-permute-start.11) | collective-permute-done | bytes 393248 | tf_op jit(solution)/shard_map/ppermute | solution.py:335
  37.2 0.4 collective-permute-done.12.refs_3_
  37.6 0.4 collective-permute-start.15
  38.1 0.3 collective-permute-start.13
  38.4 0.4 collective-permute-start.16
  38.8 7.5 %collective-permute-done.14.refs_5_ = bf16[256,768]{1,0:T(8,128)(2,1)S(1)} collective-permute-done((bf16[256,768]{1,0:T(8,128)(2,1)S(1)}, bf16[256,768]{1,0:T(8,128)(2,1)S(1)}, u32[]{:S(2)}, u32[]{:S(2)}) %collective-permute-start.14) | collective-permute-done | bytes 393248 | tf_op jit(solution)/shard_map/ppermute | solution.py:335
  46.3 0.9 %collective-permute-start.17 = (bf16[256,768]{1,0:T(8,128)(2,1)S(1)}, bf16[256,768]{1,0:T(8,128)(2,1)S(1)}, u32[]{:S(2)}, u32[]{:S(2)}) collective-permute-start(bf16[256,768]{1,0:T(8,128)(2,1)S(1)} %collective-permute-done.14.refs_5_), channel_id=1, source_target_pairs={{0,1},{1,0},{2,3},{3,2},{4,5},{5,4},{6,7},{7,6},{8,9},{9,8},{10,11... | collective-permute-start | bytes 1179656 | tf_op jit(solution)/shard_map/ppermute | solution.py:335
  47.3 0.8 %shard_map.96 = (bf16[256,1024]{1,0:T(8,128)(2,1)S(1)}, bf16[256,1024]{1,0:T(8,128)(2,1)S(1)}) custom-call(f32[32,4096]{1,0:T(8,128)S(1)} %get-tuple-element.61.g0, bf16[32,4096]{1,0:T(8,128)(2,1)S(1)} %collective-permute-done.13.g1, bf16[256,1024]{1,0:T(8,128)(2,1)S(1)} %bitcast.3, f32[1,1024]{1,0:T(1,128)S(1)} %bitcast.4, bf16[128,1024]{1,0:T(8,128)(2,1)S(1)} %copy-done.4, ...), custom_call_target="tpu_custom_call" | custom-call | flops 268435456 | bytes 1572864 | tf_op jit(solution)/shard_map/pallas_call | solution.py:284
  48.1 0.6 %collective-permute-done.17.refs_9_ = bf16[256,768]{1,0:T(8,128)(2,1)S(1)} collective-permute-done((bf16[256,768]{1,0:T(8,128)(2,1)S(1)}, bf16[256,768]{1,0:T(8,128)(2,1)S(1)}, u32[]{:S(2)}, u32[]{:S(2)}) %collective-permute-start.17) | collective-permute-done | bytes 393248 | tf_op jit(solution)/shard_map/ppermute | solution.py:335
  48.6 2.8 %shard_map.97 = bf16[256,3072]{1,0:T(8,128)(2,1)} custom-call(bf16[256,1024]{1,0:T(8,128)(2,1)S(1)} %get-tuple-element.68.hid, bf16[256,1024]{1,0:T(8,128)(2,1)S(1)} %get-tuple-element.69.turned, bf16[1024,768]{1,0:T(8,128)(2,1)S(1)} %copy-done.1, bf16[1024,768]{1,0:T(8,128)(2,1)S(1)} %collective-permute-done.8.refs_1_, ...), custom_call_target="tpu_custom_call" | custom-call | tf_op jit(solution)/shard_map/pallas_call | solution.py:324
  (31 shorter events, 0.8 us)
Async XLA Ops:
  0.0 10.0 %copy-start.1 = (bf16[1024,768]{1,0:T(8,128)(2,1)S(1)}, bf16[1024,768]{1,0:T(8,128)(2,1)}, u32[]{:S(2)}) copy-start(bf16[1024,768]{1,0:T(8,128)(2,1)} %refs_0_.1) | copy-start | bytes 4718596
  1.1 15.7 %collective-permute-start.3 = (bf16[256,768]{1,0:T(8,128)(2,1)S(1)}, bf16[256,768]{1,0:T(8,128)(2,1)S(1)}, u32[]{:S(2)}, u32[]{:S(2)}) collective-permute-start(bf16[256,768]{1,0:T(8,128)(2,1)S(1)} %constant_dynamic-slice_fusion.1), channel_id=1, source_target_pairs={{0,2},{2,0},{1,3},{3,1},{4,6},{6,4},{5,7},{7,5},{8,10},{10,8},{9,1... | collective-permute-start | bytes 1179656 | tf_op jit(solution)/shard_map/ppermute | solution.py:335
  2.4 14.4 %collective-permute-start.4 = (bf16[128,1024]{1,0:T(8,128)(2,1)}, bf16[128,1024]{1,0:T(8,128)(2,1)S(1)}, u32[]{:S(2)}, u32[]{:S(2)}) collective-permute-start(bf16[128,1024]{1,0:T(8,128)(2,1)} %refs_0_), channel_id=1, source_target_pairs={{0,2},{2,0},{1,3},{3,1},{4,6},{6,4},{5,7},{7,5},{8,10},{10,8},{9,1... | collective-permute-start | bytes 786440 | tf_op jit(solution)/shard_map/ppermute | solution.py:335
  2.7 7.4 %collective-permute-start = (bf16[128,512]{1,0:T(8,128)(2,1)}, bf16[128,512]{1,0:T(8,128)(2,1)S(1)}, u32[]{:S(2)}, u32[]{:S(2)}) collective-permute-start(bf16[128,512]{1,0:T(8,128)(2,1)} %q.1), channel_id=1, source_target_pairs={{8,0},{12,4},{9,1},{13,5},{10,2},{14,6},{11,3},{15,7},{24,16},{28,... | collective-permute-start | bytes 393224 | tf_op jit(solution)/shard_map/ppermute | solution.py:354
  4.6 6.2 %collective-permute-start.1 = (bf16[128,512]{1,0:T(8,128)(2,1)}, bf16[128,512]{1,0:T(8,128)(2,1)S(1)}, u32[]{:S(2)}, u32[]{:S(2)}) collective-permute-start(bf16[128,512]{1,0:T(8,128)(2,1)} %k.1), channel_id=1, source_target_pairs={{0,4},{4,8},{8,12},{1,5},{5,9},{9,13},{2,6},{6,10},{10,14},{3,7},{... | collective-permute-start | bytes 393224 | tf_op jit(solution)/shard_map/ppermute | solution.py:355
  5.9 8.2 %collective-permute-start.2 = (bf16[128,512]{1,0:T(8,128)(2,1)}, bf16[128,512]{1,0:T(8,128)(2,1)S(1)}, u32[]{:S(2)}, u32[]{:S(2)}) collective-permute-start(bf16[128,512]{1,0:T(8,128)(2,1)} %v.1), channel_id=1, source_target_pairs={{0,4},{4,8},{8,12},{1,5},{5,9},{9,13},{2,6},{6,10},{10,14},{3,7},{... | collective-permute-start | bytes 393224 | tf_op jit(solution)/shard_map/ppermute | solution.py:356
  7.2 0.9 %copy-start.5 = (bf16[128,512]{1,0:T(8,128)(2,1)S(1)}, bf16[128,512]{1,0:T(8,128)(2,1)}, u32[]{:S(2)}) copy-start(bf16[128,512]{1,0:T(8,128)(2,1)} %q.1) | copy-start | bytes 393220
  8.2 0.9 %copy-start.6 = (bf16[128,512]{1,0:T(8,128)(2,1)S(1)}, bf16[128,512]{1,0:T(8,128)(2,1)}, u32[]{:S(2)}) copy-start(bf16[128,512]{1,0:T(8,128)(2,1)} %k.1) | copy-start | bytes 393220
  9.1 0.9 %copy-start.7 = (bf16[128,512]{1,0:T(8,128)(2,1)S(1)}, bf16[128,512]{1,0:T(8,128)(2,1)}, u32[]{:S(2)}) copy-start(bf16[128,512]{1,0:T(8,128)(2,1)} %v.1) | copy-start | bytes 393220
  16.8 16.6 %collective-permute-start.8 = (bf16[1024,768]{1,0:T(8,128)(2,1)S(1)}, bf16[1024,768]{1,0:T(8,128)(2,1)S(1)}, u32[]{:S(2)}, u32[]{:S(2)}) collective-permute-start(bf16[1024,768]{1,0:T(8,128)(2,1)S(1)} %copy-done.1), channel_id=1, source_target_pairs={{0,1},{1,0},{2,3},{3,2},{4,5},{5,4},{6,7},{7,6},{8,9},{9,8},{10,11... | collective-permute-start | bytes 4718600 | tf_op jit(solution)/shard_map/ppermute | solution.py:335
  18.4 15.0 %collective-permute-start.6 = (bf16[256,768]{1,0:T(8,128)(2,1)S(1)}, bf16[256,768]{1,0:T(8,128)(2,1)S(1)}, u32[]{:S(2)}, u32[]{:S(2)}) collective-permute-start(bf16[256,768]{1,0:T(8,128)(2,1)S(1)} %collective-permute-done.3.refs_2_), channel_id=1, source_target_pairs={{0,1},{1,0},{2,3},{3,2},{4,5},{5,4},{6,7},{7,6},{8,9},{9,8},{10,11... | collective-permute-start | bytes 1179656 | tf_op jit(solution)/shard_map/ppermute | solution.py:335
  18.4 15.0 %collective-permute-start.7 = (bf16[256,768]{1,0:T(8,128)(2,1)S(1)}, bf16[256,768]{1,0:T(8,128)(2,1)S(1)}, u32[]{:S(2)}, u32[]{:S(2)}) collective-permute-start(bf16[256,768]{1,0:T(8,128)(2,1)S(1)} %constant_dynamic-slice_fusion), channel_id=1, source_target_pairs={{0,2},{2,0},{1,3},{3,1},{4,6},{6,4},{5,7},{7,5},{8,10},{10,8},{9,1... | collective-permute-start | bytes 1179656 | tf_op jit(solution)/shard_map/ppermute | solution.py:335
  19.6 15.6 %collective-permute-start.10 = (bf16[256,768]{1,0:T(8,128)(2,1)S(1)}, bf16[256,768]{1,0:T(8,128)(2,1)S(1)}, u32[]{:S(2)}, u32[]{:S(2)}) collective-permute-start(bf16[256,768]{1,0:T(8,128)(2,1)S(1)} %collective-permute-done.3.refs_2_), channel_id=1, source_target_pairs={{0,16},{16,0},{1,17},{17,1},{2,18},{18,2},{3,19},{19,3},{4,20},{20... | collective-permute-start | bytes 1179656 | tf_op jit(solution)/shard_map/ppermute | solution.py:335
  21.8 11.6 %collective-permute-start.5 = (bf16[144,512]{1,0:T(8,128)(2,1)S(1)}, bf16[144,512]{1,0:T(8,128)(2,1)S(1)}, u32[]{:S(2)}, u32[]{:S(2)}) collective-permute-start(bf16[144,512]{1,0:T(8,128)(2,1)S(1)} %get-tuple-element.47), channel_id=1, source_target_pairs={{0,8},{4,12},{1,9},{5,13},{2,10},{6,14},{3,11},{7,15},{16,24},{20,... | collective-permute-start | bytes 442376 | tf_op jit(solution)/shard_map/ppermute | solution.py:364
  23.1 2.2 %copy-start = (bf16[512,4096]{1,0:T(8,128)(2,1)S(1)}, bf16[512,4096]{1,0:T(8,128)(2,1)}, u32[]{:S(2)}) copy-start(bf16[512,4096]{1,0:T(8,128)(2,1)} %source) | copy-start | bytes 12582916
  25.2 8.1 %copy-start.3 = (bf16[128,1024]{1,0:T(8,128)(2,1)S(1)}, bf16[128,1024]{1,0:T(8,128)(2,1)}, u32[]{:S(2)}) copy-start(bf16[128,1024]{1,0:T(8,128)(2,1)} %x.1) | copy-start | bytes 786436
  34.5 3.8 %copy-start.4 = (bf16[128,1024]{1,0:T(8,128)(2,1)S(1)}, bf16[128,1024]{1,0:T(8,128)(2,1)}, u32[]{:S(2)}) copy-start(bf16[128,1024]{1,0:T(8,128)(2,1)} %refs_0_) | copy-start | bytes 786436
  34.5 12.7 %copy-start.2 = (bf16[32,8,1024]{2,1,0:T(8,128)(2,1)S(1)}, bf16[32,8,1024]{2,1,0:T(8,128)(2,1)}, u32[]{:S(2)}) copy-start(bf16[32,8,1024]{2,1,0:T(8,128)(2,1)} %param.15) | copy-start | bytes 1572868
  34.6 12.7 %copy-start.8 = (f32[1024]{0:T(1024)S(1)}, f32[1024]{0:T(1024)}, u32[]{:S(2)}) copy-start(f32[1024]{0:T(1024)} %param.16) | copy-start | bytes 12292
  34.6 3.0 %collective-permute-start.9 = (bf16[64,4096]{1,0:T(8,128)(2,1)S(1)}, bf16[64,4096]{1,0:T(8,128)(2,1)S(1)}, u32[]{:S(2)}, u32[]{:S(2)}) collective-permute-start(bf16[64,4096]{1,0:T(8,128)(2,1)S(1)} %get-tuple-element.56), channel_id=1, source_target_pairs={{0,1},{1,0},{2,3},{3,2},{4,5},{5,4},{6,7},{7,6},{8,9},{9,8},{10,11... | collective-permute-start | bytes 1572872 | tf_op jit(solution)/shard_map/ppermute | solution.py:335
  35.1 2.1 %collective-permute-start.11 = (bf16[256,768]{1,0:T(8,128)(2,1)S(1)}, bf16[256,768]{1,0:T(8,128)(2,1)S(1)}, u32[]{:S(2)}, u32[]{:S(2)}) collective-permute-start(bf16[256,768]{1,0:T(8,128)(2,1)S(1)} %collective-permute-done.10.refs_4_), channel_id=1, source_target_pairs={{0,1},{1,0},{2,3},{3,2},{4,5},{5,4},{6,7},{7,6},{8,9},{9,8},{10,11... | collective-permute-start | bytes 1179656 | tf_op jit(solution)/shard_map/ppermute | solution.py:335
  35.2 2.4 %collective-permute-start.12 = (bf16[128,1024]{1,0:T(8,128)(2,1)S(1)}, bf16[128,1024]{1,0:T(8,128)(2,1)S(1)}, u32[]{:S(2)}, u32[]{:S(2)}) collective-permute-start(bf16[128,1024]{1,0:T(8,128)(2,1)S(1)} %collective-permute-done.4.refs_2_), channel_id=1, source_target_pairs={{0,1},{1,0},{2,3},{3,2},{4,5},{5,4},{6,7},{7,6},{8,9},{9,8},{10,11... | collective-permute-start | bytes 786440 | tf_op jit(solution)/shard_map/ppermute | solution.py:335
  35.7 10.7 %collective-permute-start.14 = (bf16[256,768]{1,0:T(8,128)(2,1)S(1)}, bf16[256,768]{1,0:T(8,128)(2,1)S(1)}, u32[]{:S(2)}, u32[]{:S(2)}) collective-permute-start(bf16[256,768]{1,0:T(8,128)(2,1)S(1)} %collective-permute-done.7.refs_3_), channel_id=1, source_target_pairs={{0,16},{16,0},{1,17},{17,1},{2,18},{18,2},{3,19},{19,3},{4,20},{20... | collective-permute-start | bytes 1179656 | tf_op jit(solution)/shard_map/ppermute | solution.py:335
  37.6 8.7 %collective-permute-start.15 = (bf16[256,768]{1,0:T(8,128)(2,1)S(1)}, bf16[256,768]{1,0:T(8,128)(2,1)S(1)}, u32[]{:S(2)}, u32[]{:S(2)}) collective-permute-start(bf16[256,768]{1,0:T(8,128)(2,1)S(1)} %collective-permute-done.7.refs_3_), channel_id=1, source_target_pairs={{0,1},{1,0},{2,3},{3,2},{4,5},{5,4},{6,7},{7,6},{8,9},{9,8},{10,11... | collective-permute-start | bytes 1179656 | tf_op jit(solution)/shard_map/ppermute | solution.py:335
  38.1 8.3 %collective-permute-start.13 = (bf16[32,4096]{1,0:T(8,128)(2,1)S(1)}, bf16[32,4096]{1,0:T(8,128)(2,1)S(1)}, u32[]{:S(2)}, u32[]{:S(2)}) collective-permute-start(bf16[32,4096]{1,0:T(8,128)(2,1)S(1)} %get-tuple-element.62), channel_id=1, source_target_pairs={{0,2},{2,0},{1,3},{3,1},{4,6},{6,4},{5,7},{7,5},{8,10},{10,8},{9,1... | collective-permute-start | bytes 786440 | tf_op jit(solution)/shard_map/ppermute | solution.py:335
  38.4 8.0 %collective-permute-start.16 = (bf16[128,1024]{1,0:T(8,128)(2,1)S(1)}, bf16[128,1024]{1,0:T(8,128)(2,1)S(1)}, u32[]{:S(2)}, u32[]{:S(2)}) collective-permute-start(bf16[128,1024]{1,0:T(8,128)(2,1)S(1)} %copy-done.4), channel_id=1, source_target_pairs={{0,1},{1,0},{2,3},{3,2},{4,5},{5,4},{6,7},{7,6},{8,9},{9,8},{10,11... | collective-permute-start | bytes 786440 | tf_op jit(solution)/shard_map/ppermute | solution.py:335
  46.3 2.3 %collective-permute-start.17 = (bf16[256,768]{1,0:T(8,128)(2,1)S(1)}, bf16[256,768]{1,0:T(8,128)(2,1)S(1)}, u32[]{:S(2)}, u32[]{:S(2)}) collective-permute-start(bf16[256,768]{1,0:T(8,128)(2,1)S(1)} %collective-permute-done.14.refs_5_), channel_id=1, source_target_pairs={{0,1},{1,0},{2,3},{3,2},{4,5},{5,4},{6,7},{7,6},{8,9},{9,8},{10,11... | collective-permute-start | bytes 1179656 | tf_op jit(solution)/shard_map/ppermute | solution.py:335

commit v6 on v5

--- a/solution.py
+++ b/solution.py
@@ -63,43 +63,54 @@
     return result.reshape(byte_embed.shape[0], P_SIZE, 3 * DL)
 
 
-def attend_kernel(held, q_up, k_low, v_low, own, own_log, up):
-    rows, width = q_up.shape
-    heads = width // HD
-    has_low = lax.axis_index("ctx") >= 1
+def attend_block(queries, held, k_low, v_low, h, mask, target):
+    rows = queries.shape[0]
+    width = k_low.shape[1]
+    cols = pl.ds(h * HD, HD)
+    k, v = (held[:, pl.ds(i * width + h * HD, HD)] for i in (1, 2))
+    kh = jnp.concatenate([k, k_low[:, cols]], axis=0)
+    vh = jnp.concatenate([v, v_low[:, cols]], axis=0)
+    scores = lax.dot_general(
+        queries[:, cols], kh, (((1,), (1,)), ((), ())), preferred_element_type=F32
+    ) * SCALE
+    scores = jnp.where(mask, scores, -jnp.inf)
+    top = jnp.max(scores, axis=1, keepdims=True)
+    probs = jnp.exp(scores - top)
+    total = jnp.sum(probs, axis=1, keepdims=True)
+    mixed = dot(probs.astype(BF16), vh) / total
+    target[pl.ds(0, rows), cols] = mixed.astype(target.dtype)
+    return top + jnp.log(total)
+
+
+def masks(rows):
     row = lax.broadcasted_iota(jnp.int32, (rows, 2 * rows), 0)
     col = lax.broadcasted_iota(jnp.int32, (rows, 2 * rows), 1)
-    low = jnp.logical_and(col >= rows, has_low)
-    full = jnp.logical_or(col < rows, low)
-    causal = jnp.logical_or(row >= col, low)
-    logs = [[], []]
-    for h in range(heads):
-        cols = pl.ds(h * HD, HD)
-        qh, k, v = (held[:, pl.ds(i * width + h * HD, HD)] for i in range(3))
-        kh = jnp.concatenate([k, k_low[:, cols]], axis=0)
-        vh = jnp.concatenate([v, v_low[:, cols]], axis=0)
-        for i, (queries, mask, target) in enumerate(((qh, causal, own), (q_up[:, cols], full, up))):
-            scores = lax.dot_general(
-                queries, kh, (((1,), (1,)), ((), ())), preferred_element_type=F32
-            ) * SCALE
-            scores = jnp.where(mask, scores, -jnp.inf)
-            top = jnp.max(scores, axis=1, keepdims=True)
-            probs = jnp.exp(scores - top)
-            total = jnp.sum(probs, axis=1, keepdims=True)
-            mixed = dot(probs.astype(BF16), vh) / total
-            target[pl.ds(0, rows), cols] = mixed.astype(target.dtype)
-            logs[i].append(top + jnp.log(total))
+    low = jnp.logical_and(col >= rows, lax.axis_index("ctx") >= 1)
+    return col < rows, low, row >= col
+
+
+def by_lane(columns):
+    rows = columns[0].shape[0]
     lane = lax.broadcasted_iota(jnp.int32, (rows, HD), 1)
-
-    def by_lane(columns):
-        table = jnp.zeros((rows, HD), F32)
-        for i, column in enumerate(columns):
-            table = jnp.where(lane == i, column, table)
-        return table
-
-    own_log[...] = by_lane(logs[0])
+    table = jnp.zeros((rows, HD), F32)
+    for i, column in enumerate(columns):
+        table = jnp.where(lane == i, column, table)
+    return table
+
+
+def attend_own_kernel(held, k_low, v_low, own, own_log):
+    _, low, causal = masks(own.shape[0])
+    mask = jnp.logical_or(causal, low)
+    heads = range(own.shape[1] // HD)
+    own_log[...] = by_lane([attend_block(held, held, k_low, v_low, h, mask, own) for h in heads])
+
+
+def attend_up_kernel(held, q_up, k_low, v_low, up):
+    rows, width = q_up.shape
+    here, low, _ = masks(rows)
+    mask = jnp.logical_or(here, low)
+    rest = [attend_block(q_up, held, k_low, v_low, h, mask, up) for h in range(width // HD)]
     terms = []
-    rest = logs[1]
     for _ in range(3):
         high = [r.astype(BF16).astype(F32) for r in rest]
         rest = [r - t for r, t in zip(rest, high)]
@@ -108,23 +119,28 @@
     up[pl.ds(rows, 16), pl.ds(0, HD)] = by_lane(terms).T[:16, :rows].astype(BF16)
 
 
-def attend(held, q_up, k_low, v_low):
-    rows, width = q_up.shape
-    return pl.pallas_call(
-        attend_kernel,
+def attend_own(held, k_low, v_low):
+    rows, width = k_low.shape
+    return pl.pallas_call(
+        attend_own_kernel,
         out_shape=(
             jax.ShapeDtypeStruct((rows, width), F32),
             jax.ShapeDtypeStruct((rows, HD), F32),
-            jax.ShapeDtypeStruct((rows + 16, width), BF16),
         ),
+        in_specs=[VMEM] * 3,
+        out_specs=(VMEM,) * 2,
+        compiler_params=pltpu.CompilerParams(vmem_limit_bytes=6 * 2**20),
+    )(held, k_low, v_low)
+
+
+def attend_up(held, q_up, k_low, v_low):
+    rows, width = q_up.shape
+    return pl.pallas_call(
+        attend_up_kernel,
+        out_shape=jax.ShapeDtypeStruct((rows + 16, width), BF16),
         in_specs=[VMEM] * 4,
-        out_specs=(VMEM,) * 3,
+        out_specs=VMEM,
         compiler_params=pltpu.CompilerParams(vmem_limit_bytes=6 * 2**20),
-        cost_estimate=pl.CostEstimate(
-            flops=16 * rows * rows * width,
-            bytes_accessed=24 * rows * width,
-            transcendentals=4 * rows * rows * width // HD,
-        ),
     )(held, q_up, k_low, v_low)
 
 
@@ -249,15 +265,20 @@
 
 
 def bytes_kernel(g0, g1, embed, gain, *refs):
-    bridge = refs[:4]
-    hid, turned, bw = refs[4:]
+    bridge, halves = refs[:2], refs[2:6]
+    hid, turned, bw = refs[6:]
     dp, sub, grp = lax.axis_index("dp"), lax.axis_index("sub"), lax.axis_index("groups")
     patches = g0.shape[0]
     bytes_ = g0.shape[1] // DSLICE
     rows = patches * bytes_
     depth = bridge[0].shape[0]
-    for b, ref in zip(block_order(dp, sub), bridge):
+    order = block_order(dp, sub)
+    cut = halves[0].shape[0]
+    for b, ref in zip(order[:2], bridge):
         bw[pl.ds(pl.multiple_of(b * depth, depth), depth), :] = ref[...]
+    for i, ref in enumerate(halves):
+        row = order[2 + i // 2] * depth + i % 2 * cut
+        bw[pl.ds(pl.multiple_of(row, 32), ref.shape[0]), :] = ref[...]
     glob = (g0[...] + g1[...].astype(F32)).astype(BF16)
     stacked = jnp.concatenate(
         [glob[:, p * DSLICE : (p + 1) * DSLICE] for p in range(bytes_)], axis=0
@@ -284,7 +305,7 @@
     return pl.pallas_call(
         bytes_kernel,
         out_shape=(jax.ShapeDtypeStruct((rows, DL), BF16),) * 2,
-        in_specs=[VMEM] * 8,
+        in_specs=[VMEM] * 10,
         out_specs=(VMEM,) * 2,
         scratch_shapes=[pltpu.VMEM((DSLICE, DL), BF16)],
         compiler_params=pltpu.CompilerParams(vmem_limit_bytes=10 * 2**20),
@@ -350,42 +371,46 @@
     w1 = lax.dynamic_slice_in_dim(after(qkv_weight, held), (grp * 2 + 1) * quarter, quarter, 0)
 
     x0 = swap(w0, "dp")
-    bridge_x = swap(bridge_weight, "dp")
+    bridge_rows = bridge_weight.shape[0] // 4 * 3
+    bridge_a = swap(bridge_weight[:bridge_rows], "dp")
     q_up = lax.ppermute(q_glob, "ctx", [(2, 0), (3, 1)])
     k_low = lax.ppermute(k_glob, "ctx", [(0, 1), (1, 2), (2, 3)])
     v_low = lax.ppermute(v_glob, "ctx", [(0, 1), (1, 2), (2, 3)])
-    q_up, k_low, v_low, x0, bridge_x, held, w1, bridge_weight, qkv_weight = (
+    q_up, k_low, v_low, x0, bridge_a, held, w1, bridge_weight, qkv_weight = (
         lax.optimization_barrier(
-            (q_up, k_low, v_low, x0, bridge_x, held, w1, bridge_weight, qkv_weight)
+            (q_up, k_low, v_low, x0, bridge_a, held, w1, bridge_weight, qkv_weight)
         )
     )
 
-    own, own_log, up = attend(held, q_up, k_low, v_low)
+    up = attend_up(held, q_up, k_low, v_low)
+    own, own_log = attend_own(held, k_low, v_low)
     low = lax.ppermute(up, "ctx", [(0, 2), (1, 3)])
     x1 = swap(w1, "dp")
     y0 = swap(x0, "groups")
     other_core = swap(qkv_weight, "sub")
-    core_x0 = swap(x0, "sub")
     out_weight = bring(after(out_weight, up), 4)
-    low, core_x0, x1, other_core, out_weight, bridge_x = lax.optimization_barrier(
-        (low, core_x0, x1, other_core, out_weight, bridge_x)
+    bridge_b = swap(bridge_weight[bridge_rows:], "dp")
+    low, x0, x1, other_core, out_weight, bridge_a, bridge_b = lax.optimization_barrier(
+        (low, x0, x1, other_core, out_weight, bridge_a, bridge_b)
     )
 
     away, kept = project(own, own_log, low, x_glob, out_weight)
     away = swap(away, "sub")
     y1 = swap(x1, "groups")
-    bridge_both = swap(bridge_x, "sub")
+    core_bridge_a = swap(bridge_a, "sub")
+    core_bridge_b = swap(bridge_b, "sub")
     core_y0 = swap(y0, "sub")
-    away, core_y0, bridge_both, x1, bridge_weight = lax.optimization_barrier(
-        (away, core_y0, bridge_both, x1, bridge_weight)
+    away, core_y0, core_bridge_a, core_bridge_b, x0, x1, bridge_weight = lax.optimization_barrier(
+        (away, core_y0, core_bridge_a, core_bridge_b, x0, x1, bridge_weight)
     )
 
     send, stay = sum_cores(kept, away)
     across = swap(send, "dp")
     core_x1 = swap(x1, "sub")
     bridge_core = swap(bridge_weight, "sub")
-    across, y1, core_x1, bridge_core = lax.optimization_barrier(
-        (across, y1, core_x1, bridge_core)
+    core_x0 = swap(x0, "sub")
+    across, y1, core_x0, core_x1, bridge_core = lax.optimization_barrier(
+        (across, y1, core_x0, core_x1, bridge_core)
     )
 
     core_y1 = swap(y1, "sub")
@@ -395,7 +420,7 @@
         across,
         byte_embed.reshape(rows, DL),
         norm_gain.reshape(1, DL),
-        [bridge_weight, bridge_core, bridge_x, bridge_both],
+        [bridge_weight, bridge_core, bridge_a, bridge_b, core_bridge_a, core_bridge_b],
     )
     result = local(
         hidden,

time: 51.7 us -> 51.2 us (level)
  waiting for transfers between devices: 24.4 us -> 20 us
  local copies, waits for them, and re-layouts: 6.09 us -> 7.78 us
  starting transfers between devices: 14.7 us -> 16.3 us
    ppermute x1, waiting for transfers between devices: 7.78 us -> 2.31 us  [small_mesh(): low = lax.ppermute(up, 'ctx', [(0, 2), (1, 3)])]
    ppermute x14 -> x16, starting transfers between devices: 8.88 us -> 10.5 us  [swap(): return lax.ppermute(x, axis, [(0, 1), (1, 0)])]
    ppermute x14 -> x16, waiting for transfers between devices: 12.5 us -> 13.6 us  [swap(): return lax.ppermute(x, axis, [(0, 1), (1, 0)])]
    slice x0 -> x2, local copies, waits for them, and re-layouts: none -> 0.95 us  [the longest x1 0.94 us: small_mesh(): bridge_a = swap(bridge_weight[:bridge_rows], 'dp')]
    dynamic_slice x1, local copies, waits for them, and re-layouts: 1.14 us -> 1.88 us  [small_mesh(): w0 = lax.dynamic_slice_in_dim(qkv_weight, grp * 2 * quarter, quarter, 0)]
    pallas_call x1 -> x2, Pallas kernels: 0.94 us -> 1.45 us  [the longest x1 0.76 us: attend_up(): pl.pallas_call(attend_up_kernel, out_shape=jax.ShapeDtypeStruct((rows + 1...]
  transfers between devices with their start and end apart: 18 -> 20, of which waited for: 8 -> 9; matrix products, arithmetic and copies ran while one was open for 0% -> 2% of each run, Pallas kernels for 6% -> 7%
where the time goes in v6:
time: 51.2 us; the launch traced here: 50.9 us
  waiting for transfers between devices  20 us (39%)
  starting transfers between devices  16.3 us (32%)
  local copies, waits for them, and re-layouts  7.78 us (15%)
  Pallas kernels  6.56 us (13%)
    ppermute x16, waiting for transfers between devices, swap(): return lax.ppermute(x, axis, [(0, 1), (1, 0)])  13.6 us
    ppermute x16, starting transfers between devices, swap(): return lax.ppermute(x, axis, [(0, 1), (1, 0)])  10.5 us
    unnamed x18, local copies, waits for them, and re-layouts  4.91 us
    ppermute x1, waiting for transfers between devices, small_mesh(): v_low = lax.ppermute(v_glob, 'ctx', [(0, 1), (1, 2), (2, 3)])  3.28 us
    pallas_call x1, Pallas kernels, local(): pl.pallas_call(functools.partial(local_kernel, counts=tuple((len(block) f...  2.77 us
    ppermute x1, waiting for transfers between devices, small_mesh(): low = lax.ppermute(up, 'ctx', [(0, 2), (1, 3)])  2.31 us
    ppermute x1, starting transfers between devices, small_mesh(): q_up = lax.ppermute(q_glob, 'ctx', [(2, 0), (3, 1)])  1.96 us
    dynamic_slice x1, local copies, waits for them, and re-layouts, small_mesh(): w0 = lax.dynamic_slice_in_dim(qkv_weight, grp * 2 * quarter, quarter, 0)  1.88 us
  transfers between devices with their start and end apart: 20, of which 9 were waited for; matrix products, arithmetic and copies ran while one was open for 2% of the time, Pallas kernels for 7%

profile of v6, /device:TPU:25, one launch (start us, length us, event | category | flops | bytes accessed | tf_op | source)
XLA Modules:
  0.0 50.9 jit_solution(3313711147164396921)
XLA Ops:
  0.0 1.9 %constant_dynamic-slice_fusion.1 = bf16[256,768]{1,0:T(8,128)(2,1)} fusion(bf16[1024,768]{1,0:T(8,128)(2,1)} %refs_0_.1, s32[]{:T(128)S(6)} %select_n.6), kind=kLoop, calls=%fused_computation.1 | loop fusion | bytes 786436 | tf_op jit(solution)/shard_map/dynamic_slice | solution.py:370
  1.9 1.2 %collective-permute-start.3 = (bf16[256,768]{1,0:T(8,128)(2,1)}, bf16[256,768]{1,0:T(8,128)(2,1)S(1)}, u32[]{:S(2)}, u32[]{:S(2)}) collective-permute-start(bf16[256,768]{1,0:T(8,128)(2,1)} %constant_dynamic-slice_fusion.1), channel_id=1, source_target_pairs={{0,2},{2,0},{1,3},{3,1},{4,6},{6,4},{5,7},{7,5},{8,10},{10,8},{9,1... | collective-permute-start | bytes 1179656 | tf_op jit(solution)/shard_map/ppermute | solution.py:356
  3.1 0.9 %slice.6 = bf16[96,1024]{1,0:T(8,128)(2,1)S(1)} slice(bf16[128,1024]{1,0:T(8,128)(2,1)} %refs_0_), slice={[0:96], [0:1024]} | slice | bytes 393216 | tf_op jit(solution)/shard_map/slice | solution.py:375
  4.4 2.0 %collective-permute-start = (bf16[128,512]{1,0:T(8,128)(2,1)}, bf16[128,512]{1,0:T(8,128)(2,1)S(1)}, u32[]{:S(2)}, u32[]{:S(2)}) collective-permute-start(bf16[128,512]{1,0:T(8,128)(2,1)} %q.1), channel_id=1, source_target_pairs={{8,0},{12,4},{9,1},{13,5},{10,2},{14,6},{11,3},{15,7},{24,16},{28,... | collective-permute-start | bytes 393224 | tf_op jit(solution)/shard_map/ppermute | solution.py:376
  6.3 1.3 %collective-permute-start.1 = (bf16[128,512]{1,0:T(8,128)(2,1)}, bf16[128,512]{1,0:T(8,128)(2,1)S(1)}, u32[]{:S(2)}, u32[]{:S(2)}) collective-permute-start(bf16[128,512]{1,0:T(8,128)(2,1)} %k.1), channel_id=1, source_target_pairs={{0,4},{4,8},{8,12},{1,5},{5,9},{9,13},{2,6},{6,10},{10,14},{3,7},{... | collective-permute-start | bytes 393224 | tf_op jit(solution)/shard_map/ppermute | solution.py:377
  7.6 1.3 %collective-permute-start.2 = (bf16[128,512]{1,0:T(8,128)(2,1)}, bf16[128,512]{1,0:T(8,128)(2,1)S(1)}, u32[]{:S(2)}, u32[]{:S(2)}) collective-permute-start(bf16[128,512]{1,0:T(8,128)(2,1)} %v.1), channel_id=1, source_target_pairs={{0,4},{4,8},{8,12},{1,5},{5,9},{9,13},{2,6},{6,10},{10,14},{3,7},{... | collective-permute-start | bytes 393224 | tf_op jit(solution)/shard_map/ppermute | solution.py:378
  8.9 0.9 %copy-done.5 = bf16[128,512]{1,0:T(8,128)(2,1)S(1)} copy-done((bf16[128,512]{1,0:T(8,128)(2,1)S(1)}, bf16[128,512]{1,0:T(8,128)(2,1)}, u32[]{:S(2)}) %copy-start.5) | copy-done | bytes 131096
  9.8 0.9 %copy-done.6 = bf16[128,512]{1,0:T(8,128)(2,1)S(1)} copy-done((bf16[128,512]{1,0:T(8,128)(2,1)S(1)}, bf16[128,512]{1,0:T(8,128)(2,1)}, u32[]{:S(2)}) %copy-start.6) | copy-done | bytes 131096
  10.7 0.9 %copy-done.7 = bf16[128,512]{1,0:T(8,128)(2,1)S(1)} copy-done((bf16[128,512]{1,0:T(8,128)(2,1)S(1)}, bf16[128,512]{1,0:T(8,128)(2,1)}, u32[]{:S(2)}) %copy-start.7) | copy-done | bytes 131096
  11.7 0.8 %collective-permute-done.1.k_low = bf16[128,512]{1,0:T(8,128)(2,1)S(1)} collective-permute-done((bf16[128,512]{1,0:T(8,128)(2,1)}, bf16[128,512]{1,0:T(8,128)(2,1)S(1)}, u32[]{:S(2)}, u32[]{:S(2)}) %collective-permute-start.1) | collective-permute-done | bytes 131104 | tf_op jit(solution)/shard_map/ppermute | solution.py:377
  12.6 3.3 %collective-permute-done.2.v_low = bf16[128,512]{1,0:T(8,128)(2,1)S(1)} collective-permute-done((bf16[128,512]{1,0:T(8,128)(2,1)}, bf16[128,512]{1,0:T(8,128)(2,1)S(1)}, u32[]{:S(2)}, u32[]{:S(2)}) %collective-permute-start.2) | collective-permute-done | bytes 131104 | tf_op jit(solution)/shard_map/ppermute | solution.py:378
  15.8 0.5 collective-permute-done.4.refs_2_
  16.3 1.5 %collective-permute-start.7 = (bf16[1024,768]{1,0:T(8,128)(2,1)S(1)}, bf16[1024,768]{1,0:T(8,128)(2,1)S(1)}, u32[]{:S(2)}, u32[]{:S(2)}) collective-permute-start(bf16[1024,768]{1,0:T(8,128)(2,1)S(1)} %copy-done.1), channel_id=1, source_target_pairs={{0,1},{1,0},{2,3},{3,2},{4,5},{5,4},{6,7},{7,6},{8,9},{9,8},{10,11... | collective-permute-start | bytes 4718600 | tf_op jit(solution)/shard_map/ppermute | solution.py:356
  17.8 1.2 %collective-permute-start.6 = (bf16[256,768]{1,0:T(8,128)(2,1)S(1)}, bf16[256,768]{1,0:T(8,128)(2,1)S(1)}, u32[]{:S(2)}, u32[]{:S(2)}) collective-permute-start(bf16[256,768]{1,0:T(8,128)(2,1)S(1)} %constant_dynamic-slice_fusion), channel_id=1, source_target_pairs={{0,2},{2,0},{1,3},{3,1},{4,6},{6,4},{5,7},{7,5},{8,10},{10,8},{9,1... | collective-permute-start | bytes 1179656 | tf_op jit(solution)/shard_map/ppermute | solution.py:356
  19.1 1.2 %collective-permute-start.10 = (bf16[256,768]{1,0:T(8,128)(2,1)S(1)}, bf16[256,768]{1,0:T(8,128)(2,1)S(1)}, u32[]{:S(2)}, u32[]{:S(2)}) collective-permute-start(bf16[256,768]{1,0:T(8,128)(2,1)S(1)} %collective-permute-done.3.refs_2_), channel_id=1, source_target_pairs={{0,16},{16,0},{1,17},{17,1},{2,18},{18,2},{3,19},{19,3},{4,20},{20... | collective-permute-start | bytes 1179656 | tf_op jit(solution)/shard_map/ppermute | solution.py:356
  20.3 0.8 %shard_map.93 = bf16[144,512]{1,0:T(8,128)(2,1)S(1)} custom-call(bf16[128,1536]{1,0:T(8,128)(2,1)S(1)} %shard_map.91.held, bf16[128,512]{1,0:T(8,128)(2,1)S(1)} %collective-permute-done.q_up, bf16[128,512]{1,0:T(8,128)(2,1)S(1)} %collective-permute-done.1.k_low, bf16[128,512]{1,0:T(8,128)(2,1)S(1)} %collective-permute-done.2.v_low), custom_call_target="tpu_custom_call" | custom-call | tf_op jit(solution)/shard_map/pallas_call | solution.py:138
  21.1 1.3 %collective-permute-start.5 = (bf16[144,512]{1,0:T(8,128)(2,1)S(1)}, bf16[144,512]{1,0:T(8,128)(2,1)S(1)}, u32[]{:S(2)}, u32[]{:S(2)}) collective-permute-start(bf16[144,512]{1,0:T(8,128)(2,1)S(1)} %shard_map.93), channel_id=1, source_target_pairs={{0,8},{4,12},{1,9},{5,13},{2,10},{6,14},{3,11},{7,15},{16,24},{20,... | collective-permute-start | bytes 442376 | tf_op jit(solution)/shard_map/ppermute | solution.py:387
  22.7 0.7 %shard_map.92 = (f32[128,512]{1,0:T(8,128)S(1)}, f32[128,128]{1,0:T(8,128)S(1)}) custom-call(bf16[128,1536]{1,0:T(8,128)(2,1)S(1)} %shard_map.91.held, bf16[128,512]{1,0:T(8,128)(2,1)S(1)} %collective-permute-done.1.k_low, bf16[128,512]{1,0:T(8,128)(2,1)S(1)} %collective-permute-done.2.v_low), custom_call_target="tpu_custom_call" | custom-call | tf_op jit(solution)/shard_map/pallas_call | solution.py:124
  23.4 2.2 %copy-done = bf16[512,4096]{1,0:T(8,128)(2,1)S(1)} copy-done((bf16[512,4096]{1,0:T(8,128)(2,1)S(1)}, bf16[512,4096]{1,0:T(8,128)(2,1)}, u32[]{:S(2)}) %copy-start) | copy-done | bytes 4194328
  25.9 4.1 %collective-permute-done.8.refs_3_ = bf16[32,1024]{1,0:T(8,128)(2,1)S(1)} collective-permute-done((bf16[32,1024]{1,0:T(8,128)(2,1)S(1)}, bf16[32,1024]{1,0:T(8,128)(2,1)S(1)}, u32[]{:S(2)}, u32[]{:S(2)}) %collective-permute-start.8) | collective-permute-done | bytes 65568 | tf_op jit(solution)/shard_map/ppermute | solution.py:356
  30.0 2.3 %collective-permute-done.5.low = bf16[144,512]{1,0:T(8,128)(2,1)S(1)} collective-permute-done((bf16[144,512]{1,0:T(8,128)(2,1)S(1)}, bf16[144,512]{1,0:T(8,128)(2,1)S(1)}, u32[]{:S(2)}, u32[]{:S(2)}) %collective-permute-start.5) | collective-permute-done | bytes 147488 | tf_op jit(solution)/shard_map/ppermute | solution.py:387
  32.3 1.1 %shard_map.95 = (bf16[64,4096]{1,0:T(8,128)(2,1)S(1)}, f32[64,4096]{1,0:T(8,128)S(1)}) custom-call(f32[128,512]{1,0:T(8,128)S(1)} %get-tuple-element.47.own, f32[128,128]{1,0:T(8,128)S(1)} %get-tuple-element.48.own_log, bf16[144,512]{1,0:T(8,128)(2,1)S(1)} %collective-permute-done.5.low, bf16[128,1024]{1,0:T(8,128)(2,1)S(1)} %copy-done.4, ...), custom_call_target="tpu_custom_call" | custom-call | flops 536870912 | bytes 5767168 | tf_op jit(solution)/shard_map/pallas_call | solution.py:228
  33.5 1.0 %collective-permute-start.9 = (bf16[64,4096]{1,0:T(8,128)(2,1)S(1)}, bf16[64,4096]{1,0:T(8,128)(2,1)S(1)}, u32[]{:S(2)}, u32[]{:S(2)}) collective-permute-start(bf16[64,4096]{1,0:T(8,128)(2,1)S(1)} %get-tuple-element.59), channel_id=1, source_target_pairs={{0,1},{1,0},{2,3},{3,2},{4,5},{5,4},{6,7},{7,6},{8,9},{9,8},{10,11... | collective-permute-start | bytes 1572872 | tf_op jit(solution)/shard_map/ppermute | solution.py:356
  34.6 0.4 collective-permute-start.12
  35.4 1.3 %collective-permute-done.11.refs_8_ = bf16[256,768]{1,0:T(8,128)(2,1)S(1)} collective-permute-done((bf16[256,768]{1,0:T(8,128)(2,1)S(1)}, bf16[256,768]{1,0:T(8,128)(2,1)S(1)}, u32[]{:S(2)}, u32[]{:S(2)}) %collective-permute-start.11) | collective-permute-done | bytes 393248 | tf_op jit(solution)/shard_map/ppermute | solution.py:356
  37.0 0.4 collective-permute-start.16
  37.9 0.7 %collective-permute-start.18 = (bf16[128,1024]{1,0:T(8,128)(2,1)S(1)}, bf16[128,1024]{1,0:T(8,128)(2,1)S(1)}, u32[]{:S(2)}, u32[]{:S(2)}) collective-permute-start(bf16[128,1024]{1,0:T(8,128)(2,1)S(1)} %copy-done.2), channel_id=1, source_target_pairs={{0,1},{1,0},{2,3},{3,2},{4,5},{5,4},{6,7},{7,6},{8,9},{9,8},{10,11... | collective-permute-start | bytes 786440 | tf_op jit(solution)/shard_map/ppermute | solution.py:356
  38.6 6.8 %collective-permute-done.15.refs_5_ = bf16[256,768]{1,0:T(8,128)(2,1)S(1)} collective-permute-done((bf16[256,768]{1,0:T(8,128)(2,1)S(1)}, bf16[256,768]{1,0:T(8,128)(2,1)S(1)}, u32[]{:S(2)}, u32[]{:S(2)}) %collective-permute-start.15) | collective-permute-done | bytes 393248 | tf_op jit(solution)/shard_map/ppermute | solution.py:356
  45.4 1.3 %collective-permute-start.19 = (bf16[256,768]{1,0:T(8,128)(2,1)S(1)}, bf16[256,768]{1,0:T(8,128)(2,1)S(1)}, u32[]{:S(2)}, u32[]{:S(2)}) collective-permute-start(bf16[256,768]{1,0:T(8,128)(2,1)S(1)} %collective-permute-done.15.refs_5_), channel_id=1, source_target_pairs={{0,1},{1,0},{2,3},{3,2},{4,5},{5,4},{6,7},{7,6},{8,9},{9,8},{10,11... | collective-permute-start | bytes 1179656 | tf_op jit(solution)/shard_map/ppermute | solution.py:356
  46.8 0.8 %shard_map.97 = (bf16[256,1024]{1,0:T(8,128)(2,1)S(1)}, bf16[256,1024]{1,0:T(8,128)(2,1)S(1)}) custom-call(f32[32,4096]{1,0:T(8,128)S(1)} %get-tuple-element.65.g0, bf16[32,4096]{1,0:T(8,128)(2,1)S(1)} %collective-permute-done.14.g1, bf16[256,1024]{1,0:T(8,128)(2,1)S(1)} %bitcast.3, f32[1,1024]{1,0:T(1,128)S(1)} %bitcast.4, bf16[128,1024]{1,0:T(8,128)(2,1)S(1)} %copy-done.2, ...), custom_call_target="tpu_custom_call" | custom-call | flops 268435456 | bytes 1572864 | tf_op jit(solution)/shard_map/pallas_call | solution.py:305
  47.5 0.6 %collective-permute-done.19.refs_9_ = bf16[256,768]{1,0:T(8,128)(2,1)S(1)} collective-permute-done((bf16[256,768]{1,0:T(8,128)(2,1)S(1)}, bf16[256,768]{1,0:T(8,128)(2,1)S(1)}, u32[]{:S(2)}, u32[]{:S(2)}) %collective-permute-start.19) | collective-permute-done | bytes 393248 | tf_op jit(solution)/shard_map/ppermute | solution.py:356
  48.1 2.8 %shard_map.98 = bf16[256,3072]{1,0:T(8,128)(2,1)} custom-call(bf16[256,1024]{1,0:T(8,128)(2,1)S(1)} %get-tuple-element.74.hid, bf16[256,1024]{1,0:T(8,128)(2,1)S(1)} %get-tuple-element.75.turned, bf16[1024,768]{1,0:T(8,128)(2,1)S(1)} %copy-done.1, bf16[1024,768]{1,0:T(8,128)(2,1)S(1)} %collective-permute-done.7.refs_1_, ...), custom_call_target="tpu_custom_call" | custom-call | tf_op jit(solution)/shard_map/pallas_call | solution.py:345
  (38 shorter events, 2.4 us)
Async XLA Ops:
  0.0 11.7 %copy-start.1 = (bf16[1024,768]{1,0:T(8,128)(2,1)S(1)}, bf16[1024,768]{1,0:T(8,128)(2,1)}, u32[]{:S(2)}) copy-start(bf16[1024,768]{1,0:T(8,128)(2,1)} %refs_0_.1) | copy-start | bytes 4718596
  1.9 20.5 %copy-start.2 = (bf16[128,1024]{1,0:T(8,128)(2,1)S(1)}, bf16[128,1024]{1,0:T(8,128)(2,1)}, u32[]{:S(2)}) copy-start(bf16[128,1024]{1,0:T(8,128)(2,1)} %refs_0_) | copy-start | bytes 786436
  1.9 14.4 %collective-permute-start.3 = (bf16[256,768]{1,0:T(8,128)(2,1)}, bf16[256,768]{1,0:T(8,128)(2,1)S(1)}, u32[]{:S(2)}, u32[]{:S(2)}) collective-permute-start(bf16[256,768]{1,0:T(8,128)(2,1)} %constant_dynamic-slice_fusion.1), channel_id=1, source_target_pairs={{0,2},{2,0},{1,3},{3,1},{4,6},{6,4},{5,7},{7,5},{8,10},{10,8},{9,1... | collective-permute-start | bytes 1179656 | tf_op jit(solution)/shard_map/ppermute | solution.py:356
  4.0 12.3 %collective-permute-start.4 = (bf16[96,1024]{1,0:T(8,128)(2,1)S(1)}, bf16[96,1024]{1,0:T(8,128)(2,1)S(1)}, u32[]{:S(2)}, u32[]{:S(2)}) collective-permute-start(bf16[96,1024]{1,0:T(8,128)(2,1)S(1)} %slice.6), channel_id=1, source_target_pairs={{0,2},{2,0},{1,3},{3,1},{4,6},{6,4},{5,7},{7,5},{8,10},{10,8},{9,1... | collective-permute-start | bytes 589832 | tf_op jit(solution)/shard_map/ppermute | solution.py:356
  4.4 7.4 %collective-permute-start = (bf16[128,512]{1,0:T(8,128)(2,1)}, bf16[128,512]{1,0:T(8,128)(2,1)S(1)}, u32[]{:S(2)}, u32[]{:S(2)}) collective-permute-start(bf16[128,512]{1,0:T(8,128)(2,1)} %q.1), channel_id=1, source_target_pairs={{8,0},{12,4},{9,1},{13,5},{10,2},{14,6},{11,3},{15,7},{24,16},{28,... | collective-permute-start | bytes 393224 | tf_op jit(solution)/shard_map/ppermute | solution.py:376
  6.3 6.2 %collective-permute-start.1 = (bf16[128,512]{1,0:T(8,128)(2,1)}, bf16[128,512]{1,0:T(8,128)(2,1)S(1)}, u32[]{:S(2)}, u32[]{:S(2)}) collective-permute-start(bf16[128,512]{1,0:T(8,128)(2,1)} %k.1), channel_id=1, source_target_pairs={{0,4},{4,8},{8,12},{1,5},{5,9},{9,13},{2,6},{6,10},{10,14},{3,7},{... | collective-permute-start | bytes 393224 | tf_op jit(solution)/shard_map/ppermute | solution.py:377
  7.6 8.2 %collective-permute-start.2 = (bf16[128,512]{1,0:T(8,128)(2,1)}, bf16[128,512]{1,0:T(8,128)(2,1)S(1)}, u32[]{:S(2)}, u32[]{:S(2)}) collective-permute-start(bf16[128,512]{1,0:T(8,128)(2,1)} %v.1), channel_id=1, source_target_pairs={{0,4},{4,8},{8,12},{1,5},{5,9},{9,13},{2,6},{6,10},{10,14},{3,7},{... | collective-permute-start | bytes 393224 | tf_op jit(solution)/shard_map/ppermute | solution.py:378
  8.9 0.9 %copy-start.5 = (bf16[128,512]{1,0:T(8,128)(2,1)S(1)}, bf16[128,512]{1,0:T(8,128)(2,1)}, u32[]{:S(2)}) copy-start(bf16[128,512]{1,0:T(8,128)(2,1)} %q.1) | copy-start | bytes 393220
  9.8 0.9 %copy-start.6 = (bf16[128,512]{1,0:T(8,128)(2,1)S(1)}, bf16[128,512]{1,0:T(8,128)(2,1)}, u32[]{:S(2)}) copy-start(bf16[128,512]{1,0:T(8,128)(2,1)} %k.1) | copy-start | bytes 393220
  10.7 0.9 %copy-start.7 = (bf16[128,512]{1,0:T(8,128)(2,1)S(1)}, bf16[128,512]{1,0:T(8,128)(2,1)}, u32[]{:S(2)}) copy-start(bf16[128,512]{1,0:T(8,128)(2,1)} %v.1) | copy-start | bytes 393220
  16.3 16.0 %collective-permute-start.7 = (bf16[1024,768]{1,0:T(8,128)(2,1)S(1)}, bf16[1024,768]{1,0:T(8,128)(2,1)S(1)}, u32[]{:S(2)}, u32[]{:S(2)}) collective-permute-start(bf16[1024,768]{1,0:T(8,128)(2,1)S(1)} %copy-done.1), channel_id=1, source_target_pairs={{0,1},{1,0},{2,3},{3,2},{4,5},{5,4},{6,7},{7,6},{8,9},{9,8},{10,11... | collective-permute-start | bytes 4718600 | tf_op jit(solution)/shard_map/ppermute | solution.py:356
  17.8 14.5 %collective-permute-start.6 = (bf16[256,768]{1,0:T(8,128)(2,1)S(1)}, bf16[256,768]{1,0:T(8,128)(2,1)S(1)}, u32[]{:S(2)}, u32[]{:S(2)}) collective-permute-start(bf16[256,768]{1,0:T(8,128)(2,1)S(1)} %constant_dynamic-slice_fusion), channel_id=1, source_target_pairs={{0,2},{2,0},{1,3},{3,1},{4,6},{6,4},{5,7},{7,5},{8,10},{10,8},{9,1... | collective-permute-start | bytes 1179656 | tf_op jit(solution)/shard_map/ppermute | solution.py:356
  19.1 15.5 %collective-permute-start.10 = (bf16[256,768]{1,0:T(8,128)(2,1)S(1)}, bf16[256,768]{1,0:T(8,128)(2,1)S(1)}, u32[]{:S(2)}, u32[]{:S(2)}) collective-permute-start(bf16[256,768]{1,0:T(8,128)(2,1)S(1)} %collective-permute-done.3.refs_2_), channel_id=1, source_target_pairs={{0,16},{16,0},{1,17},{17,1},{2,18},{18,2},{3,19},{19,3},{4,20},{20... | collective-permute-start | bytes 1179656 | tf_op jit(solution)/shard_map/ppermute | solution.py:356
  21.1 11.2 %collective-permute-start.5 = (bf16[144,512]{1,0:T(8,128)(2,1)S(1)}, bf16[144,512]{1,0:T(8,128)(2,1)S(1)}, u32[]{:S(2)}, u32[]{:S(2)}) collective-permute-start(bf16[144,512]{1,0:T(8,128)(2,1)S(1)} %shard_map.93), channel_id=1, source_target_pairs={{0,8},{4,12},{1,9},{5,13},{2,10},{6,14},{3,11},{7,15},{16,24},{20,... | collective-permute-start | bytes 442376 | tf_op jit(solution)/shard_map/ppermute | solution.py:387
  22.4 7.6 %collective-permute-start.8 = (bf16[32,1024]{1,0:T(8,128)(2,1)S(1)}, bf16[32,1024]{1,0:T(8,128)(2,1)S(1)}, u32[]{:S(2)}, u32[]{:S(2)}) collective-permute-start(bf16[32,1024]{1,0:T(8,128)(2,1)S(1)} %slice.7), channel_id=1, source_target_pairs={{0,2},{2,0},{1,3},{3,1},{4,6},{6,4},{5,7},{7,5},{8,10},{10,8},{9,1... | collective-permute-start | bytes 196616 | tf_op jit(solution)/shard_map/ppermute | solution.py:356
  23.4 2.2 %copy-start = (bf16[512,4096]{1,0:T(8,128)(2,1)S(1)}, bf16[512,4096]{1,0:T(8,128)(2,1)}, u32[]{:S(2)}) copy-start(bf16[512,4096]{1,0:T(8,128)(2,1)} %source) | copy-start | bytes 12582916
  25.6 6.7 %copy-start.4 = (bf16[128,1024]{1,0:T(8,128)(2,1)S(1)}, bf16[128,1024]{1,0:T(8,128)(2,1)}, u32[]{:S(2)}) copy-start(bf16[128,1024]{1,0:T(8,128)(2,1)} %x.1) | copy-start | bytes 786436
  33.5 13.3 %copy-start.3 = (bf16[32,8,1024]{2,1,0:T(8,128)(2,1)S(1)}, bf16[32,8,1024]{2,1,0:T(8,128)(2,1)}, u32[]{:S(2)}) copy-start(bf16[32,8,1024]{2,1,0:T(8,128)(2,1)} %param.15) | copy-start | bytes 1572868
  33.5 13.3 %copy-start.8 = (f32[1024]{0:T(1024)S(1)}, f32[1024]{0:T(1024)}, u32[]{:S(2)}) copy-start(f32[1024]{0:T(1024)} %param.16) | copy-start | bytes 12292
  33.5 3.5 %collective-permute-start.9 = (bf16[64,4096]{1,0:T(8,128)(2,1)S(1)}, bf16[64,4096]{1,0:T(8,128)(2,1)S(1)}, u32[]{:S(2)}, u32[]{:S(2)}) collective-permute-start(bf16[64,4096]{1,0:T(8,128)(2,1)S(1)} %get-tuple-element.59), channel_id=1, source_target_pairs={{0,1},{1,0},{2,3},{3,2},{4,5},{5,4},{6,7},{7,6},{8,9},{9,8},{10,11... | collective-permute-start | bytes 1572872 | tf_op jit(solution)/shard_map/ppermute | solution.py:356
  34.5 2.1 %collective-permute-start.11 = (bf16[256,768]{1,0:T(8,128)(2,1)S(1)}, bf16[256,768]{1,0:T(8,128)(2,1)S(1)}, u32[]{:S(2)}, u32[]{:S(2)}) collective-permute-start(bf16[256,768]{1,0:T(8,128)(2,1)S(1)} %collective-permute-done.10.refs_4_), channel_id=1, source_target_pairs={{0,1},{1,0},{2,3},{3,2},{4,5},{5,4},{6,7},{7,6},{8,9},{9,8},{10,11... | collective-permute-start | bytes 1179656 | tf_op jit(solution)/shard_map/ppermute | solution.py:356
  34.6 2.4 %collective-permute-start.12 = (bf16[96,1024]{1,0:T(8,128)(2,1)S(1)}, bf16[96,1024]{1,0:T(8,128)(2,1)S(1)}, u32[]{:S(2)}, u32[]{:S(2)}) collective-permute-start(bf16[96,1024]{1,0:T(8,128)(2,1)S(1)} %collective-permute-done.4.refs_2_), channel_id=1, source_target_pairs={{0,1},{1,0},{2,3},{3,2},{4,5},{5,4},{6,7},{7,6},{8,9},{9,8},{10,11... | collective-permute-start | bytes 589832 | tf_op jit(solution)/shard_map/ppermute | solution.py:356
  35.0 2.0 %collective-permute-start.13 = (bf16[32,1024]{1,0:T(8,128)(2,1)S(1)}, bf16[32,1024]{1,0:T(8,128)(2,1)S(1)}, u32[]{:S(2)}, u32[]{:S(2)}) collective-permute-start(bf16[32,1024]{1,0:T(8,128)(2,1)S(1)} %collective-permute-done.8.refs_3_), channel_id=1, source_target_pairs={{0,1},{1,0},{2,3},{3,2},{4,5},{5,4},{6,7},{7,6},{8,9},{9,8},{10,11... | collective-permute-start | bytes 196616 | tf_op jit(solution)/shard_map/ppermute | solution.py:356
  35.1 10.3 %collective-permute-start.15 = (bf16[256,768]{1,0:T(8,128)(2,1)S(1)}, bf16[256,768]{1,0:T(8,128)(2,1)S(1)}, u32[]{:S(2)}, u32[]{:S(2)}) collective-permute-start(bf16[256,768]{1,0:T(8,128)(2,1)S(1)} %collective-permute-done.6.refs_3_), channel_id=1, source_target_pairs={{0,16},{16,0},{1,17},{17,1},{2,18},{18,2},{3,19},{19,3},{4,20},{20... | collective-permute-start | bytes 1179656 | tf_op jit(solution)/shard_map/ppermute | solution.py:356
  37.0 8.4 %collective-permute-start.16 = (bf16[256,768]{1,0:T(8,128)(2,1)S(1)}, bf16[256,768]{1,0:T(8,128)(2,1)S(1)}, u32[]{:S(2)}, u32[]{:S(2)}) collective-permute-start(bf16[256,768]{1,0:T(8,128)(2,1)S(1)} %collective-permute-done.3.refs_2_), channel_id=1, source_target_pairs={{0,1},{1,0},{2,3},{3,2},{4,5},{5,4},{6,7},{7,6},{8,9},{9,8},{10,11... | collective-permute-start | bytes 1179656 | tf_op jit(solution)/shard_map/ppermute | solution.py:356
  37.4 8.0 %collective-permute-start.17 = (bf16[256,768]{1,0:T(8,128)(2,1)S(1)}, bf16[256,768]{1,0:T(8,128)(2,1)S(1)}, u32[]{:S(2)}, u32[]{:S(2)}) collective-permute-start(bf16[256,768]{1,0:T(8,128)(2,1)S(1)} %collective-permute-done.6.refs_3_), channel_id=1, source_target_pairs={{0,1},{1,0},{2,3},{3,2},{4,5},{5,4},{6,7},{7,6},{8,9},{9,8},{10,11... | collective-permute-start | bytes 1179656 | tf_op jit(solution)/shard_map/ppermute | solution.py:356
  37.6 7.8 %collective-permute-start.14 = (bf16[32,4096]{1,0:T(8,128)(2,1)S(1)}, bf16[32,4096]{1,0:T(8,128)(2,1)S(1)}, u32[]{:S(2)}, u32[]{:S(2)}) collective-permute-start(bf16[32,4096]{1,0:T(8,128)(2,1)S(1)} %get-tuple-element.66), channel_id=1, source_target_pairs={{0,2},{2,0},{1,3},{3,1},{4,6},{6,4},{5,7},{7,5},{8,10},{10,8},{9,1... | collective-permute-start | bytes 786440 | tf_op jit(solution)/shard_map/ppermute | solution.py:356
  37.9 7.5 %collective-permute-start.18 = (bf16[128,1024]{1,0:T(8,128)(2,1)S(1)}, bf16[128,1024]{1,0:T(8,128)(2,1)S(1)}, u32[]{:S(2)}, u32[]{:S(2)}) collective-permute-start(bf16[128,1024]{1,0:T(8,128)(2,1)S(1)} %copy-done.2), channel_id=1, source_target_pairs={{0,1},{1,0},{2,3},{3,2},{4,5},{5,4},{6,7},{7,6},{8,9},{9,8},{10,11... | collective-permute-start | bytes 786440 | tf_op jit(solution)/shard_map/ppermute | solution.py:356
  45.4 2.7 %collective-permute-start.19 = (bf16[256,768]{1,0:T(8,128)(2,1)S(1)}, bf16[256,768]{1,0:T(8,128)(2,1)S(1)}, u32[]{:S(2)}, u32[]{:S(2)}) collective-permute-start(bf16[256,768]{1,0:T(8,128)(2,1)S(1)} %collective-permute-done.15.refs_5_), channel_id=1, source_target_pairs={{0,1},{1,0},{2,3},{3,2},{4,5},{5,4},{6,7},{7,6},{8,9},{9,8},{10,11... | collective-permute-start | bytes 1179656 | tf_op jit(solution)/shard_map/ppermute | solution.py:356

commit v7 on v6

--- a/solution.py
+++ b/solution.py
@@ -315,22 +315,34 @@
     )(g0, g1, embed, gain, *bridge)
 
 
-def local_kernel(hid, turned, *refs, counts):
-    dp, sub = lax.axis_index("dp"), lax.axis_index("sub")
-    width = refs[0].shape[1]
-    out, held, sems = refs[sum(counts) :]
-    copies, at = [], 0
-    for i, b in enumerate(block_order(dp, sub)):
-        source = hid if counts[i] == 1 else turned
-        total, row = None, 0
-        for ref in refs[at : at + counts[i]]:
-            term = dot(source[:, row : row + ref.shape[0]], ref[...])
-            total = term if total is None else total + term
-            row += ref.shape[0]
-        at += counts[i]
-        held[i, :, :] = total.astype(BF16)
+def project_pieces(source, refs):
+    total, row = None, 0
+    for ref in refs:
+        term = dot(source[:, row : row + ref.shape[0]], ref[...])
+        total = term if total is None else total + term
+        row += ref.shape[0]
+    return total.astype(BF16)
+
+
+def first_blocks_kernel(hid, turned, *refs, counts):
+    out, at = refs[-1], 0
+    for i, count in enumerate(counts):
+        out[i, :, :] = project_pieces(hid if count == 1 else turned, refs[at : at + count])
+        at += count
+
+
+def last_block_kernel(turned, first, *refs):
+    pieces, (out, held, sems) = refs[:-3], refs[-3:]
+    width = held.shape[1]
+    order = block_order(lax.axis_index("dp"), lax.axis_index("sub"))
+    copies = []
+    for i, b in enumerate(order):
+        if i == len(order) - 1:
+            held[...] = project_pieces(turned, pieces)
         copy = pltpu.make_async_copy(
-            held.at[i], out.at[:, pl.ds(pl.multiple_of(b * width, 128), width)], sems.at[i]
+            first.at[i] if i < len(order) - 1 else held,
+            out.at[:, pl.ds(pl.multiple_of(b * width, 128), width)],
+            sems.at[i],
         )
         copy.start()
         copies.append(copy)
@@ -340,16 +352,28 @@
 
 def local(hid, turned, *blocks):
     rows = hid.shape[0]
-    weights = [piece for block in blocks for piece in block]
+    weights = [piece for block in blocks[:-1] for piece in block]
     width = weights[0].shape[1]
-    return pl.pallas_call(
-        functools.partial(local_kernel, counts=tuple(len(block) for block in blocks)),
-        out_shape=jax.ShapeDtypeStruct((rows, 4 * width), BF16),
+    first = pl.pallas_call(
+        functools.partial(
+            first_blocks_kernel, counts=tuple(len(block) for block in blocks[:-1])
+        ),
+        out_shape=jax.ShapeDtypeStruct((len(blocks) - 1, rows, width), BF16),
         in_specs=[VMEM] * (2 + len(weights)),
-        out_specs=pl.BlockSpec(memory_space=pl.ANY),
-        scratch_shapes=[pltpu.VMEM((4, rows, width), BF16), pltpu.SemaphoreType.DMA((4,))],
+        out_specs=VMEM,
         compiler_params=pltpu.CompilerParams(vmem_limit_bytes=12 * 2**20),
     )(hid, turned, *weights)
+    return pl.pallas_call(
+        last_block_kernel,
+        out_shape=jax.ShapeDtypeStruct((rows, len(blocks) * width), BF16),
+        in_specs=[VMEM] * (2 + len(blocks[-1])),
+        out_specs=pl.BlockSpec(memory_space=pl.ANY),
+        scratch_shapes=[
+            pltpu.VMEM((rows, width), BF16),
+            pltpu.SemaphoreType.DMA((len(blocks),)),
+        ],
+        compiler_params=pltpu.CompilerParams(vmem_limit_bytes=12 * 2**20),
+    )(turned, first, *blocks[-1])
 
 
 def swap(x, axis):

time: 51.2 us -> 50.9 us (level)
  waiting for transfers between devices: 20 us -> 19.4 us
    ppermute x16, waiting for transfers between devices: 13.6 us -> 13 us  [swap(): return lax.ppermute(x, axis, [(0, 1), (1, 0)])]
    pallas_call x1 -> x2, Pallas kernels: 2.77 us -> 2.97 us  [the longest x1 1.57 us: local(): pl.pallas_call(last_block_kernel, out_shape=jax.ShapeDtypeStruct((rows, l...]
  transfers between devices with their start and end apart: 20 -> 20, of which waited for: 9 -> 8; matrix products, arithmetic and copies ran while one was open for 2% -> 2% of each run, Pallas kernels for 7% -> 10%
where the time goes in v7:
time: 50.9 us; the launch traced here: 50.5 us
  waiting for transfers between devices  19.4 us (38%)
  starting transfers between devices  16.3 us (32%)
  local copies, waits for them, and re-layouts  7.78 us (15%)
  Pallas kernels  6.76 us (13%)
    ppermute x16, waiting for transfers between devices, swap(): return lax.ppermute(x, axis, [(0, 1), (1, 0)])  13 us
    ppermute x16, starting transfers between devices, swap(): return lax.ppermute(x, axis, [(0, 1), (1, 0)])  10.5 us
    unnamed x18, local copies, waits for them, and re-layouts  4.91 us
    ppermute x1, waiting for transfers between devices, small_mesh(): v_low = lax.ppermute(v_glob, 'ctx', [(0, 1), (1, 2), (2, 3)])  3.28 us
    ppermute x1, waiting for transfers between devices, small_mesh(): low = lax.ppermute(up, 'ctx', [(0, 2), (1, 3)])  2.31 us
    ppermute x1, starting transfers between devices, small_mesh(): q_up = lax.ppermute(q_glob, 'ctx', [(2, 0), (3, 1)])  1.96 us
    dynamic_slice x1, local copies, waits for them, and re-layouts, small_mesh(): w0 = lax.dynamic_slice_in_dim(qkv_weight, grp * 2 * quarter, quarter, 0)  1.88 us
    pallas_call x1, Pallas kernels, local(): pl.pallas_call(last_block_kernel, out_shape=jax.ShapeDtypeStruct((rows, l...  1.57 us
  transfers between devices with their start and end apart: 20, of which 8 were waited for; matrix products, arithmetic and copies ran while one was open for 2% of the time, Pallas kernels for 10%

profile of v7, /device:TPU:25, one launch (start us, length us, event | category | flops | bytes accessed | tf_op | source)
XLA Modules:
  0.0 50.5 jit_solution(16820778662840828179)
XLA Ops:
  0.0 1.9 %constant_dynamic-slice_fusion.1 = bf16[256,768]{1,0:T(8,128)(2,1)} fusion(bf16[1024,768]{1,0:T(8,128)(2,1)} %refs_0_.1, s32[]{:T(128)S(6)} %select_n.6), kind=kLoop, calls=%fused_computation.1 | loop fusion | bytes 786436 | tf_op jit(solution)/shard_map/dynamic_slice | solution.py:394
  1.9 1.2 %collective-permute-start.3 = (bf16[256,768]{1,0:T(8,128)(2,1)}, bf16[256,768]{1,0:T(8,128)(2,1)S(1)}, u32[]{:S(2)}, u32[]{:S(2)}) collective-permute-start(bf16[256,768]{1,0:T(8,128)(2,1)} %constant_dynamic-slice_fusion.1), channel_id=1, source_target_pairs={{0,2},{2,0},{1,3},{3,1},{4,6},{6,4},{5,7},{7,5},{8,10},{10,8},{9,1... | collective-permute-start | bytes 1179656 | tf_op jit(solution)/shard_map/ppermute | solution.py:380
  3.1 0.9 %slice.6 = bf16[96,1024]{1,0:T(8,128)(2,1)S(1)} slice(bf16[128,1024]{1,0:T(8,128)(2,1)} %refs_0_), slice={[0:96], [0:1024]} | slice | bytes 393216 | tf_op jit(solution)/shard_map/slice | solution.py:399
  4.4 2.0 %collective-permute-start = (bf16[128,512]{1,0:T(8,128)(2,1)}, bf16[128,512]{1,0:T(8,128)(2,1)S(1)}, u32[]{:S(2)}, u32[]{:S(2)}) collective-permute-start(bf16[128,512]{1,0:T(8,128)(2,1)} %q.1), channel_id=1, source_target_pairs={{8,0},{12,4},{9,1},{13,5},{10,2},{14,6},{11,3},{15,7},{24,16},{28,... | collective-permute-start | bytes 393224 | tf_op jit(solution)/shard_map/ppermute | solution.py:400
  6.3 1.3 %collective-permute-start.1 = (bf16[128,512]{1,0:T(8,128)(2,1)}, bf16[128,512]{1,0:T(8,128)(2,1)S(1)}, u32[]{:S(2)}, u32[]{:S(2)}) collective-permute-start(bf16[128,512]{1,0:T(8,128)(2,1)} %k.1), channel_id=1, source_target_pairs={{0,4},{4,8},{8,12},{1,5},{5,9},{9,13},{2,6},{6,10},{10,14},{3,7},{... | collective-permute-start | bytes 393224 | tf_op jit(solution)/shard_map/ppermute | solution.py:401
  7.6 1.3 %collective-permute-start.2 = (bf16[128,512]{1,0:T(8,128)(2,1)}, bf16[128,512]{1,0:T(8,128)(2,1)S(1)}, u32[]{:S(2)}, u32[]{:S(2)}) collective-permute-start(bf16[128,512]{1,0:T(8,128)(2,1)} %v.1), channel_id=1, source_target_pairs={{0,4},{4,8},{8,12},{1,5},{5,9},{9,13},{2,6},{6,10},{10,14},{3,7},{... | collective-permute-start | bytes 393224 | tf_op jit(solution)/shard_map/ppermute | solution.py:402
  8.9 0.9 %copy-done.5 = bf16[128,512]{1,0:T(8,128)(2,1)S(1)} copy-done((bf16[128,512]{1,0:T(8,128)(2,1)S(1)}, bf16[128,512]{1,0:T(8,128)(2,1)}, u32[]{:S(2)}) %copy-start.5) | copy-done | bytes 131096
  9.8 0.9 %copy-done.6 = bf16[128,512]{1,0:T(8,128)(2,1)S(1)} copy-done((bf16[128,512]{1,0:T(8,128)(2,1)S(1)}, bf16[128,512]{1,0:T(8,128)(2,1)}, u32[]{:S(2)}) %copy-start.6) | copy-done | bytes 131096
  10.7 0.9 %copy-done.7 = bf16[128,512]{1,0:T(8,128)(2,1)S(1)} copy-done((bf16[128,512]{1,0:T(8,128)(2,1)S(1)}, bf16[128,512]{1,0:T(8,128)(2,1)}, u32[]{:S(2)}) %copy-start.7) | copy-done | bytes 131096
  11.7 0.8 %collective-permute-done.1.k_low = bf16[128,512]{1,0:T(8,128)(2,1)S(1)} collective-permute-done((bf16[128,512]{1,0:T(8,128)(2,1)}, bf16[128,512]{1,0:T(8,128)(2,1)S(1)}, u32[]{:S(2)}, u32[]{:S(2)}) %collective-permute-start.1) | collective-permute-done | bytes 131104 | tf_op jit(solution)/shard_map/ppermute | solution.py:401
  12.6 3.3 %collective-permute-done.2.v_low = bf16[128,512]{1,0:T(8,128)(2,1)S(1)} collective-permute-done((bf16[128,512]{1,0:T(8,128)(2,1)}, bf16[128,512]{1,0:T(8,128)(2,1)S(1)}, u32[]{:S(2)}, u32[]{:S(2)}) %collective-permute-start.2) | collective-permute-done | bytes 131104 | tf_op jit(solution)/shard_map/ppermute | solution.py:402
  15.8 0.5 collective-permute-done.4.refs_2_
  16.3 1.5 %collective-permute-start.7 = (bf16[1024,768]{1,0:T(8,128)(2,1)S(1)}, bf16[1024,768]{1,0:T(8,128)(2,1)S(1)}, u32[]{:S(2)}, u32[]{:S(2)}) collective-permute-start(bf16[1024,768]{1,0:T(8,128)(2,1)S(1)} %copy-done.1), channel_id=1, source_target_pairs={{0,1},{1,0},{2,3},{3,2},{4,5},{5,4},{6,7},{7,6},{8,9},{9,8},{10,11... | collective-permute-start | bytes 4718600 | tf_op jit(solution)/shard_map/ppermute | solution.py:380
  17.8 1.2 %collective-permute-start.6 = (bf16[256,768]{1,0:T(8,128)(2,1)S(1)}, bf16[256,768]{1,0:T(8,128)(2,1)S(1)}, u32[]{:S(2)}, u32[]{:S(2)}) collective-permute-start(bf16[256,768]{1,0:T(8,128)(2,1)S(1)} %constant_dynamic-slice_fusion), channel_id=1, source_target_pairs={{0,2},{2,0},{1,3},{3,1},{4,6},{6,4},{5,7},{7,5},{8,10},{10,8},{9,1... | collective-permute-start | bytes 1179656 | tf_op jit(solution)/shard_map/ppermute | solution.py:380
  19.1 1.2 %collective-permute-start.10 = (bf16[256,768]{1,0:T(8,128)(2,1)S(1)}, bf16[256,768]{1,0:T(8,128)(2,1)S(1)}, u32[]{:S(2)}, u32[]{:S(2)}) collective-permute-start(bf16[256,768]{1,0:T(8,128)(2,1)S(1)} %collective-permute-done.3.refs_2_), channel_id=1, source_target_pairs={{0,16},{16,0},{1,17},{17,1},{2,18},{18,2},{3,19},{19,3},{4,20},{20... | collective-permute-start | bytes 1179656 | tf_op jit(solution)/shard_map/ppermute | solution.py:380
  20.3 0.8 %shard_map.93 = bf16[144,512]{1,0:T(8,128)(2,1)S(1)} custom-call(bf16[128,1536]{1,0:T(8,128)(2,1)S(1)} %shard_map.91.held, bf16[128,512]{1,0:T(8,128)(2,1)S(1)} %collective-permute-done.q_up, bf16[128,512]{1,0:T(8,128)(2,1)S(1)} %collective-permute-done.1.k_low, bf16[128,512]{1,0:T(8,128)(2,1)S(1)} %collective-permute-done.2.v_low), custom_call_target="tpu_custom_call" | custom-call | tf_op jit(solution)/shard_map/pallas_call | solution.py:138
  21.1 1.3 %collective-permute-start.5 = (bf16[144,512]{1,0:T(8,128)(2,1)S(1)}, bf16[144,512]{1,0:T(8,128)(2,1)S(1)}, u32[]{:S(2)}, u32[]{:S(2)}) collective-permute-start(bf16[144,512]{1,0:T(8,128)(2,1)S(1)} %shard_map.93), channel_id=1, source_target_pairs={{0,8},{4,12},{1,9},{5,13},{2,10},{6,14},{3,11},{7,15},{16,24},{20,... | collective-permute-start | bytes 442376 | tf_op jit(solution)/shard_map/ppermute | solution.py:411
  22.7 0.7 %shard_map.92 = (f32[128,512]{1,0:T(8,128)S(1)}, f32[128,128]{1,0:T(8,128)S(1)}) custom-call(bf16[128,1536]{1,0:T(8,128)(2,1)S(1)} %shard_map.91.held, bf16[128,512]{1,0:T(8,128)(2,1)S(1)} %collective-permute-done.1.k_low, bf16[128,512]{1,0:T(8,128)(2,1)S(1)} %collective-permute-done.2.v_low), custom_call_target="tpu_custom_call" | custom-call | tf_op jit(solution)/shard_map/pallas_call | solution.py:124
  23.4 2.2 %copy-done = bf16[512,4096]{1,0:T(8,128)(2,1)S(1)} copy-done((bf16[512,4096]{1,0:T(8,128)(2,1)S(1)}, bf16[512,4096]{1,0:T(8,128)(2,1)}, u32[]{:S(2)}) %copy-start) | copy-done | bytes 4194328
  25.9 4.1 %collective-permute-done.8.refs_3_ = bf16[32,1024]{1,0:T(8,128)(2,1)S(1)} collective-permute-done((bf16[32,1024]{1,0:T(8,128)(2,1)S(1)}, bf16[32,1024]{1,0:T(8,128)(2,1)S(1)}, u32[]{:S(2)}, u32[]{:S(2)}) %collective-permute-start.8) | collective-permute-done | bytes 65568 | tf_op jit(solution)/shard_map/ppermute | solution.py:380
  30.0 2.3 %collective-permute-done.5.low = bf16[144,512]{1,0:T(8,128)(2,1)S(1)} collective-permute-done((bf16[144,512]{1,0:T(8,128)(2,1)S(1)}, bf16[144,512]{1,0:T(8,128)(2,1)S(1)}, u32[]{:S(2)}, u32[]{:S(2)}) %collective-permute-start.5) | collective-permute-done | bytes 147488 | tf_op jit(solution)/shard_map/ppermute | solution.py:411
  32.3 1.1 %shard_map.95 = (bf16[64,4096]{1,0:T(8,128)(2,1)S(1)}, f32[64,4096]{1,0:T(8,128)S(1)}) custom-call(f32[128,512]{1,0:T(8,128)S(1)} %get-tuple-element.47.own, f32[128,128]{1,0:T(8,128)S(1)} %get-tuple-element.48.own_log, bf16[144,512]{1,0:T(8,128)(2,1)S(1)} %collective-permute-done.5.low, bf16[128,1024]{1,0:T(8,128)(2,1)S(1)} %copy-done.4, ...), custom_call_target="tpu_custom_call" | custom-call | flops 536870912 | bytes 5767168 | tf_op jit(solution)/shard_map/pallas_call | solution.py:228
  33.5 1.0 %collective-permute-start.9 = (bf16[64,4096]{1,0:T(8,128)(2,1)S(1)}, bf16[64,4096]{1,0:T(8,128)(2,1)S(1)}, u32[]{:S(2)}, u32[]{:S(2)}) collective-permute-start(bf16[64,4096]{1,0:T(8,128)(2,1)S(1)} %get-tuple-element.59), channel_id=1, source_target_pairs={{0,1},{1,0},{2,3},{3,2},{4,5},{5,4},{6,7},{7,6},{8,9},{9,8},{10,11... | collective-permute-start | bytes 1572872 | tf_op jit(solution)/shard_map/ppermute | solution.py:380
  34.6 0.4 collective-permute-start.12
  35.4 1.3 %collective-permute-done.11.refs_2_ = bf16[256,768]{1,0:T(8,128)(2,1)S(1)} collective-permute-done((bf16[256,768]{1,0:T(8,128)(2,1)S(1)}, bf16[256,768]{1,0:T(8,128)(2,1)S(1)}, u32[]{:S(2)}, u32[]{:S(2)}) %collective-permute-start.11) | collective-permute-done | bytes 393248 | tf_op jit(solution)/shard_map/ppermute | solution.py:380
  37.0 0.4 collective-permute-start.16
  37.9 0.7 %collective-permute-start.18 = (bf16[128,1024]{1,0:T(8,128)(2,1)S(1)}, bf16[128,1024]{1,0:T(8,128)(2,1)S(1)}, u32[]{:S(2)}, u32[]{:S(2)}) collective-permute-start(bf16[128,1024]{1,0:T(8,128)(2,1)S(1)} %copy-done.2), channel_id=1, source_target_pairs={{0,1},{1,0},{2,3},{3,2},{4,5},{5,4},{6,7},{7,6},{8,9},{9,8},{10,11... | collective-permute-start | bytes 786440 | tf_op jit(solution)/shard_map/ppermute | solution.py:380
  38.6 6.8 %collective-permute-done.15.refs_5_ = bf16[256,768]{1,0:T(8,128)(2,1)S(1)} collective-permute-done((bf16[256,768]{1,0:T(8,128)(2,1)S(1)}, bf16[256,768]{1,0:T(8,128)(2,1)S(1)}, u32[]{:S(2)}, u32[]{:S(2)}) %collective-permute-start.15) | collective-permute-done | bytes 393248 | tf_op jit(solution)/shard_map/ppermute | solution.py:380
  45.4 1.3 %collective-permute-start.19 = (bf16[256,768]{1,0:T(8,128)(2,1)S(1)}, bf16[256,768]{1,0:T(8,128)(2,1)S(1)}, u32[]{:S(2)}, u32[]{:S(2)}) collective-permute-start(bf16[256,768]{1,0:T(8,128)(2,1)S(1)} %collective-permute-done.15.refs_5_), channel_id=1, source_target_pairs={{0,1},{1,0},{2,3},{3,2},{4,5},{5,4},{6,7},{7,6},{8,9},{9,8},{10,11... | collective-permute-start | bytes 1179656 | tf_op jit(solution)/shard_map/ppermute | solution.py:380
  46.8 0.8 %shard_map.97 = (bf16[256,1024]{1,0:T(8,128)(2,1)S(1)}, bf16[256,1024]{1,0:T(8,128)(2,1)S(1)}) custom-call(f32[32,4096]{1,0:T(8,128)S(1)} %get-tuple-element.65.g0, bf16[32,4096]{1,0:T(8,128)(2,1)S(1)} %collective-permute-done.14.g1, bf16[256,1024]{1,0:T(8,128)(2,1)S(1)} %bitcast.3, f32[1,1024]{1,0:T(1,128)S(1)} %bitcast.4, bf16[128,1024]{1,0:T(8,128)(2,1)S(1)} %copy-done.2, ...), custom_call_target="tpu_custom_call" | custom-call | flops 268435456 | bytes 1572864 | tf_op jit(solution)/shard_map/pallas_call | solution.py:305
  47.5 1.4 %shard_map.98.first = bf16[3,256,768]{2,1,0:T(8,128)(2,1)S(1)} custom-call(bf16[256,1024]{1,0:T(8,128)(2,1)S(1)} %get-tuple-element.75.hid, bf16[256,1024]{1,0:T(8,128)(2,1)S(1)} %get-tuple-element.74.turned, bf16[1024,768]{1,0:T(8,128)(2,1)S(1)} %copy-done.1, bf16[1024,768]{1,0:T(8,128)(2,1)S(1)} %collective-permute-done.7.refs_1_, ...), custom_call_target="tpu_custom_call" | custom-call | tf_op jit(solution)/shard_map/pallas_call | solution.py:357
  48.9 1.6 %shard_map.99 = bf16[256,3072]{1,0:T(8,128)(2,1)} custom-call(bf16[256,1024]{1,0:T(8,128)(2,1)S(1)} %get-tuple-element.74.turned, bf16[3,256,768]{2,1,0:T(8,128)(2,1)S(1)} %shard_map.98.first, bf16[256,768]{1,0:T(8,128)(2,1)S(1)} %collective-permute-done.16.refs_0_, bf16[256,768]{1,0:T(8,128)(2,1)S(1)} %collective-permute-done.17.refs_1_, ...), custom_call_target="tpu_custom_call" | custom-call | tf_op jit(solution)/shard_map/pallas_call | solution.py:366
  (39 shorter events, 2.4 us)
Async XLA Ops:
  0.0 11.7 %copy-start.1 = (bf16[1024,768]{1,0:T(8,128)(2,1)S(1)}, bf16[1024,768]{1,0:T(8,128)(2,1)}, u32[]{:S(2)}) copy-start(bf16[1024,768]{1,0:T(8,128)(2,1)} %refs_0_.1) | copy-start | bytes 4718596
  1.9 20.5 %copy-start.2 = (bf16[128,1024]{1,0:T(8,128)(2,1)S(1)}, bf16[128,1024]{1,0:T(8,128)(2,1)}, u32[]{:S(2)}) copy-start(bf16[128,1024]{1,0:T(8,128)(2,1)} %refs_0_) | copy-start | bytes 786436
  1.9 14.4 %collective-permute-start.3 = (bf16[256,768]{1,0:T(8,128)(2,1)}, bf16[256,768]{1,0:T(8,128)(2,1)S(1)}, u32[]{:S(2)}, u32[]{:S(2)}) collective-permute-start(bf16[256,768]{1,0:T(8,128)(2,1)} %constant_dynamic-slice_fusion.1), channel_id=1, source_target_pairs={{0,2},{2,0},{1,3},{3,1},{4,6},{6,4},{5,7},{7,5},{8,10},{10,8},{9,1... | collective-permute-start | bytes 1179656 | tf_op jit(solution)/shard_map/ppermute | solution.py:380
  4.0 12.3 %collective-permute-start.4 = (bf16[96,1024]{1,0:T(8,128)(2,1)S(1)}, bf16[96,1024]{1,0:T(8,128)(2,1)S(1)}, u32[]{:S(2)}, u32[]{:S(2)}) collective-permute-start(bf16[96,1024]{1,0:T(8,128)(2,1)S(1)} %slice.6), channel_id=1, source_target_pairs={{0,2},{2,0},{1,3},{3,1},{4,6},{6,4},{5,7},{7,5},{8,10},{10,8},{9,1... | collective-permute-start | bytes 589832 | tf_op jit(solution)/shard_map/ppermute | solution.py:380
  4.4 7.4 %collective-permute-start = (bf16[128,512]{1,0:T(8,128)(2,1)}, bf16[128,512]{1,0:T(8,128)(2,1)S(1)}, u32[]{:S(2)}, u32[]{:S(2)}) collective-permute-start(bf16[128,512]{1,0:T(8,128)(2,1)} %q.1), channel_id=1, source_target_pairs={{8,0},{12,4},{9,1},{13,5},{10,2},{14,6},{11,3},{15,7},{24,16},{28,... | collective-permute-start | bytes 393224 | tf_op jit(solution)/shard_map/ppermute | solution.py:400
  6.3 6.2 %collective-permute-start.1 = (bf16[128,512]{1,0:T(8,128)(2,1)}, bf16[128,512]{1,0:T(8,128)(2,1)S(1)}, u32[]{:S(2)}, u32[]{:S(2)}) collective-permute-start(bf16[128,512]{1,0:T(8,128)(2,1)} %k.1), channel_id=1, source_target_pairs={{0,4},{4,8},{8,12},{1,5},{5,9},{9,13},{2,6},{6,10},{10,14},{3,7},{... | collective-permute-start | bytes 393224 | tf_op jit(solution)/shard_map/ppermute | solution.py:401
  7.6 8.2 %collective-permute-start.2 = (bf16[128,512]{1,0:T(8,128)(2,1)}, bf16[128,512]{1,0:T(8,128)(2,1)S(1)}, u32[]{:S(2)}, u32[]{:S(2)}) collective-permute-start(bf16[128,512]{1,0:T(8,128)(2,1)} %v.1), channel_id=1, source_target_pairs={{0,4},{4,8},{8,12},{1,5},{5,9},{9,13},{2,6},{6,10},{10,14},{3,7},{... | collective-permute-start | bytes 393224 | tf_op jit(solution)/shard_map/ppermute | solution.py:402
  8.9 0.9 %copy-start.5 = (bf16[128,512]{1,0:T(8,128)(2,1)S(1)}, bf16[128,512]{1,0:T(8,128)(2,1)}, u32[]{:S(2)}) copy-start(bf16[128,512]{1,0:T(8,128)(2,1)} %q.1) | copy-start | bytes 393220
  9.8 0.9 %copy-start.6 = (bf16[128,512]{1,0:T(8,128)(2,1)S(1)}, bf16[128,512]{1,0:T(8,128)(2,1)}, u32[]{:S(2)}) copy-start(bf16[128,512]{1,0:T(8,128)(2,1)} %k.1) | copy-start | bytes 393220
  10.7 0.9 %copy-start.7 = (bf16[128,512]{1,0:T(8,128)(2,1)S(1)}, bf16[128,512]{1,0:T(8,128)(2,1)}, u32[]{:S(2)}) copy-start(bf16[128,512]{1,0:T(8,128)(2,1)} %v.1) | copy-start | bytes 393220
  16.3 16.0 %collective-permute-start.7 = (bf16[1024,768]{1,0:T(8,128)(2,1)S(1)}, bf16[1024,768]{1,0:T(8,128)(2,1)S(1)}, u32[]{:S(2)}, u32[]{:S(2)}) collective-permute-start(bf16[1024,768]{1,0:T(8,128)(2,1)S(1)} %copy-done.1), channel_id=1, source_target_pairs={{0,1},{1,0},{2,3},{3,2},{4,5},{5,4},{6,7},{7,6},{8,9},{9,8},{10,11... | collective-permute-start | bytes 4718600 | tf_op jit(solution)/shard_map/ppermute | solution.py:380
  17.8 14.5 %collective-permute-start.6 = (bf16[256,768]{1,0:T(8,128)(2,1)S(1)}, bf16[256,768]{1,0:T(8,128)(2,1)S(1)}, u32[]{:S(2)}, u32[]{:S(2)}) collective-permute-start(bf16[256,768]{1,0:T(8,128)(2,1)S(1)} %constant_dynamic-slice_fusion), channel_id=1, source_target_pairs={{0,2},{2,0},{1,3},{3,1},{4,6},{6,4},{5,7},{7,5},{8,10},{10,8},{9,1... | collective-permute-start | bytes 1179656 | tf_op jit(solution)/shard_map/ppermute | solution.py:380
  19.1 15.5 %collective-permute-start.10 = (bf16[256,768]{1,0:T(8,128)(2,1)S(1)}, bf16[256,768]{1,0:T(8,128)(2,1)S(1)}, u32[]{:S(2)}, u32[]{:S(2)}) collective-permute-start(bf16[256,768]{1,0:T(8,128)(2,1)S(1)} %collective-permute-done.3.refs_2_), channel_id=1, source_target_pairs={{0,16},{16,0},{1,17},{17,1},{2,18},{18,2},{3,19},{19,3},{4,20},{20... | collective-permute-start | bytes 1179656 | tf_op jit(solution)/shard_map/ppermute | solution.py:380
  21.1 11.2 %collective-permute-start.5 = (bf16[144,512]{1,0:T(8,128)(2,1)S(1)}, bf16[144,512]{1,0:T(8,128)(2,1)S(1)}, u32[]{:S(2)}, u32[]{:S(2)}) collective-permute-start(bf16[144,512]{1,0:T(8,128)(2,1)S(1)} %shard_map.93), channel_id=1, source_target_pairs={{0,8},{4,12},{1,9},{5,13},{2,10},{6,14},{3,11},{7,15},{16,24},{20,... | collective-permute-start | bytes 442376 | tf_op jit(solution)/shard_map/ppermute | solution.py:411
  22.4 7.6 %collective-permute-start.8 = (bf16[32,1024]{1,0:T(8,128)(2,1)S(1)}, bf16[32,1024]{1,0:T(8,128)(2,1)S(1)}, u32[]{:S(2)}, u32[]{:S(2)}) collective-permute-start(bf16[32,1024]{1,0:T(8,128)(2,1)S(1)} %slice.7), channel_id=1, source_target_pairs={{0,2},{2,0},{1,3},{3,1},{4,6},{6,4},{5,7},{7,5},{8,10},{10,8},{9,1... | collective-permute-start | bytes 196616 | tf_op jit(solution)/shard_map/ppermute | solution.py:380
  23.4 2.2 %copy-start = (bf16[512,4096]{1,0:T(8,128)(2,1)S(1)}, bf16[512,4096]{1,0:T(8,128)(2,1)}, u32[]{:S(2)}) copy-start(bf16[512,4096]{1,0:T(8,128)(2,1)} %source) | copy-start | bytes 12582916
  25.6 6.7 %copy-start.4 = (bf16[128,1024]{1,0:T(8,128)(2,1)S(1)}, bf16[128,1024]{1,0:T(8,128)(2,1)}, u32[]{:S(2)}) copy-start(bf16[128,1024]{1,0:T(8,128)(2,1)} %x.1) | copy-start | bytes 786436
  33.5 13.3 %copy-start.3 = (bf16[32,8,1024]{2,1,0:T(8,128)(2,1)S(1)}, bf16[32,8,1024]{2,1,0:T(8,128)(2,1)}, u32[]{:S(2)}) copy-start(bf16[32,8,1024]{2,1,0:T(8,128)(2,1)} %param.15) | copy-start | bytes 1572868
  33.5 13.3 %copy-start.8 = (f32[1024]{0:T(1024)S(1)}, f32[1024]{0:T(1024)}, u32[]{:S(2)}) copy-start(f32[1024]{0:T(1024)} %param.16) | copy-start | bytes 12292
  33.5 3.5 %collective-permute-start.9 = (bf16[64,4096]{1,0:T(8,128)(2,1)S(1)}, bf16[64,4096]{1,0:T(8,128)(2,1)S(1)}, u32[]{:S(2)}, u32[]{:S(2)}) collective-permute-start(bf16[64,4096]{1,0:T(8,128)(2,1)S(1)} %get-tuple-element.59), channel_id=1, source_target_pairs={{0,1},{1,0},{2,3},{3,2},{4,5},{5,4},{6,7},{7,6},{8,9},{9,8},{10,11... | collective-permute-start | bytes 1572872 | tf_op jit(solution)/shard_map/ppermute | solution.py:380
  34.5 2.1 %collective-permute-start.11 = (bf16[256,768]{1,0:T(8,128)(2,1)S(1)}, bf16[256,768]{1,0:T(8,128)(2,1)S(1)}, u32[]{:S(2)}, u32[]{:S(2)}) collective-permute-start(bf16[256,768]{1,0:T(8,128)(2,1)S(1)} %collective-permute-done.10.refs_4_), channel_id=1, source_target_pairs={{0,1},{1,0},{2,3},{3,2},{4,5},{5,4},{6,7},{7,6},{8,9},{9,8},{10,11... | collective-permute-start | bytes 1179656 | tf_op jit(solution)/shard_map/ppermute | solution.py:380
  34.6 2.4 %collective-permute-start.12 = (bf16[96,1024]{1,0:T(8,128)(2,1)S(1)}, bf16[96,1024]{1,0:T(8,128)(2,1)S(1)}, u32[]{:S(2)}, u32[]{:S(2)}) collective-permute-start(bf16[96,1024]{1,0:T(8,128)(2,1)S(1)} %collective-permute-done.4.refs_2_), channel_id=1, source_target_pairs={{0,1},{1,0},{2,3},{3,2},{4,5},{5,4},{6,7},{7,6},{8,9},{9,8},{10,11... | collective-permute-start | bytes 589832 | tf_op jit(solution)/shard_map/ppermute | solution.py:380
  35.0 2.0 %collective-permute-start.13 = (bf16[32,1024]{1,0:T(8,128)(2,1)S(1)}, bf16[32,1024]{1,0:T(8,128)(2,1)S(1)}, u32[]{:S(2)}, u32[]{:S(2)}) collective-permute-start(bf16[32,1024]{1,0:T(8,128)(2,1)S(1)} %collective-permute-done.8.refs_3_), channel_id=1, source_target_pairs={{0,1},{1,0},{2,3},{3,2},{4,5},{5,4},{6,7},{7,6},{8,9},{9,8},{10,11... | collective-permute-start | bytes 196616 | tf_op jit(solution)/shard_map/ppermute | solution.py:380
  35.1 10.3 %collective-permute-start.15 = (bf16[256,768]{1,0:T(8,128)(2,1)S(1)}, bf16[256,768]{1,0:T(8,128)(2,1)S(1)}, u32[]{:S(2)}, u32[]{:S(2)}) collective-permute-start(bf16[256,768]{1,0:T(8,128)(2,1)S(1)} %collective-permute-done.6.refs_3_), channel_id=1, source_target_pairs={{0,16},{16,0},{1,17},{17,1},{2,18},{18,2},{3,19},{19,3},{4,20},{20... | collective-permute-start | bytes 1179656 | tf_op jit(solution)/shard_map/ppermute | solution.py:380
  37.0 8.4 %collective-permute-start.16 = (bf16[256,768]{1,0:T(8,128)(2,1)S(1)}, bf16[256,768]{1,0:T(8,128)(2,1)S(1)}, u32[]{:S(2)}, u32[]{:S(2)}) collective-permute-start(bf16[256,768]{1,0:T(8,128)(2,1)S(1)} %collective-permute-done.3.refs_2_), channel_id=1, source_target_pairs={{0,1},{1,0},{2,3},{3,2},{4,5},{5,4},{6,7},{7,6},{8,9},{9,8},{10,11... | collective-permute-start | bytes 1179656 | tf_op jit(solution)/shard_map/ppermute | solution.py:380
  37.4 8.0 %collective-permute-start.17 = (bf16[256,768]{1,0:T(8,128)(2,1)S(1)}, bf16[256,768]{1,0:T(8,128)(2,1)S(1)}, u32[]{:S(2)}, u32[]{:S(2)}) collective-permute-start(bf16[256,768]{1,0:T(8,128)(2,1)S(1)} %collective-permute-done.6.refs_3_), channel_id=1, source_target_pairs={{0,1},{1,0},{2,3},{3,2},{4,5},{5,4},{6,7},{7,6},{8,9},{9,8},{10,11... | collective-permute-start | bytes 1179656 | tf_op jit(solution)/shard_map/ppermute | solution.py:380
  37.6 7.8 %collective-permute-start.14 = (bf16[32,4096]{1,0:T(8,128)(2,1)S(1)}, bf16[32,4096]{1,0:T(8,128)(2,1)S(1)}, u32[]{:S(2)}, u32[]{:S(2)}) collective-permute-start(bf16[32,4096]{1,0:T(8,128)(2,1)S(1)} %get-tuple-element.66), channel_id=1, source_target_pairs={{0,2},{2,0},{1,3},{3,1},{4,6},{6,4},{5,7},{7,5},{8,10},{10,8},{9,1... | collective-permute-start | bytes 786440 | tf_op jit(solution)/shard_map/ppermute | solution.py:380
  37.9 7.5 %collective-permute-start.18 = (bf16[128,1024]{1,0:T(8,128)(2,1)S(1)}, bf16[128,1024]{1,0:T(8,128)(2,1)S(1)}, u32[]{:S(2)}, u32[]{:S(2)}) collective-permute-start(bf16[128,1024]{1,0:T(8,128)(2,1)S(1)} %copy-done.2), channel_id=1, source_target_pairs={{0,1},{1,0},{2,3},{3,2},{4,5},{5,4},{6,7},{7,6},{8,9},{9,8},{10,11... | collective-permute-start | bytes 786440 | tf_op jit(solution)/shard_map/ppermute | solution.py:380
  45.4 3.5 %collective-permute-start.19 = (bf16[256,768]{1,0:T(8,128)(2,1)S(1)}, bf16[256,768]{1,0:T(8,128)(2,1)S(1)}, u32[]{:S(2)}, u32[]{:S(2)}) collective-permute-start(bf16[256,768]{1,0:T(8,128)(2,1)S(1)} %collective-permute-done.15.refs_5_), channel_id=1, source_target_pairs={{0,1},{1,0},{2,3},{3,2},{4,5},{5,4},{6,7},{7,6},{8,9},{9,8},{10,11... | collective-permute-start | bytes 1179656 | tf_op jit(solution)/shard_map/ppermute | solution.py:380

commit v8 on v7

--- a/solution.py
+++ b/solution.py
@@ -278,7 +278,7 @@
         bw[pl.ds(pl.multiple_of(b * depth, depth), depth), :] = ref[...]
     for i, ref in enumerate(halves):
         row = order[2 + i // 2] * depth + i % 2 * cut
-        bw[pl.ds(pl.multiple_of(row, 32), ref.shape[0]), :] = ref[...]
+        bw[pl.ds(pl.multiple_of(row, 16), ref.shape[0]), :] = ref[...]
     glob = (g0[...] + g1[...].astype(F32)).astype(BF16)
     stacked = jnp.concatenate(
         [glob[:, p * DSLICE : (p + 1) * DSLICE] for p in range(bytes_)], axis=0
@@ -333,19 +333,21 @@
 
 def last_block_kernel(turned, first, *refs):
     pieces, (out, held, sems) = refs[:-3], refs[-3:]
-    width = held.shape[1]
+    width = first.shape[2]
     order = block_order(lax.axis_index("dp"), lax.axis_index("sub"))
     copies = []
-    for i, b in enumerate(order):
-        if i == len(order) - 1:
-            held[...] = project_pieces(turned, pieces)
-        copy = pltpu.make_async_copy(
-            first.at[i] if i < len(order) - 1 else held,
-            out.at[:, pl.ds(pl.multiple_of(b * width, 128), width)],
-            sems.at[i],
-        )
-        copy.start()
-        copies.append(copy)
+    last = len(order) - 1
+    for i, b in enumerate(order[:last]):
+        columns = pl.ds(pl.multiple_of(b * width, 128), width)
+        copies.append(pltpu.make_async_copy(first.at[i], out.at[:, columns], sems.at[i]))
+        copies[-1].start()
+    half = width // 2
+    for i in range(2):
+        cut = pl.ds(i * half, half)
+        held[i, :, :] = project_pieces(turned, [piece.at[:, cut] for piece in pieces])
+        columns = pl.ds(pl.multiple_of(order[last] * width + i * half, 128), half)
+        copies.append(pltpu.make_async_copy(held.at[i], out.at[:, columns], sems.at[last + i]))
+        copies[-1].start()
     for copy in copies:
         copy.wait()
 
@@ -369,8 +371,8 @@
         in_specs=[VMEM] * (2 + len(blocks[-1])),
         out_specs=pl.BlockSpec(memory_space=pl.ANY),
         scratch_shapes=[
-            pltpu.VMEM((rows, width), BF16),
-            pltpu.SemaphoreType.DMA((len(blocks),)),
+            pltpu.VMEM((2, rows, width // 2), BF16),
+            pltpu.SemaphoreType.DMA((len(blocks) + 1,)),
         ],
         compiler_params=pltpu.CompilerParams(vmem_limit_bytes=12 * 2**20),
     )(turned, first, *blocks[-1])
@@ -395,7 +397,7 @@
     w1 = lax.dynamic_slice_in_dim(after(qkv_weight, held), (grp * 2 + 1) * quarter, quarter, 0)
 
     x0 = swap(w0, "dp")
-    bridge_rows = bridge_weight.shape[0] // 4 * 3
+    bridge_rows = bridge_weight.shape[0] // 8 * 5
     bridge_a = swap(bridge_weight[:bridge_rows], "dp")
     q_up = lax.ppermute(q_glob, "ctx", [(2, 0), (3, 1)])
     k_low = lax.ppermute(k_glob, "ctx", [(0, 1), (1, 2), (2, 3)])

time: 50.9 us -> 50.6 us (level)
  waiting for transfers between devices: 19.4 us -> 18.8 us
    ppermute x1, waiting for transfers between devices: 2.31 us -> 1.52 us  [small_mesh(): low = lax.ppermute(up, 'ctx', [(0, 2), (1, 3)])]
  transfers between devices with their start and end apart: 20 -> 20, of which waited for: 8 -> 7; matrix products, arithmetic and copies ran while one was open for 2% -> 2% of each run, Pallas kernels for 10% -> 10%
where the time goes in v8:
time: 50.6 us; the launch traced here: 50.3 us
  waiting for transfers between devices  18.8 us (37%)
  starting transfers between devices  16.8 us (33%)
  local copies, waits for them, and re-layouts  7.77 us (15%)
  Pallas kernels  6.72 us (13%)
    ppermute x16, waiting for transfers between devices, swap(): return lax.ppermute(x, axis, [(0, 1), (1, 0)])  13.2 us
    ppermute x16, starting transfers between devices, swap(): return lax.ppermute(x, axis, [(0, 1), (1, 0)])  11 us
    unnamed x18, local copies, waits for them, and re-layouts  4.91 us
    ppermute x1, waiting for transfers between devices, small_mesh(): v_low = lax.ppermute(v_glob, 'ctx', [(0, 1), (1, 2), (2, 3)])  3.28 us
    ppermute x1, starting transfers between devices, small_mesh(): q_up = lax.ppermute(q_glob, 'ctx', [(2, 0), (3, 1)])  1.96 us
    dynamic_slice x1, local copies, waits for them, and re-layouts, small_mesh(): w0 = lax.dynamic_slice_in_dim(qkv_weight, grp * 2 * quarter, quarter, 0)  1.88 us
    pallas_call x1, Pallas kernels, local(): pl.pallas_call(last_block_kernel, out_shape=jax.ShapeDtypeStruct((rows, l...  1.53 us
    ppermute x1, waiting for transfers between devices, small_mesh(): low = lax.ppermute(up, 'ctx', [(0, 2), (1, 3)])  1.52 us
  transfers between devices with their start and end apart: 20, of which 7 were waited for; matrix products, arithmetic and copies ran while one was open for 2% of the time, Pallas kernels for 10%

profile of v8, /device:TPU:25, one launch (start us, length us, event | category | flops | bytes accessed | tf_op | source)
XLA Modules:
  0.0 50.3 jit_solution(2928965864296701507)
XLA Ops:
  0.0 1.9 %constant_dynamic-slice_fusion.1 = bf16[256,768]{1,0:T(8,128)(2,1)} fusion(bf16[1024,768]{1,0:T(8,128)(2,1)} %refs_0_.1, s32[]{:T(128)S(6)} %select_n.6), kind=kLoop, calls=%fused_computation.1 | loop fusion | bytes 786436 | tf_op jit(solution)/shard_map/dynamic_slice | solution.py:396
  1.9 1.2 %collective-permute-start.3 = (bf16[256,768]{1,0:T(8,128)(2,1)}, bf16[256,768]{1,0:T(8,128)(2,1)S(1)}, u32[]{:S(2)}, u32[]{:S(2)}) collective-permute-start(bf16[256,768]{1,0:T(8,128)(2,1)} %constant_dynamic-slice_fusion.1), channel_id=1, source_target_pairs={{0,2},{2,0},{1,3},{3,1},{4,6},{6,4},{5,7},{7,5},{8,10},{10,8},{9,1... | collective-permute-start | bytes 1179656 | tf_op jit(solution)/shard_map/ppermute | solution.py:382
  3.1 0.9 %slice.6 = bf16[80,1024]{1,0:T(8,128)(2,1)S(1)} slice(bf16[128,1024]{1,0:T(8,128)(2,1)} %refs_0_), slice={[0:80], [0:1024]} | slice | bytes 327680 | tf_op jit(solution)/shard_map/slice | solution.py:401
  4.4 2.0 %collective-permute-start = (bf16[128,512]{1,0:T(8,128)(2,1)}, bf16[128,512]{1,0:T(8,128)(2,1)S(1)}, u32[]{:S(2)}, u32[]{:S(2)}) collective-permute-start(bf16[128,512]{1,0:T(8,128)(2,1)} %q.1), channel_id=1, source_target_pairs={{8,0},{12,4},{9,1},{13,5},{10,2},{14,6},{11,3},{15,7},{24,16},{28,... | collective-permute-start | bytes 393224 | tf_op jit(solution)/shard_map/ppermute | solution.py:402
  6.3 1.3 %collective-permute-start.1 = (bf16[128,512]{1,0:T(8,128)(2,1)}, bf16[128,512]{1,0:T(8,128)(2,1)S(1)}, u32[]{:S(2)}, u32[]{:S(2)}) collective-permute-start(bf16[128,512]{1,0:T(8,128)(2,1)} %k.1), channel_id=1, source_target_pairs={{0,4},{4,8},{8,12},{1,5},{5,9},{9,13},{2,6},{6,10},{10,14},{3,7},{... | collective-permute-start | bytes 393224 | tf_op jit(solution)/shard_map/ppermute | solution.py:403
  7.6 1.3 %collective-permute-start.2 = (bf16[128,512]{1,0:T(8,128)(2,1)}, bf16[128,512]{1,0:T(8,128)(2,1)S(1)}, u32[]{:S(2)}, u32[]{:S(2)}) collective-permute-start(bf16[128,512]{1,0:T(8,128)(2,1)} %v.1), channel_id=1, source_target_pairs={{0,4},{4,8},{8,12},{1,5},{5,9},{9,13},{2,6},{6,10},{10,14},{3,7},{... | collective-permute-start | bytes 393224 | tf_op jit(solution)/shard_map/ppermute | solution.py:404
  8.9 0.9 %copy-done.5 = bf16[128,512]{1,0:T(8,128)(2,1)S(1)} copy-done((bf16[128,512]{1,0:T(8,128)(2,1)S(1)}, bf16[128,512]{1,0:T(8,128)(2,1)}, u32[]{:S(2)}) %copy-start.5) | copy-done | bytes 131096
  9.8 0.9 %copy-done.6 = bf16[128,512]{1,0:T(8,128)(2,1)S(1)} copy-done((bf16[128,512]{1,0:T(8,128)(2,1)S(1)}, bf16[128,512]{1,0:T(8,128)(2,1)}, u32[]{:S(2)}) %copy-start.6) | copy-done | bytes 131096
  10.7 0.9 %copy-done.7 = bf16[128,512]{1,0:T(8,128)(2,1)S(1)} copy-done((bf16[128,512]{1,0:T(8,128)(2,1)S(1)}, bf16[128,512]{1,0:T(8,128)(2,1)}, u32[]{:S(2)}) %copy-start.7) | copy-done | bytes 131096
  11.7 0.8 %collective-permute-done.1.k_low = bf16[128,512]{1,0:T(8,128)(2,1)S(1)} collective-permute-done((bf16[128,512]{1,0:T(8,128)(2,1)}, bf16[128,512]{1,0:T(8,128)(2,1)S(1)}, u32[]{:S(2)}, u32[]{:S(2)}) %collective-permute-start.1) | collective-permute-done | bytes 131104 | tf_op jit(solution)/shard_map/ppermute | solution.py:403
  12.5 3.3 %collective-permute-done.2.v_low = bf16[128,512]{1,0:T(8,128)(2,1)S(1)} collective-permute-done((bf16[128,512]{1,0:T(8,128)(2,1)}, bf16[128,512]{1,0:T(8,128)(2,1)S(1)}, u32[]{:S(2)}, u32[]{:S(2)}) %collective-permute-start.2) | collective-permute-done | bytes 131104 | tf_op jit(solution)/shard_map/ppermute | solution.py:404
  15.8 1.9 %collective-permute-start.7 = (bf16[1024,768]{1,0:T(8,128)(2,1)S(1)}, bf16[1024,768]{1,0:T(8,128)(2,1)S(1)}, u32[]{:S(2)}, u32[]{:S(2)}) collective-permute-start(bf16[1024,768]{1,0:T(8,128)(2,1)S(1)} %copy-done.1), channel_id=1, source_target_pairs={{0,1},{1,0},{2,3},{3,2},{4,5},{5,4},{6,7},{7,6},{8,9},{9,8},{10,11... | collective-permute-start | bytes 4718600 | tf_op jit(solution)/shard_map/ppermute | solution.py:382
  17.7 1.2 %collective-permute-start.6 = (bf16[256,768]{1,0:T(8,128)(2,1)S(1)}, bf16[256,768]{1,0:T(8,128)(2,1)S(1)}, u32[]{:S(2)}, u32[]{:S(2)}) collective-permute-start(bf16[256,768]{1,0:T(8,128)(2,1)S(1)} %constant_dynamic-slice_fusion), channel_id=1, source_target_pairs={{0,2},{2,0},{1,3},{3,1},{4,6},{6,4},{5,7},{7,5},{8,10},{10,8},{9,1... | collective-permute-start | bytes 1179656 | tf_op jit(solution)/shard_map/ppermute | solution.py:382
  18.9 1.2 %collective-permute-start.10 = (bf16[256,768]{1,0:T(8,128)(2,1)S(1)}, bf16[256,768]{1,0:T(8,128)(2,1)S(1)}, u32[]{:S(2)}, u32[]{:S(2)}) collective-permute-start(bf16[256,768]{1,0:T(8,128)(2,1)S(1)} %collective-permute-done.3.refs_2_), channel_id=1, source_target_pairs={{0,16},{16,0},{1,17},{17,1},{2,18},{18,2},{3,19},{19,3},{4,20},{20... | collective-permute-start | bytes 1179656 | tf_op jit(solution)/shard_map/ppermute | solution.py:382
  20.1 0.8 %shard_map.93 = bf16[144,512]{1,0:T(8,128)(2,1)S(1)} custom-call(bf16[128,1536]{1,0:T(8,128)(2,1)S(1)} %shard_map.91.held, bf16[128,512]{1,0:T(8,128)(2,1)S(1)} %collective-permute-done.q_up, bf16[128,512]{1,0:T(8,128)(2,1)S(1)} %collective-permute-done.1.k_low, bf16[128,512]{1,0:T(8,128)(2,1)S(1)} %collective-permute-done.2.v_low), custom_call_target="tpu_custom_call" | custom-call | tf_op jit(solution)/shard_map/pallas_call | solution.py:138
  20.9 1.3 %collective-permute-start.5 = (bf16[144,512]{1,0:T(8,128)(2,1)S(1)}, bf16[144,512]{1,0:T(8,128)(2,1)S(1)}, u32[]{:S(2)}, u32[]{:S(2)}) collective-permute-start(bf16[144,512]{1,0:T(8,128)(2,1)S(1)} %shard_map.93), channel_id=1, source_target_pairs={{0,8},{4,12},{1,9},{5,13},{2,10},{6,14},{3,11},{7,15},{16,24},{20,... | collective-permute-start | bytes 442376 | tf_op jit(solution)/shard_map/ppermute | solution.py:413
  22.5 0.7 %shard_map.92 = (f32[128,512]{1,0:T(8,128)S(1)}, f32[128,128]{1,0:T(8,128)S(1)}) custom-call(bf16[128,1536]{1,0:T(8,128)(2,1)S(1)} %shard_map.91.held, bf16[128,512]{1,0:T(8,128)(2,1)S(1)} %collective-permute-done.1.k_low, bf16[128,512]{1,0:T(8,128)(2,1)S(1)} %collective-permute-done.2.v_low), custom_call_target="tpu_custom_call" | custom-call | tf_op jit(solution)/shard_map/pallas_call | solution.py:124
  23.2 2.2 %copy-done = bf16[512,4096]{1,0:T(8,128)(2,1)S(1)} copy-done((bf16[512,4096]{1,0:T(8,128)(2,1)S(1)}, bf16[512,4096]{1,0:T(8,128)(2,1)}, u32[]{:S(2)}) %copy-start) | copy-done | bytes 4194328
  25.8 4.7 %collective-permute-done.8.refs_3_ = bf16[48,1024]{1,0:T(8,128)(2,1)S(1)} collective-permute-done((bf16[48,1024]{1,0:T(8,128)(2,1)S(1)}, bf16[48,1024]{1,0:T(8,128)(2,1)S(1)}, u32[]{:S(2)}, u32[]{:S(2)}) %collective-permute-start.8) | collective-permute-done | bytes 98336 | tf_op jit(solution)/shard_map/ppermute | solution.py:382
  30.5 1.5 %collective-permute-done.5.low = bf16[144,512]{1,0:T(8,128)(2,1)S(1)} collective-permute-done((bf16[144,512]{1,0:T(8,128)(2,1)S(1)}, bf16[144,512]{1,0:T(8,128)(2,1)S(1)}, u32[]{:S(2)}, u32[]{:S(2)}) %collective-permute-start.5) | collective-permute-done | bytes 147488 | tf_op jit(solution)/shard_map/ppermute | solution.py:413
  32.0 1.1 %shard_map.95 = (bf16[64,4096]{1,0:T(8,128)(2,1)S(1)}, f32[64,4096]{1,0:T(8,128)S(1)}) custom-call(f32[128,512]{1,0:T(8,128)S(1)} %get-tuple-element.47.own, f32[128,128]{1,0:T(8,128)S(1)} %get-tuple-element.48.own_log, bf16[144,512]{1,0:T(8,128)(2,1)S(1)} %collective-permute-done.5.low, bf16[128,1024]{1,0:T(8,128)(2,1)S(1)} %copy-done.4, ...), custom_call_target="tpu_custom_call" | custom-call | flops 536870912 | bytes 5767168 | tf_op jit(solution)/shard_map/pallas_call | solution.py:228
  33.2 1.2 %collective-permute-start.9 = (bf16[64,4096]{1,0:T(8,128)(2,1)S(1)}, bf16[64,4096]{1,0:T(8,128)(2,1)S(1)}, u32[]{:S(2)}, u32[]{:S(2)}) collective-permute-start(bf16[64,4096]{1,0:T(8,128)(2,1)S(1)} %get-tuple-element.59), channel_id=1, source_target_pairs={{0,1},{1,0},{2,3},{3,2},{4,5},{5,4},{6,7},{7,6},{8,9},{9,8},{10,11... | collective-permute-start | bytes 1572872 | tf_op jit(solution)/shard_map/ppermute | solution.py:382
  34.4 0.4 collective-permute-start.12
  35.2 1.3 %collective-permute-done.11.refs_2_ = bf16[256,768]{1,0:T(8,128)(2,1)S(1)} collective-permute-done((bf16[256,768]{1,0:T(8,128)(2,1)S(1)}, bf16[256,768]{1,0:T(8,128)(2,1)S(1)}, u32[]{:S(2)}, u32[]{:S(2)}) %collective-permute-start.11) | collective-permute-done | bytes 393248 | tf_op jit(solution)/shard_map/ppermute | solution.py:382
  36.5 0.4 collective-permute-done.13.refs_5_
  36.8 0.4 collective-permute-start.16
  37.7 0.7 %collective-permute-start.18 = (bf16[128,1024]{1,0:T(8,128)(2,1)S(1)}, bf16[128,1024]{1,0:T(8,128)(2,1)S(1)}, u32[]{:S(2)}, u32[]{:S(2)}) collective-permute-start(bf16[128,1024]{1,0:T(8,128)(2,1)S(1)} %copy-done.2), channel_id=1, source_target_pairs={{0,1},{1,0},{2,3},{3,2},{4,5},{5,4},{6,7},{7,6},{8,9},{9,8},{10,11... | collective-permute-start | bytes 786440 | tf_op jit(solution)/shard_map/ppermute | solution.py:382
  38.4 6.8 %collective-permute-done.15.refs_5_ = bf16[256,768]{1,0:T(8,128)(2,1)S(1)} collective-permute-done((bf16[256,768]{1,0:T(8,128)(2,1)S(1)}, bf16[256,768]{1,0:T(8,128)(2,1)S(1)}, u32[]{:S(2)}, u32[]{:S(2)}) %collective-permute-start.15) | collective-permute-done | bytes 393248 | tf_op jit(solution)/shard_map/ppermute | solution.py:382
  45.2 1.3 %collective-permute-start.19 = (bf16[256,768]{1,0:T(8,128)(2,1)S(1)}, bf16[256,768]{1,0:T(8,128)(2,1)S(1)}, u32[]{:S(2)}, u32[]{:S(2)}) collective-permute-start(bf16[256,768]{1,0:T(8,128)(2,1)S(1)} %collective-permute-done.15.refs_5_), channel_id=1, source_target_pairs={{0,1},{1,0},{2,3},{3,2},{4,5},{5,4},{6,7},{7,6},{8,9},{9,8},{10,11... | collective-permute-start | bytes 1179656 | tf_op jit(solution)/shard_map/ppermute | solution.py:382
  46.6 0.8 %shard_map.97 = (bf16[256,1024]{1,0:T(8,128)(2,1)S(1)}, bf16[256,1024]{1,0:T(8,128)(2,1)S(1)}) custom-call(f32[32,4096]{1,0:T(8,128)S(1)} %get-tuple-element.65.g0, bf16[32,4096]{1,0:T(8,128)(2,1)S(1)} %collective-permute-done.14.g1, bf16[256,1024]{1,0:T(8,128)(2,1)S(1)} %bitcast.3, f32[1,1024]{1,0:T(1,128)S(1)} %bitcast.4, bf16[128,1024]{1,0:T(8,128)(2,1)S(1)} %copy-done.2, ...), custom_call_target="tpu_custom_call" | custom-call | flops 268435456 | bytes 1572864 | tf_op jit(solution)/shard_map/pallas_call | solution.py:305
  47.4 1.4 %shard_map.98.first = bf16[3,256,768]{2,1,0:T(8,128)(2,1)S(1)} custom-call(bf16[256,1024]{1,0:T(8,128)(2,1)S(1)} %get-tuple-element.75.hid, bf16[256,1024]{1,0:T(8,128)(2,1)S(1)} %get-tuple-element.74.turned, bf16[1024,768]{1,0:T(8,128)(2,1)S(1)} %copy-done.1, bf16[1024,768]{1,0:T(8,128)(2,1)S(1)} %collective-permute-done.7.refs_1_, ...), custom_call_target="tpu_custom_call" | custom-call | tf_op jit(solution)/shard_map/pallas_call | solution.py:359
  48.8 1.5 %shard_map.99 = bf16[256,3072]{1,0:T(8,128)(2,1)} custom-call(bf16[256,1024]{1,0:T(8,128)(2,1)S(1)} %get-tuple-element.74.turned, bf16[3,256,768]{2,1,0:T(8,128)(2,1)S(1)} %shard_map.98.first, bf16[256,768]{1,0:T(8,128)(2,1)S(1)} %collective-permute-done.16.refs_0_, bf16[256,768]{1,0:T(8,128)(2,1)S(1)} %collective-permute-done.17.refs_1_, ...), custom_call_target="tpu_custom_call" | custom-call | tf_op jit(solution)/shard_map/pallas_call | solution.py:368
  (39 shorter events, 2.0 us)
Async XLA Ops:
  0.0 11.7 %copy-start.1 = (bf16[1024,768]{1,0:T(8,128)(2,1)S(1)}, bf16[1024,768]{1,0:T(8,128)(2,1)}, u32[]{:S(2)}) copy-start(bf16[1024,768]{1,0:T(8,128)(2,1)} %refs_0_.1) | copy-start | bytes 4718596
  1.9 20.3 %copy-start.2 = (bf16[128,1024]{1,0:T(8,128)(2,1)S(1)}, bf16[128,1024]{1,0:T(8,128)(2,1)}, u32[]{:S(2)}) copy-start(bf16[128,1024]{1,0:T(8,128)(2,1)} %refs_0_) | copy-start | bytes 786436
  1.9 13.9 %collective-permute-start.3 = (bf16[256,768]{1,0:T(8,128)(2,1)}, bf16[256,768]{1,0:T(8,128)(2,1)S(1)}, u32[]{:S(2)}, u32[]{:S(2)}) collective-permute-start(bf16[256,768]{1,0:T(8,128)(2,1)} %constant_dynamic-slice_fusion.1), channel_id=1, source_target_pairs={{0,2},{2,0},{1,3},{3,1},{4,6},{6,4},{5,7},{7,5},{8,10},{10,8},{9,1... | collective-permute-start | bytes 1179656 | tf_op jit(solution)/shard_map/ppermute | solution.py:382
  4.0 11.8 %collective-permute-start.4 = (bf16[80,1024]{1,0:T(8,128)(2,1)S(1)}, bf16[80,1024]{1,0:T(8,128)(2,1)S(1)}, u32[]{:S(2)}, u32[]{:S(2)}) collective-permute-start(bf16[80,1024]{1,0:T(8,128)(2,1)S(1)} %slice.6), channel_id=1, source_target_pairs={{0,2},{2,0},{1,3},{3,1},{4,6},{6,4},{5,7},{7,5},{8,10},{10,8},{9,1... | collective-permute-start | bytes 491528 | tf_op jit(solution)/shard_map/ppermute | solution.py:382
  4.4 7.4 %collective-permute-start = (bf16[128,512]{1,0:T(8,128)(2,1)}, bf16[128,512]{1,0:T(8,128)(2,1)S(1)}, u32[]{:S(2)}, u32[]{:S(2)}) collective-permute-start(bf16[128,512]{1,0:T(8,128)(2,1)} %q.1), channel_id=1, source_target_pairs={{8,0},{12,4},{9,1},{13,5},{10,2},{14,6},{11,3},{15,7},{24,16},{28,... | collective-permute-start | bytes 393224 | tf_op jit(solution)/shard_map/ppermute | solution.py:402
  6.3 6.2 %collective-permute-start.1 = (bf16[128,512]{1,0:T(8,128)(2,1)}, bf16[128,512]{1,0:T(8,128)(2,1)S(1)}, u32[]{:S(2)}, u32[]{:S(2)}) collective-permute-start(bf16[128,512]{1,0:T(8,128)(2,1)} %k.1), channel_id=1, source_target_pairs={{0,4},{4,8},{8,12},{1,5},{5,9},{9,13},{2,6},{6,10},{10,14},{3,7},{... | collective-permute-start | bytes 393224 | tf_op jit(solution)/shard_map/ppermute | solution.py:403
  7.6 8.2 %collective-permute-start.2 = (bf16[128,512]{1,0:T(8,128)(2,1)}, bf16[128,512]{1,0:T(8,128)(2,1)S(1)}, u32[]{:S(2)}, u32[]{:S(2)}) collective-permute-start(bf16[128,512]{1,0:T(8,128)(2,1)} %v.1), channel_id=1, source_target_pairs={{0,4},{4,8},{8,12},{1,5},{5,9},{9,13},{2,6},{6,10},{10,14},{3,7},{... | collective-permute-start | bytes 393224 | tf_op jit(solution)/shard_map/ppermute | solution.py:404
  8.9 0.9 %copy-start.5 = (bf16[128,512]{1,0:T(8,128)(2,1)S(1)}, bf16[128,512]{1,0:T(8,128)(2,1)}, u32[]{:S(2)}) copy-start(bf16[128,512]{1,0:T(8,128)(2,1)} %q.1) | copy-start | bytes 393220
  9.8 0.9 %copy-start.6 = (bf16[128,512]{1,0:T(8,128)(2,1)S(1)}, bf16[128,512]{1,0:T(8,128)(2,1)}, u32[]{:S(2)}) copy-start(bf16[128,512]{1,0:T(8,128)(2,1)} %k.1) | copy-start | bytes 393220
  10.7 0.9 %copy-start.7 = (bf16[128,512]{1,0:T(8,128)(2,1)S(1)}, bf16[128,512]{1,0:T(8,128)(2,1)}, u32[]{:S(2)}) copy-start(bf16[128,512]{1,0:T(8,128)(2,1)} %v.1) | copy-start | bytes 393220
  15.8 16.2 %collective-permute-start.7 = (bf16[1024,768]{1,0:T(8,128)(2,1)S(1)}, bf16[1024,768]{1,0:T(8,128)(2,1)S(1)}, u32[]{:S(2)}, u32[]{:S(2)}) collective-permute-start(bf16[1024,768]{1,0:T(8,128)(2,1)S(1)} %copy-done.1), channel_id=1, source_target_pairs={{0,1},{1,0},{2,3},{3,2},{4,5},{5,4},{6,7},{7,6},{8,9},{9,8},{10,11... | collective-permute-start | bytes 4718600 | tf_op jit(solution)/shard_map/ppermute | solution.py:382
  17.7 14.3 %collective-permute-start.6 = (bf16[256,768]{1,0:T(8,128)(2,1)S(1)}, bf16[256,768]{1,0:T(8,128)(2,1)S(1)}, u32[]{:S(2)}, u32[]{:S(2)}) collective-permute-start(bf16[256,768]{1,0:T(8,128)(2,1)S(1)} %constant_dynamic-slice_fusion), channel_id=1, source_target_pairs={{0,2},{2,0},{1,3},{3,1},{4,6},{6,4},{5,7},{7,5},{8,10},{10,8},{9,1... | collective-permute-start | bytes 1179656 | tf_op jit(solution)/shard_map/ppermute | solution.py:382
  18.9 15.5 %collective-permute-start.10 = (bf16[256,768]{1,0:T(8,128)(2,1)S(1)}, bf16[256,768]{1,0:T(8,128)(2,1)S(1)}, u32[]{:S(2)}, u32[]{:S(2)}) collective-permute-start(bf16[256,768]{1,0:T(8,128)(2,1)S(1)} %collective-permute-done.3.refs_2_), channel_id=1, source_target_pairs={{0,16},{16,0},{1,17},{17,1},{2,18},{18,2},{3,19},{19,3},{4,20},{20... | collective-permute-start | bytes 1179656 | tf_op jit(solution)/shard_map/ppermute | solution.py:382
  20.9 11.1 %collective-permute-start.5 = (bf16[144,512]{1,0:T(8,128)(2,1)S(1)}, bf16[144,512]{1,0:T(8,128)(2,1)S(1)}, u32[]{:S(2)}, u32[]{:S(2)}) collective-permute-start(bf16[144,512]{1,0:T(8,128)(2,1)S(1)} %shard_map.93), channel_id=1, source_target_pairs={{0,8},{4,12},{1,9},{5,13},{2,10},{6,14},{3,11},{7,15},{16,24},{20,... | collective-permute-start | bytes 442376 | tf_op jit(solution)/shard_map/ppermute | solution.py:413
  22.2 8.2 %collective-permute-start.8 = (bf16[48,1024]{1,0:T(8,128)(2,1)S(1)}, bf16[48,1024]{1,0:T(8,128)(2,1)S(1)}, u32[]{:S(2)}, u32[]{:S(2)}) collective-permute-start(bf16[48,1024]{1,0:T(8,128)(2,1)S(1)} %slice.7), channel_id=1, source_target_pairs={{0,2},{2,0},{1,3},{3,1},{4,6},{6,4},{5,7},{7,5},{8,10},{10,8},{9,1... | collective-permute-start | bytes 294920 | tf_op jit(solution)/shard_map/ppermute | solution.py:382
  23.2 2.2 %copy-start = (bf16[512,4096]{1,0:T(8,128)(2,1)S(1)}, bf16[512,4096]{1,0:T(8,128)(2,1)}, u32[]{:S(2)}) copy-start(bf16[512,4096]{1,0:T(8,128)(2,1)} %source) | copy-start | bytes 12582916
  25.4 6.6 %copy-start.4 = (bf16[128,1024]{1,0:T(8,128)(2,1)S(1)}, bf16[128,1024]{1,0:T(8,128)(2,1)}, u32[]{:S(2)}) copy-start(bf16[128,1024]{1,0:T(8,128)(2,1)} %x.1) | copy-start | bytes 786436
  33.1 13.4 %copy-start.3 = (bf16[32,8,1024]{2,1,0:T(8,128)(2,1)S(1)}, bf16[32,8,1024]{2,1,0:T(8,128)(2,1)}, u32[]{:S(2)}) copy-start(bf16[32,8,1024]{2,1,0:T(8,128)(2,1)} %param.15) | copy-start | bytes 1572868
  33.2 13.4 %copy-start.8 = (f32[1024]{0:T(1024)S(1)}, f32[1024]{0:T(1024)}, u32[]{:S(2)}) copy-start(f32[1024]{0:T(1024)} %param.16) | copy-start | bytes 12292
  33.2 3.7 %collective-permute-start.9 = (bf16[64,4096]{1,0:T(8,128)(2,1)S(1)}, bf16[64,4096]{1,0:T(8,128)(2,1)S(1)}, u32[]{:S(2)}, u32[]{:S(2)}) collective-permute-start(bf16[64,4096]{1,0:T(8,128)(2,1)S(1)} %get-tuple-element.59), channel_id=1, source_target_pairs={{0,1},{1,0},{2,3},{3,2},{4,5},{5,4},{6,7},{7,6},{8,9},{9,8},{10,11... | collective-permute-start | bytes 1572872 | tf_op jit(solution)/shard_map/ppermute | solution.py:382
  34.4 2.1 %collective-permute-start.11 = (bf16[256,768]{1,0:T(8,128)(2,1)S(1)}, bf16[256,768]{1,0:T(8,128)(2,1)S(1)}, u32[]{:S(2)}, u32[]{:S(2)}) collective-permute-start(bf16[256,768]{1,0:T(8,128)(2,1)S(1)} %collective-permute-done.10.refs_4_), channel_id=1, source_target_pairs={{0,1},{1,0},{2,3},{3,2},{4,5},{5,4},{6,7},{7,6},{8,9},{9,8},{10,11... | collective-permute-start | bytes 1179656 | tf_op jit(solution)/shard_map/ppermute | solution.py:382
  34.4 2.4 %collective-permute-start.12 = (bf16[80,1024]{1,0:T(8,128)(2,1)S(1)}, bf16[80,1024]{1,0:T(8,128)(2,1)S(1)}, u32[]{:S(2)}, u32[]{:S(2)}) collective-permute-start(bf16[80,1024]{1,0:T(8,128)(2,1)S(1)} %collective-permute-done.4.refs_2_), channel_id=1, source_target_pairs={{0,1},{1,0},{2,3},{3,2},{4,5},{5,4},{6,7},{7,6},{8,9},{9,8},{10,11... | collective-permute-start | bytes 491528 | tf_op jit(solution)/shard_map/ppermute | solution.py:382
  34.9 2.0 %collective-permute-start.13 = (bf16[48,1024]{1,0:T(8,128)(2,1)S(1)}, bf16[48,1024]{1,0:T(8,128)(2,1)S(1)}, u32[]{:S(2)}, u32[]{:S(2)}) collective-permute-start(bf16[48,1024]{1,0:T(8,128)(2,1)S(1)} %collective-permute-done.8.refs_3_), channel_id=1, source_target_pairs={{0,1},{1,0},{2,3},{3,2},{4,5},{5,4},{6,7},{7,6},{8,9},{9,8},{10,11... | collective-permute-start | bytes 294920 | tf_op jit(solution)/shard_map/ppermute | solution.py:382
  35.0 10.3 %collective-permute-start.15 = (bf16[256,768]{1,0:T(8,128)(2,1)S(1)}, bf16[256,768]{1,0:T(8,128)(2,1)S(1)}, u32[]{:S(2)}, u32[]{:S(2)}) collective-permute-start(bf16[256,768]{1,0:T(8,128)(2,1)S(1)} %collective-permute-done.6.refs_3_), channel_id=1, source_target_pairs={{0,16},{16,0},{1,17},{17,1},{2,18},{18,2},{3,19},{19,3},{4,20},{20... | collective-permute-start | bytes 1179656 | tf_op jit(solution)/shard_map/ppermute | solution.py:382
  36.8 8.4 %collective-permute-start.16 = (bf16[256,768]{1,0:T(8,128)(2,1)S(1)}, bf16[256,768]{1,0:T(8,128)(2,1)S(1)}, u32[]{:S(2)}, u32[]{:S(2)}) collective-permute-start(bf16[256,768]{1,0:T(8,128)(2,1)S(1)} %collective-permute-done.3.refs_2_), channel_id=1, source_target_pairs={{0,1},{1,0},{2,3},{3,2},{4,5},{5,4},{6,7},{7,6},{8,9},{9,8},{10,11... | collective-permute-start | bytes 1179656 | tf_op jit(solution)/shard_map/ppermute | solution.py:382
  37.2 8.0 %collective-permute-start.17 = (bf16[256,768]{1,0:T(8,128)(2,1)S(1)}, bf16[256,768]{1,0:T(8,128)(2,1)S(1)}, u32[]{:S(2)}, u32[]{:S(2)}) collective-permute-start(bf16[256,768]{1,0:T(8,128)(2,1)S(1)} %collective-permute-done.6.refs_3_), channel_id=1, source_target_pairs={{0,1},{1,0},{2,3},{3,2},{4,5},{5,4},{6,7},{7,6},{8,9},{9,8},{10,11... | collective-permute-start | bytes 1179656 | tf_op jit(solution)/shard_map/ppermute | solution.py:382
  37.4 7.8 %collective-permute-start.14 = (bf16[32,4096]{1,0:T(8,128)(2,1)S(1)}, bf16[32,4096]{1,0:T(8,128)(2,1)S(1)}, u32[]{:S(2)}, u32[]{:S(2)}) collective-permute-start(bf16[32,4096]{1,0:T(8,128)(2,1)S(1)} %get-tuple-element.66), channel_id=1, source_target_pairs={{0,2},{2,0},{1,3},{3,1},{4,6},{6,4},{5,7},{7,5},{8,10},{10,8},{9,1... | collective-permute-start | bytes 786440 | tf_op jit(solution)/shard_map/ppermute | solution.py:382
  37.7 7.5 %collective-permute-start.18 = (bf16[128,1024]{1,0:T(8,128)(2,1)S(1)}, bf16[128,1024]{1,0:T(8,128)(2,1)S(1)}, u32[]{:S(2)}, u32[]{:S(2)}) collective-permute-start(bf16[128,1024]{1,0:T(8,128)(2,1)S(1)} %copy-done.2), channel_id=1, source_target_pairs={{0,1},{1,0},{2,3},{3,2},{4,5},{5,4},{6,7},{7,6},{8,9},{9,8},{10,11... | collective-permute-start | bytes 786440 | tf_op jit(solution)/shard_map/ppermute | solution.py:382
  45.2 3.5 %collective-permute-start.19 = (bf16[256,768]{1,0:T(8,128)(2,1)S(1)}, bf16[256,768]{1,0:T(8,128)(2,1)S(1)}, u32[]{:S(2)}, u32[]{:S(2)}) collective-permute-start(bf16[256,768]{1,0:T(8,128)(2,1)S(1)} %collective-permute-done.15.refs_5_), channel_id=1, source_target_pairs={{0,1},{1,0},{2,3},{3,2},{4,5},{5,4},{6,7},{7,6},{8,9},{9,8},{10,11... | collective-permute-start | bytes 1179656 | tf_op jit(solution)/shard_map/ppermute | solution.py:382
